TPU v7x, 512 devices: a whole 4x8x8 slice. The times are simulated.
512 devices in a mesh: ka: 64 (over z_lo, y, core), ga: 8 (over z_hi, x).
Axes of the slice: x: 4, y: 8, z: 8 (z_hi: 2, z_lo: 4; z = z_hi * 4 + z_lo), core: 2. Of those that a mesh axis runs over, the one named last changes fastest.
Arguments:
- coeffs: bfloat16 [3584, 2, 30720], P('ka', None, 'ga'), may hold values from -1 to 1
- shift_maps: int32 [8, 3, 30720], P(None, None, 'ga'), may hold values from 0 to 30719, as said below
Outputs:
- intersections: float32 [448, 3, 2, 3584], P('ga', None, None, 'ka')
Inputs may be any that keep to these rules, and one draw needn't show every extreme that they name: `shift_maps`: for every k-point and b-vector the row is a permutation of the plane waves that maps each aligned block of 128 plane waves onto itself.
All inputs are finite; a program needn't handle non-finite values.
Results may differ from a plain program's by a relative error of at most 0.0003.
Values may be sent and summed in bfloat16 or wider, within the bound.
No kernel may reach another device: no remote copies, remote signals or barrier semaphores. Data moves between devices by JAX's collectives and lax.ppermute only.
A program may use at most 64 MiB of HBM per device.

v0:
```python
import jax
import jax.numpy as jnp
import numpy as np
from jax import lax
from jax.sharding import PartitionSpec as P

KPTS = 8


def swapped(shard, axis, bit):
    return lax.ppermute(shard, axis, [(i, i ^ 1 << bit) for i in range(lax.axis_size(axis))])


def passed_along(shard, axis, by):
    devices = lax.axis_size(axis)
    return lax.ppermute(shard, axis, [(i, (i + by) % devices) for i in range(devices)])


def per_device(coeffs, shift_maps):
    groups = lax.axis_size("ka") // KPTS
    levels = groups.bit_length() - 1
    position = lax.axis_index("ka")
    member = position % groups
    kpoint = position // groups
    width_g = coeffs.shape[-1]
    offset = lax.axis_index("ga") * width_g
    band_rows = coeffs.shape[0]
    received = []
    for bvec in range(3):
        if bvec == 0:
            incoming = swapped(coeffs, "ka", levels)
        elif bvec == 1:
            incoming = swapped(coeffs, "ka", levels + 1)
        else:
            incoming = passed_along(coeffs, "ka", 4 * groups)
        table = lax.dynamic_index_in_dim(shift_maps, kpoint, 0, keepdims=False)[bvec] - offset
        incoming = jnp.take(incoming, table, axis=2)
        received.append(incoming)
    bit_order = list(range(levels))
    gathered = coeffs
    masks = [0]
    for bit in bit_order:
        partner_rows = swapped(gathered, "ka", bit)
        gathered = jnp.concatenate([gathered, partner_rows], axis=0)
        masks = masks + [value ^ 1 << bit for value in masks]
    inverse = np.zeros(groups, dtype=np.int32)
    for place, value in enumerate(masks):
        inverse[value] = place
    inverse_table = jnp.asarray(inverse)
    block_places = jnp.take(
        inverse_table, jnp.bitwise_xor(member, jnp.arange(groups, dtype=jnp.int32))
    )
    total_rows = groups * band_rows
    every_row = jnp.arange(total_rows, dtype=jnp.int32)
    local_of = (
        jnp.take(block_places, every_row // band_rows) * band_rows + every_row % band_rows
    ).astype(jnp.int32)
    right = jnp.stack(received, axis=0).reshape(3 * band_rows * 2, width_g)
    share_rows = total_rows // lax.axis_size("ga")
    product = lax.dot_general(
        gathered.reshape(total_rows * 2, width_g),
        right,
        (((1,), (1,)), ((), ())),
        preferred_element_type=jnp.float32,
    )
    product = product.reshape(total_rows, 2, 3, band_rows, 2)
    real_part = product[:, 0, :, :, 0] + product[:, 1, :, :, 1]
    imag_part = product[:, 0, :, :, 1] - product[:, 1, :, :, 0]
    total = lax.psum(jnp.stack([real_part, imag_part], axis=2), "ga")
    wanted = lax.dynamic_slice_in_dim(local_of, lax.axis_index("ga") * share_rows, share_rows, 0)
    return jnp.take(total, wanted, axis=0)


def solution(mesh):
    return jax.shard_map(
        per_device,
        mesh=mesh,
        in_specs=(P("ka", None, "ga"), P(None, None, "ga")),
        out_specs=P("ga", None, None, "ka"),
        check_vma=False,
    )
```

profile of v0, /device:TPU:2, one launch (start us, length us, event | category | flops | bytes accessed | tf_op | source)
XLA Modules:
  0.0 370.4 jit_solution(1947084887867602794)
XLA Ops:
  7.8 1.9 collective-permute-start
  9.7 2.4 collective-permute-done
  12.2 3.5 collective-permute-start.1
  15.7 6.1 %collective-permute-start.5 = (bf16[56,2,3840]{2,0,1:T(8,128)(2,1)S(1)}, bf16[56,2,3840]{2,0,1:T(8,128)(2,1)}, u32[]{:S(2)}, u32[]{:S(2)}) collective-permute-start(bf16[56,2,3840]{2,0,1:T(8,128)(2,1)S(1)} %copy.27), channel_id=1, source_target_pairs={{0,256},{8,264},{16,272},{24,280},{32,288},{40,296},{48,304},{56,3... | collective-permute-start | bytes 2580488 | tf_op jit(solution)/shard_map/ppermute | solution.py:16
  21.8 4.3 %collective-permute-start.4 = (bf16[56,2,3840]{2,0,1:T(8,128)(2,1)S(1)}, bf16[56,2,3840]{2,0,1:T(8,128)(2,1)}, u32[]{:S(2)}, u32[]{:S(2)}) collective-permute-start(bf16[56,2,3840]{2,0,1:T(8,128)(2,1)S(1)} %copy.27), channel_id=1, source_target_pairs={{0,128},{8,136},{16,144},{24,152},{32,160},{40,168},{48,176},{56,1... | collective-permute-start | bytes 2580488 | tf_op jit(solution)/shard_map/ppermute | solution.py:11
  26.1 6.8 %collective-permute-start.3 = (bf16[56,2,3840]{2,0,1:T(8,128)(2,1)S(1)}, bf16[56,2,3840]{2,0,1:T(8,128)(2,1)}, u32[]{:S(2)}, u32[]{:S(2)}) collective-permute-start(bf16[56,2,3840]{2,0,1:T(8,128)(2,1)S(1)} %copy.27), channel_id=1, source_target_pairs={{0,64},{8,72},{16,80},{24,88},{32,96},{40,104},{48,112},{56,120},{... | collective-permute-start | bytes 2580488 | tf_op jit(solution)/shard_map/ppermute | solution.py:11
  34.9 19.7 %collective-permute-done.1 = bf16[112,2,3840]{2,0,1:T(8,128)(2,1)} collective-permute-done((bf16[112,2,3840]{2,0,1:T(8,128)(2,1)S(1)}, bf16[112,2,3840]{2,0,1:T(8,128)(2,1)}, u32[]{:S(2)}, u32[]{:S(2)}) %collective-permute-start.1) | collective-permute-done | bytes 1720352 | tf_op jit(solution)/shard_map/ppermute | solution.py:11
  54.6 3.1 pad_maximum_fusion
  57.6 6.0 %collective-permute-start.2 = (bf16[224,2,3840]{2,0,1:T(8,128)(2,1)}, bf16[224,2,3840]{2,0,1:T(8,128)(2,1)}, u32[]{:S(2)}, u32[]{:S(2)}) collective-permute-start(bf16[224,2,3840]{2,0,1:T(8,128)(2,1)} %pad_maximum_fusion), channel_id=1, source_target_pairs={{0,32},{8,40},{16,48},{24,56},{32,0},{40,8},{48,16},{56,24},{64,96... | collective-permute-start | bytes 10321928 | tf_op jit(solution)/shard_map/ppermute | solution.py:11
  63.7 3.6 copy.35
  67.3 10.4 %gather_fusion.4 = bf16[3840,56,2]{1,2,0:T(2,128)(2,1)} fusion(bf16[56,2,3840]{0,1,2:T(2,128)(2,1)S(1)} %copy.35, s32[4096]{0:T(1024)S(1)} %pad_clamp_fusion), kind=kCustom, calls=%fused_computation.2.clone | custom fusion | bytes 1735680 | tf_op jit(solution)/shard_map/jit(_take)/gather | solution.py:37
  77.8 4.9 %copy.36 = bf16[3840,56,2]{0,1,2:T(8,128)(2,1)} copy(bf16[3840,56,2]{1,2,0:T(2,128)(2,1)} %gather_fusion.4) | data formatting | bytes 1720320 | tf_op jit(solution)/shard_map/jit(_take)/gather | solution.py:37
  82.7 3.6 copy.32
  86.3 10.4 %gather_fusion.3 = bf16[3840,56,2]{1,2,0:T(2,128)(2,1)} fusion(bf16[56,2,3840]{0,1,2:T(2,128)(2,1)S(1)} %copy.32, s32[4096]{0:T(1024)S(1)} %pad_clamp_fusion.1), kind=kCustom, calls=%fused_computation.1.clone | custom fusion | bytes 1735680 | tf_op jit(solution)/shard_map/jit(_take)/gather | solution.py:37
  96.8 5.0 %copy.33 = bf16[3840,56,2]{0,1,2:T(8,128)(2,1)} copy(bf16[3840,56,2]{1,2,0:T(2,128)(2,1)} %gather_fusion.3) | data formatting | bytes 1720320 | tf_op jit(solution)/shard_map/jit(_take)/gather | solution.py:37
  101.7 3.6 copy.29
  105.4 10.4 %gather_fusion.2 = bf16[3840,56,2]{1,2,0:T(2,128)(2,1)} fusion(bf16[56,2,3840]{0,1,2:T(2,128)(2,1)S(1)} %copy.29, s32[4096]{0:T(1024)S(1)} %pad_clamp_fusion.2), kind=kCustom, calls=%fused_computation.clone | custom fusion | bytes 1735680 | tf_op jit(solution)/shard_map/jit(_take)/gather | solution.py:37
  115.8 3.9 %copy.30 = bf16[3840,56,2]{0,1,2:T(8,128)(2,1)S(1)} copy(bf16[3840,56,2]{1,2,0:T(2,128)(2,1)} %gather_fusion.2) | data formatting | bytes 1720320 | tf_op jit(solution)/shard_map/jit(_take)/gather | solution.py:37
  119.7 1.2 select_bitcast_fusion
  121.1 119.1 %collective-permute-done.2 = bf16[224,2,3840]{2,0,1:T(8,128)(2,1)} collective-permute-done((bf16[224,2,3840]{2,0,1:T(8,128)(2,1)}, bf16[224,2,3840]{2,0,1:T(8,128)(2,1)}, u32[]{:S(2)}, u32[]{:S(2)}) %collective-permute-start.2) | collective-permute-done | bytes 3440672 | tf_op jit(solution)/shard_map/ppermute | solution.py:11
  240.2 5.4 %fusion = f32[448,2,3,56,2]{0,3,4,2,1:T(8,128)S(1)} fusion(bf16[224,2,3840]{2,0,1:T(8,128)(2,1)} %collective-permute-done.2, bf16[112,2,3840]{2,0,1:T(8,128)(2,1)} %collective-permute-done.1, bf16[56,2,3840]{2,0,1:T(8,128)(2,1)S(1)} %copy-done.2, bf16[56,2,3840]{2,0,1:T(8,128)(2,1)S(1)} %copy.27, bf16[1,56,2,3840]{3,1,2,0:T(8,128)(2,1)S(1)} %select_bitcast_fusion, ...), kind=kOutput, calls=%fused_computation.6 | convolution fusion | flops 2347376640 | bytes 10665984 | tf_op jit(solution)/shard_map/dot_general | solution.py:60
  247.3 4.4 %compare_select_fusion.4 = s32[448,1]{0,1:T(1,128)S(1)} fusion(s32[]{:T(128)} %bitcast.2, s32[]{:T(128)} %bitcast.3, s32[]{:T(128)} %bitcast.4, s32[]{:T(128)} %bitcast.5, s32[]{:T(128)} %bitcast.6, s32[]{:T(128)} %bitcast.8, s32[]{:T(128)} %bitcast.7), kind=kLoop, calls=%fused_computation.48 | loop fusion | flops 10304 | bytes 1820 | tf_op jit(solution)/shard_map/jit(_take)/gather | solution.py:56
  252.5 107.0 %all-reduce.2.cloned.1.call-done = f32[448,3,2,56]{0,3,1,2:T(8,128)} async-done(((f32[448,3,2,56]{0,3,1,2:T(8,128)}), f32[448,3,2,56]{0,3,1,2:T(8,128)}) %all-reduce.2.cloned.1.call-update) | async-done | bytes 602128 | tf_op jit(solution)/shard_map/psum | solution.py:69
  359.5 2.5 copy.39
  (39 shorter events, 7.5 us)
Async XLA Ops:
  6.5 352.9 %all-reduce.2.cloned.1.call-start = ((), (), s32[]{:S(2)}) async-start(), calls=%async_computation | async-start | bytes 1376256 | tf_op jit(solution)/shard_map/psum | solution.py:69
  7.8 4.3 %collective-permute-start = (bf16[56,2,3840]{2,0,1:T(8,128)(2,1)S(1)}, bf16[56,2,3840]{2,0,1:T(8,128)(2,1)S(1)}, u32[]{:S(2)}, u32[]{:S(2)}) collective-permute-start(bf16[56,2,3840]{2,0,1:T(8,128)(2,1)S(1)} %copy.27), channel_id=1, source_target_pairs={{0,8},{8,0},{16,24},{24,16},{32,40},{40,32},{48,56},{56,48},{64,72... | collective-permute-start | bytes 2580488 | tf_op jit(solution)/shard_map/ppermute | solution.py:11
  12.1 45.6 %copy-start.1 = (bf16[56,2,3840]{2,0,1:T(8,128)(2,1)}, bf16[56,2,3840]{2,0,1:T(8,128)(2,1)S(1)}, u32[]{:S(2)}) copy-start(bf16[56,2,3840]{2,0,1:T(8,128)(2,1)S(1)} %collective-permute-done) | copy-start | bytes 2580484
  12.2 42.4 %collective-permute-start.1 = (bf16[112,2,3840]{2,0,1:T(8,128)(2,1)S(1)}, bf16[112,2,3840]{2,0,1:T(8,128)(2,1)}, u32[]{:S(2)}, u32[]{:S(2)}) collective-permute-start(bf16[112,2,3840]{2,0,1:T(8,128)(2,1)S(1)} %pad_maximum_fusion.1), channel_id=1, source_target_pairs={{0,16},{8,24},{16,0},{24,8},{32,48},{40,56},{48,32},{56,40},{64,80... | collective-permute-start | bytes 5160968 | tf_op jit(solution)/shard_map/ppermute | solution.py:11
  15.7 48.0 %collective-permute-start.5 = (bf16[56,2,3840]{2,0,1:T(8,128)(2,1)S(1)}, bf16[56,2,3840]{2,0,1:T(8,128)(2,1)}, u32[]{:S(2)}, u32[]{:S(2)}) collective-permute-start(bf16[56,2,3840]{2,0,1:T(8,128)(2,1)S(1)} %copy.27), channel_id=1, source_target_pairs={{0,256},{8,264},{16,272},{24,280},{32,288},{40,296},{48,304},{56,3... | collective-permute-start | bytes 2580488 | tf_op jit(solution)/shard_map/ppermute | solution.py:16
  21.8 60.9 %collective-permute-start.4 = (bf16[56,2,3840]{2,0,1:T(8,128)(2,1)S(1)}, bf16[56,2,3840]{2,0,1:T(8,128)(2,1)}, u32[]{:S(2)}, u32[]{:S(2)}) collective-permute-start(bf16[56,2,3840]{2,0,1:T(8,128)(2,1)S(1)} %copy.27), channel_id=1, source_target_pairs={{0,128},{8,136},{16,144},{24,152},{32,160},{40,168},{48,176},{56,1... | collective-permute-start | bytes 2580488 | tf_op jit(solution)/shard_map/ppermute | solution.py:11
  26.1 75.7 %collective-permute-start.3 = (bf16[56,2,3840]{2,0,1:T(8,128)(2,1)S(1)}, bf16[56,2,3840]{2,0,1:T(8,128)(2,1)}, u32[]{:S(2)}, u32[]{:S(2)}) collective-permute-start(bf16[56,2,3840]{2,0,1:T(8,128)(2,1)S(1)} %copy.27), channel_id=1, source_target_pairs={{0,64},{8,72},{16,80},{24,88},{32,96},{40,104},{48,112},{56,120},{... | collective-permute-start | bytes 2580488 | tf_op jit(solution)/shard_map/ppermute | solution.py:11
  57.6 182.5 %collective-permute-start.2 = (bf16[224,2,3840]{2,0,1:T(8,128)(2,1)}, bf16[224,2,3840]{2,0,1:T(8,128)(2,1)}, u32[]{:S(2)}, u32[]{:S(2)}) collective-permute-start(bf16[224,2,3840]{2,0,1:T(8,128)(2,1)} %pad_maximum_fusion), channel_id=1, source_target_pairs={{0,32},{8,40},{16,48},{24,56},{32,0},{40,8},{48,16},{56,24},{64,96... | collective-permute-start | bytes 10321928 | tf_op jit(solution)/shard_map/ppermute | solution.py:11
  115.8 5.1 %copy-start = (bf16[3840,56,2]{0,1,2:T(8,128)(2,1)S(1)}, bf16[3840,56,2]{0,1,2:T(8,128)(2,1)}, u32[]{:S(2)}) copy-start(bf16[3840,56,2]{0,1,2:T(8,128)(2,1)} %copy.33) | copy-start | bytes 2580484
  115.8 124.4 %copy-start.2 = (bf16[56,2,3840]{2,0,1:T(8,128)(2,1)S(1)}, bf16[56,2,3840]{2,0,1:T(8,128)(2,1)}, u32[]{:S(2)}) copy-start(bf16[56,2,3840]{2,0,1:T(8,128)(2,1)} %copy-done.1) | copy-start | bytes 2580484
Sparse Core Ops, SparseCore 0:
  246.7 112.6 all-reduce.1
where the time goes:
time: 377 us; the launch traced here: 370 us
  waiting for transfers between devices  248 us (66%)
  local copies, waits for them, and re-layouts  61.8 us (16%)
  starting transfers between devices  28.6 us (8%)
  between operations  13.7 us (4%)
  other arithmetic  12.8 us (3%)
  matrix products  5.39 us (1%)
    ppermute x5, waiting for transfers between devices, swapped(): lax.ppermute(shard, axis, [(i, i ^ 1 << bit) for i in range(lax.axis_size...  141 us
    psum x1, waiting for transfers between devices, per_device(): total = lax.psum(jnp.stack([real_part, imag_part], axis=2), 'ga')  107 us
    gather x6, local copies, waits for them, and re-layouts, per_device(): incoming = jnp.take(incoming, table, axis=2)  45 us
    ppermute x5, starting transfers between devices, swapped(): lax.ppermute(shard, axis, [(i, i ^ 1 << bit) for i in range(lax.axis_size...  22.5 us
  transfers between devices with their start and end apart: 7, of which 4 were waited for; matrix products, arithmetic and copies ran while one was open for 18% of the time, Pallas kernels for 0%

commit v1 on v0

v1 whole, which is shorter than its diff:
```python
import functools

import jax
import jax.numpy as jnp
from jax import lax
from jax.experimental import pallas as pl
from jax.experimental.pallas import tpu as pltpu
from jax.sharding import PartitionSpec as P

CORES = 2
YS = 8
HALF = YS // 2
LANES = 128


def place(i):
    return i // (YS * CORES), i // CORES % YS, i % CORES


def number(z, y, c):
    return (z * YS + y % YS) * CORES + c


def moved(shard, target, wanted=None):
    pairs = [(i, number(*target(*place(i)))) for i in range(lax.axis_size("ka"))]
    if wanted is not None:
        pairs = [(s, t) for s, t in pairs if wanted(*place(t))]
    return lax.ppermute(shard, "ka", pairs)


def to_sibling(z, y, c):
    return z, y, 1 - c


def along_y(z, y, c):
    return z, y + 1 - 2 * c, c


def wanted_from_sibling(hops):
    def wanted(z, y, c):
        return hops <= (HALF - 1 - y % HALF if c == 0 else y % HALF)

    return wanted


def after(shard, *others):
    return lax.optimization_barrier((shard, *others))[0]


def products_kernel(nb, has_rest, *refs):
    refs = list(refs)
    where, maps, own, sibling = refs[:4]
    del refs[:4]
    ga, gb, sa, sb = (refs[3 * i : 3 * i + 3] for i in range(4))
    del refs[:12]
    rights = refs[:nb]
    del refs[:nb]
    rest = refs.pop(0) if has_rest else None
    out, left, raw, right, total, left_sems, raw_sems = refs
    rows, width = own.shape
    half = rows // 2
    yy, core = where[0], where[1]
    reach = jnp.where(core == 0, yy, HALF - 1 - yy)

    def slot(s):
        return left.at[pl.ds(s * rows, rows)]

    for b in range(nb):
        pltpu.make_async_copy(rights[b], raw.at[b], raw_sems.at[b]).start()
    pltpu.make_async_copy(own, slot(0), left_sems.at[0]).start()
    pltpu.make_async_copy(sibling, slot(1), left_sems.at[1]).start()
    for d in range(1, HALF):
        for part, (near, far) in enumerate(((ga, sb), (gb, sa))):
            s = 2 * d + part

            @pl.when(d <= reach)
            def _():
                pltpu.make_async_copy(near[d - 1], slot(s), left_sems.at[s]).start()

            @pl.when(d > reach)
            def _():
                pltpu.make_async_copy(far[HALF - d - 1], slot(s), left_sems.at[s]).start()

    right[...] = jnp.zeros_like(right)
    inside = lax.broadcasted_iota(jnp.int32, (LANES, LANES), 0)
    for b in range(nb):
        pltpu.make_async_copy(rights[b], raw.at[b], raw_sems.at[b]).wait()
    blocks = 5

    @pl.loop(0, width // (LANES * blocks))
    def _(j):
        for i in range(blocks):
            at = pl.ds(pl.multiple_of((j * blocks + i) * LANES, LANES), LANES)
            for b in range(nb):
                chosen = jnp.where(inside == maps[b : b + 1, at], 1.0, 0.0).astype(jnp.bfloat16)
                right[pl.ds(b * LANES, rows), at] = jnp.dot(
                    raw[b, :, at], chosen, preferred_element_type=jnp.float32
                ).astype(jnp.bfloat16)

    for s in range(8):
        pltpu.make_async_copy(own, slot(s), left_sems.at[s]).wait()
    chunk = 1280
    for j in range(width // chunk):
        at = pl.ds(j * chunk, chunk)
        part = lax.dot_general(
            left[:, at], right[:, at], (((1,), (1,)), ((), ())), preferred_element_type=jnp.float32
        )
        total[...] = part if j == 0 else total[...] + part

    first = 0
    if has_rest:
        first = 1
        out[:, pl.ds(1, 2)] = rest[...]
    for s in range(8):
        d, other = s // 2, s % 2
        chip = jnp.where(core == 0, yy + HALF - d, yy + d) % HALF
        block = chip * CORES + jnp.where(other == 0, core, 1 - core)
        for b in range(nb):
            lanes = pl.ds(b * LANES, LANES)
            top = total[pl.ds(s * rows, half), lanes]
            low = total[pl.ds(s * rows + half, half), lanes]
            turned = jnp.concatenate(
                [low[:, half:rows], -low[:, :half], jnp.zeros((half, LANES - rows), jnp.float32)], axis=1
            )
            out[block, 0 if has_rest else core ^ b] = top + turned


def products(where, maps, lefts, rights, rest=None):
    nb = len(rights)
    rows, width = lefts[0].shape
    anywhere = pl.BlockSpec(memory_space=pl.ANY)
    vmem = pl.BlockSpec(memory_space=pltpu.VMEM)
    extra = [] if rest is None else [rest]
    return pl.pallas_call(
        functools.partial(products_kernel, nb, rest is not None),
        out_shape=jax.ShapeDtypeStruct((8, nb + 2 * len(extra), rows // 2, LANES), jnp.float32),
        in_specs=[pl.BlockSpec(memory_space=pltpu.SMEM), vmem]
        + [anywhere] * (len(lefts) + nb)
        + [vmem] * len(extra),
        out_specs=vmem,
        scratch_shapes=[
            pltpu.VMEM((8 * rows, width), jnp.bfloat16),
            pltpu.VMEM((nb, rows, width), jnp.bfloat16),
            pltpu.VMEM((nb * LANES, width), jnp.bfloat16),
            pltpu.VMEM((8 * rows, nb * LANES), jnp.float32),
            pltpu.SemaphoreType.DMA((8,)),
            pltpu.SemaphoreType.DMA((nb,)),
        ],
        compiler_params=pltpu.CompilerParams(vmem_limit_bytes=40 * 2**20),
        cost_estimate=pl.CostEstimate(
            flops=2 * 8 * rows * nb * LANES * width,
            bytes_accessed=(8 + nb) * rows * width * 2,
            transcendentals=0,
        ),
    )(where, maps, *lefts, *rights, *extra)


def along_z(z, y, c):
    return z ^ (1 + c), y, c


def per_device(coeffs, shift_maps):
    bands, _, width = coeffs.shape
    position = lax.axis_index("ka")
    core = position % CORES
    yy = position // CORES % HALF
    where = jnp.stack([yy, core]).astype(jnp.int32)
    kpoint = position // (CORES * HALF)
    maps = lax.dynamic_index_in_dim(shift_maps, kpoint, 0, keepdims=False) % LANES
    later_maps = jnp.where(core == 0, maps[1:], maps[:0:-1])
    mine = coeffs.transpose(1, 0, 2).reshape(2 * bands, width)

    sibling = moved(mine, to_sibling)
    za = moved(mine, along_z)
    zb = moved(after(sibling, za), along_z)
    ga, gb, sa, sb = [mine], [sibling], [None], [None]
    for hops in range(1, HALF):
        deps = {1: [], 2: [], 3: [za, sa[1], sb[1]] if hops == 3 else []}[hops]
        ga.append(moved(after(ga[-1], *deps), along_y))
        gb.append(moved(gb[-1], along_y))
        sa.append(moved(ga[-1], to_sibling, wanted_from_sibling(hops)))
        sb.append(moved(gb[-1], to_sibling, wanted_from_sibling(hops)))
    opposite = moved(after(ga[-1], zb, sa[2], sb[2]), along_y)
    zs = moved(zb, to_sibling)
    lefts = [mine, sibling, *ga[1:], *gb[1:], *sa[1:], *sb[1:]]
    later = products(where, later_maps, lefts, [za, zs])
    every = products(where, maps[:1], lefts, [opposite], later)
    shares = lax.all_to_all(every, "ga", 0, 0, tiled=True)
    total = shares.sum(axis=0)[:, :, : 2 * bands]
    return total.transpose(1, 0, 2).reshape(bands, 3, 2, bands)


def solution(mesh):
    return jax.shard_map(
        per_device,
        mesh=mesh,
        in_specs=(P("ka", None, "ga"), P(None, None, "ga")),
        out_specs=P("ga", None, None, "ka"),
        check_vma=False,
    )
```

time: 377 us -> 118 us (0.31)
  the two profiles are of different devices: /device:TPU:2 before, /device:TPU:64 now
where the time goes in v1:
time: 118 us
  starting transfers between devices  41.9 us (36%)
  blocking collectives  33.6 us (28%)
  waiting for transfers between devices  27.5 us (23%)
  Pallas kernels  11.1 us (9%)
  local copies, waits for them, and re-layouts  3 us (3%)
    ppermute x17, starting transfers between devices, moved(): return lax.ppermute(shard, 'ka', pairs)  41.9 us
    all_to_all x1, blocking collectives, per_device(): shares = lax.all_to_all(every, 'ga', 0, 0, tiled=True)  33.6 us
    ppermute x17, waiting for transfers between devices, moved(): return lax.ppermute(shard, 'ka', pairs)  27.5 us
    pallas_call x2, Pallas kernels, products(): pl.pallas_call(functools.partial(products_kernel, nb, rest is not None),...  11.1 us
  transfers between devices with their start and end apart: 17, of which 8 were waited for; matrix products, arithmetic and copies ran while one was open for 1% of the time, Pallas kernels for 5%

profile of v1, /device:TPU:64, one launch (start us, length us, event | category | flops | bytes accessed | tf_op | source)
XLA Modules:
  0.0 117.7 jit_solution(17631703091668482203)
XLA Ops:
  0.0 1.3 %copy.4 = bf16[2,56,3840]{2,1,0:T(8,128)(2,1)S(1)} copy(bf16[2,56,3840]{2,0,1:T(2,128)(2,1)} %bitcast.17) | data formatting | bytes 1720320 | tf_op jit(solution)/shard_map/transpose | solution.py:171
  1.3 1.9 %collective-permute-start = (bf16[112,3840]{1,0:T(8,128)(2,1)S(1)}, bf16[112,3840]{1,0:T(8,128)(2,1)S(1)}, u32[]{:S(2)}, u32[]{:S(2)}) collective-permute-start(bf16[112,3840]{1,0:T(8,128)(2,1)S(1)} %bitcast.12), channel_id=1, source_target_pairs={{0,8},{8,0},{16,24},{24,16},{32,40},{40,32},{48,56},{56,48},{64,72... | collective-permute-start | bytes 2580488 | tf_op jit(solution)/shard_map/ppermute | solution.py:28
  3.2 3.5 %collective-permute-start.1 = (bf16[112,3840]{1,0:T(8,128)(2,1)S(1)}, bf16[112,3840]{1,0:T(8,128)(2,1)S(1)}, u32[]{:S(2)}, u32[]{:S(2)}) collective-permute-start(bf16[112,3840]{1,0:T(8,128)(2,1)S(1)} %bitcast.13), channel_id=1, source_target_pairs={{0,16},{8,120},{16,32},{24,8},{32,48},{40,24},{48,64},{56,40},{64,... | collective-permute-start | bytes 2580488 | tf_op jit(solution)/shard_map/ppermute | solution.py:28
  6.7 3.5 %collective-permute-start.5 = (bf16[112,3840]{1,0:T(8,128)(2,1)S(1)}, bf16[112,3840]{1,0:T(8,128)(2,1)}, u32[]{:S(2)}, u32[]{:S(2)}) collective-permute-start(bf16[112,3840]{1,0:T(8,128)(2,1)S(1)} %collective-permute-done.refs_3_), channel_id=1, source_target_pairs={{0,16},{8,120},{16,32},{24,8},{32,48},{40,24},{48,64},{56,40},{64,... | collective-permute-start | bytes 2580488 | tf_op jit(solution)/shard_map/ppermute | solution.py:28
  10.2 4.2 %collective-permute-start.3 = (bf16[112,3840]{1,0:T(8,128)(2,1)S(1)}, bf16[112,3840]{1,0:T(8,128)(2,1)}, u32[]{:S(2)}, u32[]{:S(2)}) collective-permute-start(bf16[112,3840]{1,0:T(8,128)(2,1)S(1)} %bitcast.14), channel_id=1, source_target_pairs={{0,128},{8,264},{16,144},{24,280},{32,160},{40,296},{48,176},{56,3... | collective-permute-start | bytes 2580488 | tf_op jit(solution)/shard_map/ppermute | solution.py:28
  14.4 4.9 %collective-permute-done.1.refs_4_ = bf16[112,3840]{1,0:T(8,128)(2,1)S(1)} collective-permute-done((bf16[112,3840]{1,0:T(8,128)(2,1)S(1)}, bf16[112,3840]{1,0:T(8,128)(2,1)S(1)}, u32[]{:S(2)}, u32[]{:S(2)}) %collective-permute-start.1) | collective-permute-done | bytes 860192 | tf_op jit(solution)/shard_map/ppermute | solution.py:28
  19.4 2.0 %collective-permute-start.2 = (bf16[112,3840]{1,0:T(8,128)(2,1)S(1)}, bf16[112,3840]{1,0:T(8,128)(2,1)}, u32[]{:S(2)}, u32[]{:S(2)}) collective-permute-start(bf16[112,3840]{1,0:T(8,128)(2,1)S(1)} %collective-permute-done.1.refs_4_), channel_id=1, source_target_pairs={{0,16},{8,120},{16,32},{24,8},{32,48},{40,24},{48,64},{56,40},{64,... | collective-permute-start | bytes 2580488 | tf_op jit(solution)/shard_map/ppermute | solution.py:28
  21.4 1.3 %collective-permute-start.4 = (bf16[112,3840]{1,0:T(8,128)(2,1)S(1)}, bf16[112,3840]{1,0:T(8,128)(2,1)}, u32[]{:S(2)}, u32[]{:S(2)}) collective-permute-start(bf16[112,3840]{1,0:T(8,128)(2,1)S(1)} %collective-permute-done.1.refs_4_), channel_id=1, source_target_pairs={{8,0},{16,24},{24,16},{32,40},{40,32},{48,56},{72,64},{80,88},{88,... | collective-permute-start | bytes 2580488 | tf_op jit(solution)/shard_map/ppermute | solution.py:28
  22.7 6.0 %collective-permute-done.5.refs_7_ = bf16[112,3840]{1,0:T(8,128)(2,1)} collective-permute-done((bf16[112,3840]{1,0:T(8,128)(2,1)S(1)}, bf16[112,3840]{1,0:T(8,128)(2,1)}, u32[]{:S(2)}, u32[]{:S(2)}) %collective-permute-start.5) | collective-permute-done | bytes 860192 | tf_op jit(solution)/shard_map/ppermute | solution.py:28
  28.7 1.3 %collective-permute-start.6 = (bf16[112,3840]{1,0:T(8,128)(2,1)}, bf16[112,3840]{1,0:T(8,128)(2,1)}, u32[]{:S(2)}, u32[]{:S(2)}) collective-permute-start(bf16[112,3840]{1,0:T(8,128)(2,1)} %collective-permute-done.5.refs_7_), channel_id=1, source_target_pairs={{8,0},{16,24},{24,16},{32,40},{40,32},{48,56},{72,64},{80,88},{88,... | collective-permute-start | bytes 2580488 | tf_op jit(solution)/shard_map/ppermute | solution.py:28
  30.0 2.7 %collective-permute-start.8 = (bf16[112,3840]{1,0:T(8,128)(2,1)}, bf16[112,3840]{1,0:T(8,128)(2,1)}, u32[]{:S(2)}, u32[]{:S(2)}) collective-permute-start(bf16[112,3840]{1,0:T(8,128)(2,1)} %collective-permute-done.5.refs_7_), channel_id=1, source_target_pairs={{0,16},{8,120},{16,32},{24,8},{32,48},{40,24},{48,64},{56,40},{64,... | collective-permute-start | bytes 2580488 | tf_op jit(solution)/shard_map/ppermute | solution.py:28
  33.9 4.8 %collective-permute-start.14 = (bf16[112,3840]{1,0:T(8,128)(2,1)S(1)}, bf16[112,3840]{1,0:T(8,128)(2,1)}, u32[]{:S(2)}, u32[]{:S(2)}) collective-permute-start(bf16[112,3840]{1,0:T(8,128)(2,1)S(1)} %collective-permute-done.refs_3_), channel_id=1, source_target_pairs={{0,128},{8,264},{16,144},{24,280},{32,160},{40,296},{48,176},{56,3... | collective-permute-start | bytes 2580488 | tf_op jit(solution)/shard_map/ppermute | solution.py:28
  38.7 1.3 %collective-permute-start.10 = (bf16[112,3840]{1,0:T(8,128)(2,1)}, bf16[112,3840]{1,0:T(8,128)(2,1)}, u32[]{:S(2)}, u32[]{:S(2)}) collective-permute-start(bf16[112,3840]{1,0:T(8,128)(2,1)} %collective-permute-done.2.refs_5_), channel_id=1, source_target_pairs={{8,0},{24,16},{32,40},{48,56},{72,64},{88,80},{96,104},{112,120},{... | collective-permute-start | bytes 2580488 | tf_op jit(solution)/shard_map/ppermute | solution.py:28
  40.0 1.9 %collective-permute-start.7 = (bf16[112,3840]{1,0:T(8,128)(2,1)}, bf16[112,3840]{1,0:T(8,128)(2,1)}, u32[]{:S(2)}, u32[]{:S(2)}) collective-permute-start(bf16[112,3840]{1,0:T(8,128)(2,1)} %collective-permute-done.2.refs_5_), channel_id=1, source_target_pairs={{0,16},{8,120},{16,32},{24,8},{32,48},{40,24},{48,64},{56,40},{64,... | collective-permute-start | bytes 2580488 | tf_op jit(solution)/shard_map/ppermute | solution.py:28
  42.0 5.1 %collective-permute-done.8.refs_8_ = bf16[112,3840]{1,0:T(8,128)(2,1)} collective-permute-done((bf16[112,3840]{1,0:T(8,128)(2,1)}, bf16[112,3840]{1,0:T(8,128)(2,1)}, u32[]{:S(2)}, u32[]{:S(2)}) %collective-permute-start.8) | collective-permute-done | bytes 860192 | tf_op jit(solution)/shard_map/ppermute | solution.py:28
  48.4 2.0 %collective-permute-start.9 = (bf16[112,3840]{1,0:T(8,128)(2,1)}, bf16[112,3840]{1,0:T(8,128)(2,1)}, u32[]{:S(2)}, u32[]{:S(2)}) collective-permute-start(bf16[112,3840]{1,0:T(8,128)(2,1)} %collective-permute-done.8.refs_8_), channel_id=1, source_target_pairs={{0,16},{8,120},{16,32},{24,8},{32,48},{40,24},{48,64},{56,40},{64,... | collective-permute-start | bytes 2580488 | tf_op jit(solution)/shard_map/ppermute | solution.py:28
  51.4 6.0 %collective-permute-done.14 = bf16[112,3840]{1,0:T(8,128)(2,1)} collective-permute-done((bf16[112,3840]{1,0:T(8,128)(2,1)S(1)}, bf16[112,3840]{1,0:T(8,128)(2,1)}, u32[]{:S(2)}, u32[]{:S(2)}) %collective-permute-start.14) | collective-permute-done | bytes 860192 | tf_op jit(solution)/shard_map/ppermute | solution.py:28
  57.4 4.2 %collective-permute-start.16 = (bf16[112,3840]{1,0:T(8,128)(2,1)}, bf16[112,3840]{1,0:T(8,128)(2,1)S(1)}, u32[]{:S(2)}, u32[]{:S(2)}) collective-permute-start(bf16[112,3840]{1,0:T(8,128)(2,1)} %collective-permute-done.14), channel_id=1, source_target_pairs={{0,8},{8,0},{16,24},{24,16},{32,40},{40,32},{48,56},{56,48},{64,72... | collective-permute-start | bytes 2580488 | tf_op jit(solution)/shard_map/ppermute | solution.py:28
  61.6 3.5 %collective-permute-start.15 = (bf16[112,3840]{1,0:T(8,128)(2,1)}, bf16[112,3840]{1,0:T(8,128)(2,1)S(1)}, u32[]{:S(2)}, u32[]{:S(2)}) collective-permute-start(bf16[112,3840]{1,0:T(8,128)(2,1)} %collective-permute-done.7.refs_6_), channel_id=1, source_target_pairs={{0,16},{8,120},{16,32},{24,8},{32,48},{40,24},{48,64},{56,40},{64,... | collective-permute-start | bytes 2580488 | tf_op jit(solution)/shard_map/ppermute | solution.py:28
  65.1 1.3 %collective-permute-start.11 = (bf16[112,3840]{1,0:T(8,128)(2,1)}, bf16[112,3840]{1,0:T(8,128)(2,1)S(1)}, u32[]{:S(2)}, u32[]{:S(2)}) collective-permute-start(bf16[112,3840]{1,0:T(8,128)(2,1)} %collective-permute-done.7.refs_6_), channel_id=1, source_target_pairs={{8,0},{48,56},{72,64},{112,120},{136,128},{176,184},{200,192},{240... | collective-permute-start | bytes 2580488 | tf_op jit(solution)/shard_map/ppermute | solution.py:28
  68.6 3.1 %collective-permute-done.13.refs_15_ = bf16[112,3840]{1,0:T(8,128)(2,1)S(1)} collective-permute-done((bf16[112,3840]{1,0:T(8,128)(2,1)}, bf16[112,3840]{1,0:T(8,128)(2,1)S(1)}, u32[]{:S(2)}, u32[]{:S(2)}) %collective-permute-start.13) | collective-permute-done | bytes 860192 | tf_op jit(solution)/shard_map/ppermute | solution.py:28
  71.8 5.7 %shard_map.28.refs_17_ = f32[8,2,56,128]{3,2,1,0:T(8,128)S(1)} custom-call(s32[2]{0:T(128)S(1)} %pad_add_fusion.refs_0_, s32[2,3840]{1,0:T(2,128)S(1)} %broadcast_select_fusion.refs_1_, bf16[112,3840]{1,0:T(8,128)(2,1)S(1)} %bitcast.15, bf16[112,3840]{1,0:T(8,128)(2,1)S(1)} %collective-permute-done.refs_3_, ...), custom_call_target="tpu_custom_call" | custom-call | flops 1761607680 | bytes 8601600 | tf_op jit(solution)/shard_map/pallas_call | solution.py:134
  77.7 5.4 %shard_map.29 = f32[8,3,56,128]{3,2,1,0:T(8,128)S(1)} custom-call(s32[2]{0:T(128)S(1)} %pad_add_fusion.refs_0_, s32[1,3840]{1,0:T(1,128)S(1)} %slice.13.refs_1_, bf16[112,3840]{1,0:T(8,128)(2,1)S(1)} %bitcast.16, bf16[112,3840]{1,0:T(8,128)(2,1)S(1)} %collective-permute-done.refs_3_, bf16[112,3840]{1,0:T(8,128)(2,1)S(1)} %collective-permute-done.1.refs_4_, ...), custom_call_target="tpu_custom_call" | custom-call | flops 880803840 | bytes 7741440 | tf_op jit(solution)/shard_map/pallas_call | solution.py:134
  83.1 33.6 %all_to_all.5 = f32[8,3,56,128]{3,2,1,0:T(8,128)S(1)} all-to-all(f32[8,3,56,128]{3,2,1,0:T(8,128)S(1)} %shard_map.29), channel_id=1, replica_groups=mesh['ka'=64,'ga'=8] {'ga'}, dimensions={0} | all-to-all | bytes 1376256 | tf_op jit(solution)/shard_map/all_to_all | solution.py:188
  (27 shorter events, 6.8 us)
Async XLA Ops:
  0.0 32.7 %copy-start = (s32[8,3,3840]{2,0,1:T(8,128)S(1)}, s32[8,3,3840]{2,0,1:T(8,128)}, u32[]{:S(2)}) copy-start(s32[8,3,3840]{2,0,1:T(8,128)} %param.3) | copy-start | bytes 1105924
  1.3 5.4 %collective-permute-start = (bf16[112,3840]{1,0:T(8,128)(2,1)S(1)}, bf16[112,3840]{1,0:T(8,128)(2,1)S(1)}, u32[]{:S(2)}, u32[]{:S(2)}) collective-permute-start(bf16[112,3840]{1,0:T(8,128)(2,1)S(1)} %bitcast.12), channel_id=1, source_target_pairs={{0,8},{8,0},{16,24},{24,16},{32,40},{40,32},{48,56},{56,48},{64,72... | collective-permute-start | bytes 2580488 | tf_op jit(solution)/shard_map/ppermute | solution.py:28
  3.2 16.1 %collective-permute-start.1 = (bf16[112,3840]{1,0:T(8,128)(2,1)S(1)}, bf16[112,3840]{1,0:T(8,128)(2,1)S(1)}, u32[]{:S(2)}, u32[]{:S(2)}) collective-permute-start(bf16[112,3840]{1,0:T(8,128)(2,1)S(1)} %bitcast.13), channel_id=1, source_target_pairs={{0,16},{8,120},{16,32},{24,8},{32,48},{40,24},{48,64},{56,40},{64,... | collective-permute-start | bytes 2580488 | tf_op jit(solution)/shard_map/ppermute | solution.py:28
  6.7 21.9 %collective-permute-start.5 = (bf16[112,3840]{1,0:T(8,128)(2,1)S(1)}, bf16[112,3840]{1,0:T(8,128)(2,1)}, u32[]{:S(2)}, u32[]{:S(2)}) collective-permute-start(bf16[112,3840]{1,0:T(8,128)(2,1)S(1)} %collective-permute-done.refs_3_), channel_id=1, source_target_pairs={{0,16},{8,120},{16,32},{24,8},{32,48},{40,24},{48,64},{56,40},{64,... | collective-permute-start | bytes 2580488 | tf_op jit(solution)/shard_map/ppermute | solution.py:28
  10.2 23.7 %collective-permute-start.3 = (bf16[112,3840]{1,0:T(8,128)(2,1)S(1)}, bf16[112,3840]{1,0:T(8,128)(2,1)}, u32[]{:S(2)}, u32[]{:S(2)}) collective-permute-start(bf16[112,3840]{1,0:T(8,128)(2,1)S(1)} %bitcast.14), channel_id=1, source_target_pairs={{0,128},{8,264},{16,144},{24,280},{32,160},{40,296},{48,176},{56,3... | collective-permute-start | bytes 2580488 | tf_op jit(solution)/shard_map/ppermute | solution.py:28
  19.4 19.3 %collective-permute-start.2 = (bf16[112,3840]{1,0:T(8,128)(2,1)S(1)}, bf16[112,3840]{1,0:T(8,128)(2,1)}, u32[]{:S(2)}, u32[]{:S(2)}) collective-permute-start(bf16[112,3840]{1,0:T(8,128)(2,1)S(1)} %collective-permute-done.1.refs_4_), channel_id=1, source_target_pairs={{0,16},{8,120},{16,32},{24,8},{32,48},{40,24},{48,64},{56,40},{64,... | collective-permute-start | bytes 2580488 | tf_op jit(solution)/shard_map/ppermute | solution.py:28
  21.4 18.6 %collective-permute-start.4 = (bf16[112,3840]{1,0:T(8,128)(2,1)S(1)}, bf16[112,3840]{1,0:T(8,128)(2,1)}, u32[]{:S(2)}, u32[]{:S(2)}) collective-permute-start(bf16[112,3840]{1,0:T(8,128)(2,1)S(1)} %collective-permute-done.1.refs_4_), channel_id=1, source_target_pairs={{8,0},{16,24},{24,16},{32,40},{40,32},{48,56},{72,64},{80,88},{88,... | collective-permute-start | bytes 2580488 | tf_op jit(solution)/shard_map/ppermute | solution.py:28
  28.7 11.3 %collective-permute-start.6 = (bf16[112,3840]{1,0:T(8,128)(2,1)}, bf16[112,3840]{1,0:T(8,128)(2,1)}, u32[]{:S(2)}, u32[]{:S(2)}) collective-permute-start(bf16[112,3840]{1,0:T(8,128)(2,1)} %collective-permute-done.5.refs_7_), channel_id=1, source_target_pairs={{8,0},{16,24},{24,16},{32,40},{40,32},{48,56},{72,64},{80,88},{88,... | collective-permute-start | bytes 2580488 | tf_op jit(solution)/shard_map/ppermute | solution.py:28
  30.0 17.1 %collective-permute-start.8 = (bf16[112,3840]{1,0:T(8,128)(2,1)}, bf16[112,3840]{1,0:T(8,128)(2,1)}, u32[]{:S(2)}, u32[]{:S(2)}) collective-permute-start(bf16[112,3840]{1,0:T(8,128)(2,1)} %collective-permute-done.5.refs_7_), channel_id=1, source_target_pairs={{0,16},{8,120},{16,32},{24,8},{32,48},{40,24},{48,64},{56,40},{64,... | collective-permute-start | bytes 2580488 | tf_op jit(solution)/shard_map/ppermute | solution.py:28
  33.9 23.5 %collective-permute-start.14 = (bf16[112,3840]{1,0:T(8,128)(2,1)S(1)}, bf16[112,3840]{1,0:T(8,128)(2,1)}, u32[]{:S(2)}, u32[]{:S(2)}) collective-permute-start(bf16[112,3840]{1,0:T(8,128)(2,1)S(1)} %collective-permute-done.refs_3_), channel_id=1, source_target_pairs={{0,128},{8,264},{16,144},{24,280},{32,160},{40,296},{48,176},{56,3... | collective-permute-start | bytes 2580488 | tf_op jit(solution)/shard_map/ppermute | solution.py:28
  38.7 22.8 %collective-permute-start.10 = (bf16[112,3840]{1,0:T(8,128)(2,1)}, bf16[112,3840]{1,0:T(8,128)(2,1)}, u32[]{:S(2)}, u32[]{:S(2)}) collective-permute-start(bf16[112,3840]{1,0:T(8,128)(2,1)} %collective-permute-done.2.refs_5_), channel_id=1, source_target_pairs={{8,0},{24,16},{32,40},{48,56},{72,64},{88,80},{96,104},{112,120},{... | collective-permute-start | bytes 2580488 | tf_op jit(solution)/shard_map/ppermute | solution.py:28
  40.0 21.5 %collective-permute-start.7 = (bf16[112,3840]{1,0:T(8,128)(2,1)}, bf16[112,3840]{1,0:T(8,128)(2,1)}, u32[]{:S(2)}, u32[]{:S(2)}) collective-permute-start(bf16[112,3840]{1,0:T(8,128)(2,1)} %collective-permute-done.2.refs_5_), channel_id=1, source_target_pairs={{0,16},{8,120},{16,32},{24,8},{32,48},{40,24},{48,64},{56,40},{64,... | collective-permute-start | bytes 2580488 | tf_op jit(solution)/shard_map/ppermute | solution.py:28
  47.1 14.5 %collective-permute-start.12 = (bf16[112,3840]{1,0:T(8,128)(2,1)}, bf16[112,3840]{1,0:T(8,128)(2,1)}, u32[]{:S(2)}, u32[]{:S(2)}) collective-permute-start(bf16[112,3840]{1,0:T(8,128)(2,1)} %collective-permute-done.8.refs_8_), channel_id=1, source_target_pairs={{8,0},{24,16},{32,40},{48,56},{72,64},{88,80},{96,104},{112,120},{... | collective-permute-start | bytes 2580488 | tf_op jit(solution)/shard_map/ppermute | solution.py:28
  48.4 18.9 %collective-permute-start.9 = (bf16[112,3840]{1,0:T(8,128)(2,1)}, bf16[112,3840]{1,0:T(8,128)(2,1)}, u32[]{:S(2)}, u32[]{:S(2)}) collective-permute-start(bf16[112,3840]{1,0:T(8,128)(2,1)} %collective-permute-done.8.refs_8_), channel_id=1, source_target_pairs={{0,16},{8,120},{16,32},{24,8},{32,48},{40,24},{48,64},{56,40},{64,... | collective-permute-start | bytes 2580488 | tf_op jit(solution)/shard_map/ppermute | solution.py:28
  57.4 11.2 %collective-permute-start.16 = (bf16[112,3840]{1,0:T(8,128)(2,1)}, bf16[112,3840]{1,0:T(8,128)(2,1)S(1)}, u32[]{:S(2)}, u32[]{:S(2)}) collective-permute-start(bf16[112,3840]{1,0:T(8,128)(2,1)} %collective-permute-done.14), channel_id=1, source_target_pairs={{0,8},{8,0},{16,24},{24,16},{32,40},{40,32},{48,56},{56,48},{64,72... | collective-permute-start | bytes 2580488 | tf_op jit(solution)/shard_map/ppermute | solution.py:28
  61.6 16.1 %collective-permute-start.15 = (bf16[112,3840]{1,0:T(8,128)(2,1)}, bf16[112,3840]{1,0:T(8,128)(2,1)S(1)}, u32[]{:S(2)}, u32[]{:S(2)}) collective-permute-start(bf16[112,3840]{1,0:T(8,128)(2,1)} %collective-permute-done.7.refs_6_), channel_id=1, source_target_pairs={{0,16},{8,120},{16,32},{24,8},{32,48},{40,24},{48,64},{56,40},{64,... | collective-permute-start | bytes 2580488 | tf_op jit(solution)/shard_map/ppermute | solution.py:28
  65.1 6.6 %collective-permute-start.11 = (bf16[112,3840]{1,0:T(8,128)(2,1)}, bf16[112,3840]{1,0:T(8,128)(2,1)S(1)}, u32[]{:S(2)}, u32[]{:S(2)}) collective-permute-start(bf16[112,3840]{1,0:T(8,128)(2,1)} %collective-permute-done.7.refs_6_), channel_id=1, source_target_pairs={{8,0},{48,56},{72,64},{112,120},{136,128},{176,184},{200,192},{240... | collective-permute-start | bytes 2580488 | tf_op jit(solution)/shard_map/ppermute | solution.py:28
  67.3 4.5 %collective-permute-start.13 = (bf16[112,3840]{1,0:T(8,128)(2,1)}, bf16[112,3840]{1,0:T(8,128)(2,1)S(1)}, u32[]{:S(2)}, u32[]{:S(2)}) collective-permute-start(bf16[112,3840]{1,0:T(8,128)(2,1)} %collective-permute-done.9.refs_9_), channel_id=1, source_target_pairs={{8,0},{48,56},{72,64},{112,120},{136,128},{176,184},{200,192},{240... | collective-permute-start | bytes 2580488 | tf_op jit(solution)/shard_map/ppermute | solution.py:28

commit v2 on v1

--- a/solution.py
+++ b/solution.py
@@ -45,6 +45,14 @@
 
 def after(shard, *others):
     return lax.optimization_barrier((shard, *others))[0]
+
+
+def scaled(values, exponent_lane):
+    most = jnp.max(jnp.abs(values), axis=1, keepdims=True)
+    exponent = jnp.maximum(jnp.ceil(jnp.log2(jnp.maximum(most, 1e-30) / 32766.0)), -120.0)
+    whole = jnp.round(values * jnp.exp2(-exponent))
+    lane = lax.broadcasted_iota(jnp.int32, values.shape, 1)
+    return jnp.where(lane == exponent_lane, exponent, whole).astype(jnp.int32).astype(jnp.int16)
 
 
 def products_kernel(nb, has_rest, *refs):
@@ -107,14 +115,11 @@
         )
         total[...] = part if j == 0 else total[...] + part
 
-    first = 0
-    if has_rest:
-        first = 1
-        out[:, pl.ds(1, 2)] = rest[...]
     for s in range(8):
         d, other = s // 2, s % 2
         chip = jnp.where(core == 0, yy + HALF - d, yy + d) % HALF
         block = chip * CORES + jnp.where(other == 0, core, 1 - core)
+        sums = []
         for b in range(nb):
             lanes = pl.ds(b * LANES, LANES)
             top = total[pl.ds(s * rows, half), lanes]
@@ -122,7 +127,12 @@
             turned = jnp.concatenate(
                 [low[:, half:rows], -low[:, :half], jnp.zeros((half, LANES - rows), jnp.float32)], axis=1
             )
-            out[block, 0 if has_rest else core ^ b] = top + turned
+            sums.append(top + turned)
+        if has_rest:
+            out[block] = scaled(jnp.concatenate([sums[0], rest[block, 0], rest[block, 1]], axis=0), rows)
+        else:
+            for b in range(nb):
+                out[block, core ^ b] = sums[b]
 
 
 def products(where, maps, lefts, rights, rest=None):
@@ -133,7 +143,9 @@
     extra = [] if rest is None else [rest]
     return pl.pallas_call(
         functools.partial(products_kernel, nb, rest is not None),
-        out_shape=jax.ShapeDtypeStruct((8, nb + 2 * len(extra), rows // 2, LANES), jnp.float32),
+        out_shape=jax.ShapeDtypeStruct((8, 3 * rows // 2, LANES), jnp.int16)
+        if extra
+        else jax.ShapeDtypeStruct((8, nb, rows // 2, LANES), jnp.float32),
         in_specs=[pl.BlockSpec(memory_space=pltpu.SMEM), vmem]
         + [anywhere] * (len(lefts) + nb)
         + [vmem] * len(extra),
@@ -162,12 +174,11 @@
 def per_device(coeffs, shift_maps):
     bands, _, width = coeffs.shape
     position = lax.axis_index("ka")
-    core = position % CORES
-    yy = position // CORES % HALF
+    core = position & 1
+    yy = (position >> 1) & (HALF - 1)
     where = jnp.stack([yy, core]).astype(jnp.int32)
-    kpoint = position // (CORES * HALF)
-    maps = lax.dynamic_index_in_dim(shift_maps, kpoint, 0, keepdims=False) % LANES
-    later_maps = jnp.where(core == 0, maps[1:], maps[:0:-1])
+    maps = lax.dynamic_index_in_dim(shift_maps, position >> 3, 0, keepdims=False) & (LANES - 1)
+    later_maps = jnp.where(core == 0, maps[1:], jnp.stack([maps[2], maps[1]]))
     mine = coeffs.transpose(1, 0, 2).reshape(2 * bands, width)
 
     sibling = moved(mine, to_sibling)
@@ -186,7 +197,9 @@
     later = products(where, later_maps, lefts, [za, zs])
     every = products(where, maps[:1], lefts, [opposite], later)
     shares = lax.all_to_all(every, "ga", 0, 0, tiled=True)
-    total = shares.sum(axis=0)[:, :, : 2 * bands]
+    rows = 2 * bands
+    units = jnp.exp2(shares[:, :, rows : rows + 1].astype(jnp.float32))
+    total = (shares[:, :, :rows].astype(jnp.float32) * units).sum(axis=0).reshape(3, bands, rows)
     return total.transpose(1, 0, 2).reshape(bands, 3, 2, bands)
 
 

time: 118 us -> 111 us (0.941)
  the two profiles are of different devices: /device:TPU:64 before, /device:TPU:96 now
where the time goes in v2:
time: 111 us; the launch traced here: 110 us
  starting transfers between devices  34.4 us (31%)
  waiting for transfers between devices  33.9 us (31%)
  blocking collectives  26.4 us (24%)
  Pallas kernels  11.8 us (11%)
  local copies, waits for them, and re-layouts  2.24 us (2%)
    ppermute x17, starting transfers between devices, moved(): return lax.ppermute(shard, 'ka', pairs)  34.4 us
    ppermute x17, waiting for transfers between devices, moved(): return lax.ppermute(shard, 'ka', pairs)  33.9 us
    all_to_all x1, blocking collectives, per_device(): shares = lax.all_to_all(every, 'ga', 0, 0, tiled=True)  26.4 us
    pallas_call x2, Pallas kernels, products(): pl.pallas_call(functools.partial(products_kernel, nb, rest is not None),...  11.8 us
  transfers between devices with their start and end apart: 17, of which 9 were waited for; matrix products, arithmetic and copies ran while one was open for 0% of the time, Pallas kernels for 5%

profile of v2, /device:TPU:96, one launch (start us, length us, event | category | flops | bytes accessed | tf_op | source)
XLA Modules:
  0.0 110.0 jit_solution(18091953105784868941)
XLA Ops:
  0.0 1.3 %copy.6 = bf16[2,56,3840]{2,1,0:T(8,128)(2,1)S(1)} copy(bf16[2,56,3840]{2,0,1:T(2,128)(2,1)} %bitcast.24) | data formatting | bytes 1720320 | tf_op jit(solution)/shard_map/transpose | solution.py:182
  1.3 1.9 %collective-permute-start = (bf16[112,3840]{1,0:T(8,128)(2,1)S(1)}, bf16[112,3840]{1,0:T(8,128)(2,1)S(1)}, u32[]{:S(2)}, u32[]{:S(2)}) collective-permute-start(bf16[112,3840]{1,0:T(8,128)(2,1)S(1)} %bitcast.19), channel_id=1, source_target_pairs={{0,8},{8,0},{16,24},{24,16},{32,40},{40,32},{48,56},{56,48},{64,72... | collective-permute-start | bytes 2580488 | tf_op jit(solution)/shard_map/ppermute | solution.py:28
  3.2 2.6 %collective-permute-start.1 = (bf16[112,3840]{1,0:T(8,128)(2,1)S(1)}, bf16[112,3840]{1,0:T(8,128)(2,1)S(1)}, u32[]{:S(2)}, u32[]{:S(2)}) collective-permute-start(bf16[112,3840]{1,0:T(8,128)(2,1)S(1)} %bitcast.20), channel_id=1, source_target_pairs={{0,16},{8,120},{16,32},{24,8},{32,48},{40,24},{48,64},{56,40},{64,... | collective-permute-start | bytes 2580488 | tf_op jit(solution)/shard_map/ppermute | solution.py:28
  5.8 2.6 %collective-permute-start.5 = (bf16[112,3840]{1,0:T(8,128)(2,1)S(1)}, bf16[112,3840]{1,0:T(8,128)(2,1)}, u32[]{:S(2)}, u32[]{:S(2)}) collective-permute-start(bf16[112,3840]{1,0:T(8,128)(2,1)S(1)} %collective-permute-done.refs_3_), channel_id=1, source_target_pairs={{0,16},{8,120},{16,32},{24,8},{32,48},{40,24},{48,64},{56,40},{64,... | collective-permute-start | bytes 2580488 | tf_op jit(solution)/shard_map/ppermute | solution.py:28
  8.4 1.9 %collective-permute-start.3 = (bf16[112,3840]{1,0:T(8,128)(2,1)S(1)}, bf16[112,3840]{1,0:T(8,128)(2,1)}, u32[]{:S(2)}, u32[]{:S(2)}) collective-permute-start(bf16[112,3840]{1,0:T(8,128)(2,1)S(1)} %bitcast.21), channel_id=1, source_target_pairs={{0,128},{8,264},{16,144},{24,280},{32,160},{40,296},{48,176},{56,3... | collective-permute-start | bytes 2580488 | tf_op jit(solution)/shard_map/ppermute | solution.py:28
  10.5 8.6 %collective-permute-done.1.refs_4_ = bf16[112,3840]{1,0:T(8,128)(2,1)S(1)} collective-permute-done((bf16[112,3840]{1,0:T(8,128)(2,1)S(1)}, bf16[112,3840]{1,0:T(8,128)(2,1)S(1)}, u32[]{:S(2)}, u32[]{:S(2)}) %collective-permute-start.1) | collective-permute-done | bytes 860192 | tf_op jit(solution)/shard_map/ppermute | solution.py:28
  19.1 1.9 %collective-permute-start.2 = (bf16[112,3840]{1,0:T(8,128)(2,1)S(1)}, bf16[112,3840]{1,0:T(8,128)(2,1)S(1)}, u32[]{:S(2)}, u32[]{:S(2)}) collective-permute-start(bf16[112,3840]{1,0:T(8,128)(2,1)S(1)} %collective-permute-done.1.refs_4_), channel_id=1, source_target_pairs={{0,16},{8,120},{16,32},{24,8},{32,48},{40,24},{48,64},{56,40},{64,... | collective-permute-start | bytes 2580488 | tf_op jit(solution)/shard_map/ppermute | solution.py:28
  21.0 1.3 %collective-permute-start.4 = (bf16[112,3840]{1,0:T(8,128)(2,1)S(1)}, bf16[112,3840]{1,0:T(8,128)(2,1)S(1)}, u32[]{:S(2)}, u32[]{:S(2)}) collective-permute-start(bf16[112,3840]{1,0:T(8,128)(2,1)S(1)} %collective-permute-done.1.refs_4_), channel_id=1, source_target_pairs={{8,0},{16,24},{24,16},{32,40},{40,32},{48,56},{72,64},{80,88},{88,... | collective-permute-start | bytes 2580488 | tf_op jit(solution)/shard_map/ppermute | solution.py:28
  22.3 6.1 %collective-permute-done.5.refs_7_ = bf16[112,3840]{1,0:T(8,128)(2,1)} collective-permute-done((bf16[112,3840]{1,0:T(8,128)(2,1)S(1)}, bf16[112,3840]{1,0:T(8,128)(2,1)}, u32[]{:S(2)}, u32[]{:S(2)}) %collective-permute-start.5) | collective-permute-done | bytes 860192 | tf_op jit(solution)/shard_map/ppermute | solution.py:28
  28.4 1.9 %collective-permute-start.8 = (bf16[112,3840]{1,0:T(8,128)(2,1)}, bf16[112,3840]{1,0:T(8,128)(2,1)S(1)}, u32[]{:S(2)}, u32[]{:S(2)}) collective-permute-start(bf16[112,3840]{1,0:T(8,128)(2,1)} %collective-permute-done.5.refs_7_), channel_id=1, source_target_pairs={{0,16},{8,120},{16,32},{24,8},{32,48},{40,24},{48,64},{56,40},{64,... | collective-permute-start | bytes 2580488 | tf_op jit(solution)/shard_map/ppermute | solution.py:28
  30.4 1.3 %collective-permute-start.6 = (bf16[112,3840]{1,0:T(8,128)(2,1)}, bf16[112,3840]{1,0:T(8,128)(2,1)S(1)}, u32[]{:S(2)}, u32[]{:S(2)}) collective-permute-start(bf16[112,3840]{1,0:T(8,128)(2,1)} %collective-permute-done.5.refs_7_), channel_id=1, source_target_pairs={{8,0},{16,24},{24,16},{32,40},{40,32},{48,56},{72,64},{80,88},{88,... | collective-permute-start | bytes 2580488 | tf_op jit(solution)/shard_map/ppermute | solution.py:28
  32.1 2.2 %collective-permute-start.14 = (bf16[112,3840]{1,0:T(8,128)(2,1)S(1)}, bf16[112,3840]{1,0:T(8,128)(2,1)S(1)}, u32[]{:S(2)}, u32[]{:S(2)}) collective-permute-start(bf16[112,3840]{1,0:T(8,128)(2,1)S(1)} %collective-permute-done.refs_3_), channel_id=1, source_target_pairs={{0,128},{8,264},{16,144},{24,280},{32,160},{40,296},{48,176},{56,3... | collective-permute-start | bytes 2580488 | tf_op jit(solution)/shard_map/ppermute | solution.py:28
  34.3 3.2 %collective-permute-done.2.refs_5_ = bf16[112,3840]{1,0:T(8,128)(2,1)S(1)} collective-permute-done((bf16[112,3840]{1,0:T(8,128)(2,1)S(1)}, bf16[112,3840]{1,0:T(8,128)(2,1)S(1)}, u32[]{:S(2)}, u32[]{:S(2)}) %collective-permute-start.2) | collective-permute-done | bytes 860192 | tf_op jit(solution)/shard_map/ppermute | solution.py:28
  38.9 1.9 %collective-permute-start.7 = (bf16[112,3840]{1,0:T(8,128)(2,1)S(1)}, bf16[112,3840]{1,0:T(8,128)(2,1)S(1)}, u32[]{:S(2)}, u32[]{:S(2)}) collective-permute-start(bf16[112,3840]{1,0:T(8,128)(2,1)S(1)} %collective-permute-done.2.refs_5_), channel_id=1, source_target_pairs={{0,16},{8,120},{16,32},{24,8},{32,48},{40,24},{48,64},{56,40},{64,... | collective-permute-start | bytes 2580488 | tf_op jit(solution)/shard_map/ppermute | solution.py:28
  40.8 6.0 %collective-permute-done.8.refs_8_ = bf16[112,3840]{1,0:T(8,128)(2,1)S(1)} collective-permute-done((bf16[112,3840]{1,0:T(8,128)(2,1)}, bf16[112,3840]{1,0:T(8,128)(2,1)S(1)}, u32[]{:S(2)}, u32[]{:S(2)}) %collective-permute-start.8) | collective-permute-done | bytes 860192 | tf_op jit(solution)/shard_map/ppermute | solution.py:28
  48.1 1.9 %collective-permute-start.9 = (bf16[112,3840]{1,0:T(8,128)(2,1)S(1)}, bf16[112,3840]{1,0:T(8,128)(2,1)S(1)}, u32[]{:S(2)}, u32[]{:S(2)}) collective-permute-start(bf16[112,3840]{1,0:T(8,128)(2,1)S(1)} %collective-permute-done.8.refs_8_), channel_id=1, source_target_pairs={{0,16},{8,120},{16,32},{24,8},{32,48},{40,24},{48,64},{56,40},{64,... | collective-permute-start | bytes 2580488 | tf_op jit(solution)/shard_map/ppermute | solution.py:28
  50.0 4.3 %collective-permute-done.14 = bf16[112,3840]{1,0:T(8,128)(2,1)S(1)} collective-permute-done((bf16[112,3840]{1,0:T(8,128)(2,1)S(1)}, bf16[112,3840]{1,0:T(8,128)(2,1)S(1)}, u32[]{:S(2)}, u32[]{:S(2)}) %collective-permute-start.14) | collective-permute-done | bytes 860192 | tf_op jit(solution)/shard_map/ppermute | solution.py:28
  54.3 5.9 %collective-permute-start.16 = (bf16[112,3840]{1,0:T(8,128)(2,1)S(1)}, bf16[112,3840]{1,0:T(8,128)(2,1)S(1)}, u32[]{:S(2)}, u32[]{:S(2)}) collective-permute-start(bf16[112,3840]{1,0:T(8,128)(2,1)S(1)} %collective-permute-done.14), channel_id=1, source_target_pairs={{0,8},{8,0},{16,24},{24,16},{32,40},{40,32},{48,56},{56,48},{64,72... | collective-permute-start | bytes 2580488 | tf_op jit(solution)/shard_map/ppermute | solution.py:28
  60.2 1.9 %collective-permute-start.15 = (bf16[112,3840]{1,0:T(8,128)(2,1)S(1)}, bf16[112,3840]{1,0:T(8,128)(2,1)S(1)}, u32[]{:S(2)}, u32[]{:S(2)}) collective-permute-start(bf16[112,3840]{1,0:T(8,128)(2,1)S(1)} %collective-permute-done.7.refs_6_), channel_id=1, source_target_pairs={{0,16},{8,120},{16,32},{24,8},{32,48},{40,24},{48,64},{56,40},{64,... | collective-permute-start | bytes 2580488 | tf_op jit(solution)/shard_map/ppermute | solution.py:28
  63.5 1.7 %collective-permute-done.9.refs_9_ = bf16[112,3840]{1,0:T(8,128)(2,1)S(1)} collective-permute-done((bf16[112,3840]{1,0:T(8,128)(2,1)S(1)}, bf16[112,3840]{1,0:T(8,128)(2,1)S(1)}, u32[]{:S(2)}, u32[]{:S(2)}) %collective-permute-start.9) | collective-permute-done | bytes 860192 | tf_op jit(solution)/shard_map/ppermute | solution.py:28
  66.5 2.9 %collective-permute-done.13.refs_15_ = bf16[112,3840]{1,0:T(8,128)(2,1)S(1)} collective-permute-done((bf16[112,3840]{1,0:T(8,128)(2,1)S(1)}, bf16[112,3840]{1,0:T(8,128)(2,1)S(1)}, u32[]{:S(2)}, u32[]{:S(2)}) %collective-permute-start.13) | collective-permute-done | bytes 860192 | tf_op jit(solution)/shard_map/ppermute | solution.py:28
  69.5 6.0 %shard_map.28.refs_17_ = f32[8,2,56,128]{3,2,1,0:T(8,128)S(1)} custom-call(s32[2]{0:T(128)S(1)} %pad_add_fusion.refs_0_, s32[2,3840]{1,0:T(2,128)S(1)} %fusion.refs_1_, bf16[112,3840]{1,0:T(8,128)(2,1)S(1)} %bitcast.22, bf16[112,3840]{1,0:T(8,128)(2,1)S(1)} %collective-permute-done.refs_3_, bf16[112,3840]{1,0:T(8,128)(2,1)S(1)} %collective-permute-done.1.refs_4_, ...), custom_call_target="tpu_custom_call" | custom-call | flops 1761607680 | bytes 8601600 | tf_op jit(solution)/shard_map/pallas_call | solution.py:144
  76.1 5.8 %shard_map.29 = s16[8,168,128]{2,1,0:T(8,128)(2,1)S(1)} custom-call(s32[2]{0:T(128)S(1)} %pad_add_fusion.refs_0_, s32[1,3840]{1,0:T(1,128)S(1)} %get-tuple-element.13.refs_1_, bf16[112,3840]{1,0:T(8,128)(2,1)S(1)} %bitcast.23, bf16[112,3840]{1,0:T(8,128)(2,1)S(1)} %collective-permute-done.refs_3_, bf16[112,3840]{1,0:T(8,128)(2,1)S(1)} %collective-permute-done.1.refs_4_, ...), custom_call_target="tpu_custom_call" | custom-call | flops 880803840 | bytes 7741440 | tf_op jit(solution)/shard_map/pallas_call | solution.py:144
  81.9 26.4 %all_to_all.5 = s16[8,168,128]{2,1,0:T(8,128)(2,1)S(1)} all-to-all(s16[8,168,128]{2,1,0:T(8,128)(2,1)S(1)} %shard_map.29), channel_id=1, replica_groups=mesh['ka'=64,'ga'=8] {'ga'}, dimensions={0} | all-to-all | bytes 688128 | tf_op jit(solution)/shard_map/all_to_all | solution.py:199
  (25 shorter events, 8.1 us)
Async XLA Ops:
  0.0 10.4 %copy-start = (s32[8,3,3840]{2,0,1:T(8,128)S(1)}, s32[8,3,3840]{2,0,1:T(8,128)}, u32[]{:S(2)}) copy-start(s32[8,3,3840]{2,0,1:T(8,128)} %param.3) | copy-start | bytes 1105924
  1.3 4.5 %collective-permute-start = (bf16[112,3840]{1,0:T(8,128)(2,1)S(1)}, bf16[112,3840]{1,0:T(8,128)(2,1)S(1)}, u32[]{:S(2)}, u32[]{:S(2)}) collective-permute-start(bf16[112,3840]{1,0:T(8,128)(2,1)S(1)} %bitcast.19), channel_id=1, source_target_pairs={{0,8},{8,0},{16,24},{24,16},{32,40},{40,32},{48,56},{56,48},{64,72... | collective-permute-start | bytes 2580488 | tf_op jit(solution)/shard_map/ppermute | solution.py:28
  3.2 15.9 %collective-permute-start.1 = (bf16[112,3840]{1,0:T(8,128)(2,1)S(1)}, bf16[112,3840]{1,0:T(8,128)(2,1)S(1)}, u32[]{:S(2)}, u32[]{:S(2)}) collective-permute-start(bf16[112,3840]{1,0:T(8,128)(2,1)S(1)} %bitcast.20), channel_id=1, source_target_pairs={{0,16},{8,120},{16,32},{24,8},{32,48},{40,24},{48,64},{56,40},{64,... | collective-permute-start | bytes 2580488 | tf_op jit(solution)/shard_map/ppermute | solution.py:28
  5.8 22.6 %collective-permute-start.5 = (bf16[112,3840]{1,0:T(8,128)(2,1)S(1)}, bf16[112,3840]{1,0:T(8,128)(2,1)}, u32[]{:S(2)}, u32[]{:S(2)}) collective-permute-start(bf16[112,3840]{1,0:T(8,128)(2,1)S(1)} %collective-permute-done.refs_3_), channel_id=1, source_target_pairs={{0,16},{8,120},{16,32},{24,8},{32,48},{40,24},{48,64},{56,40},{64,... | collective-permute-start | bytes 2580488 | tf_op jit(solution)/shard_map/ppermute | solution.py:28
  8.4 23.7 %collective-permute-start.3 = (bf16[112,3840]{1,0:T(8,128)(2,1)S(1)}, bf16[112,3840]{1,0:T(8,128)(2,1)}, u32[]{:S(2)}, u32[]{:S(2)}) collective-permute-start(bf16[112,3840]{1,0:T(8,128)(2,1)S(1)} %bitcast.21), channel_id=1, source_target_pairs={{0,128},{8,264},{16,144},{24,280},{32,160},{40,296},{48,176},{56,3... | collective-permute-start | bytes 2580488 | tf_op jit(solution)/shard_map/ppermute | solution.py:28
  19.1 18.4 %collective-permute-start.2 = (bf16[112,3840]{1,0:T(8,128)(2,1)S(1)}, bf16[112,3840]{1,0:T(8,128)(2,1)S(1)}, u32[]{:S(2)}, u32[]{:S(2)}) collective-permute-start(bf16[112,3840]{1,0:T(8,128)(2,1)S(1)} %collective-permute-done.1.refs_4_), channel_id=1, source_target_pairs={{0,16},{8,120},{16,32},{24,8},{32,48},{40,24},{48,64},{56,40},{64,... | collective-permute-start | bytes 2580488 | tf_op jit(solution)/shard_map/ppermute | solution.py:28
  21.0 17.8 %collective-permute-start.4 = (bf16[112,3840]{1,0:T(8,128)(2,1)S(1)}, bf16[112,3840]{1,0:T(8,128)(2,1)S(1)}, u32[]{:S(2)}, u32[]{:S(2)}) collective-permute-start(bf16[112,3840]{1,0:T(8,128)(2,1)S(1)} %collective-permute-done.1.refs_4_), channel_id=1, source_target_pairs={{8,0},{16,24},{24,16},{32,40},{40,32},{48,56},{72,64},{80,88},{88,... | collective-permute-start | bytes 2580488 | tf_op jit(solution)/shard_map/ppermute | solution.py:28
  28.4 18.3 %collective-permute-start.8 = (bf16[112,3840]{1,0:T(8,128)(2,1)}, bf16[112,3840]{1,0:T(8,128)(2,1)S(1)}, u32[]{:S(2)}, u32[]{:S(2)}) collective-permute-start(bf16[112,3840]{1,0:T(8,128)(2,1)} %collective-permute-done.5.refs_7_), channel_id=1, source_target_pairs={{0,16},{8,120},{16,32},{24,8},{32,48},{40,24},{48,64},{56,40},{64,... | collective-permute-start | bytes 2580488 | tf_op jit(solution)/shard_map/ppermute | solution.py:28
  30.4 8.5 %collective-permute-start.6 = (bf16[112,3840]{1,0:T(8,128)(2,1)}, bf16[112,3840]{1,0:T(8,128)(2,1)S(1)}, u32[]{:S(2)}, u32[]{:S(2)}) collective-permute-start(bf16[112,3840]{1,0:T(8,128)(2,1)} %collective-permute-done.5.refs_7_), channel_id=1, source_target_pairs={{8,0},{16,24},{24,16},{32,40},{40,32},{48,56},{72,64},{80,88},{88,... | collective-permute-start | bytes 2580488 | tf_op jit(solution)/shard_map/ppermute | solution.py:28
  32.1 22.2 %collective-permute-start.14 = (bf16[112,3840]{1,0:T(8,128)(2,1)S(1)}, bf16[112,3840]{1,0:T(8,128)(2,1)S(1)}, u32[]{:S(2)}, u32[]{:S(2)}) collective-permute-start(bf16[112,3840]{1,0:T(8,128)(2,1)S(1)} %collective-permute-done.refs_3_), channel_id=1, source_target_pairs={{0,128},{8,264},{16,144},{24,280},{32,160},{40,296},{48,176},{56,3... | collective-permute-start | bytes 2580488 | tf_op jit(solution)/shard_map/ppermute | solution.py:28
  37.5 22.6 %collective-permute-start.10 = (bf16[112,3840]{1,0:T(8,128)(2,1)S(1)}, bf16[112,3840]{1,0:T(8,128)(2,1)S(1)}, u32[]{:S(2)}, u32[]{:S(2)}) collective-permute-start(bf16[112,3840]{1,0:T(8,128)(2,1)S(1)} %collective-permute-done.2.refs_5_), channel_id=1, source_target_pairs={{8,0},{24,16},{32,40},{48,56},{72,64},{88,80},{96,104},{112,120},{... | collective-permute-start | bytes 2580488 | tf_op jit(solution)/shard_map/ppermute | solution.py:28
  38.9 21.4 %collective-permute-start.7 = (bf16[112,3840]{1,0:T(8,128)(2,1)S(1)}, bf16[112,3840]{1,0:T(8,128)(2,1)S(1)}, u32[]{:S(2)}, u32[]{:S(2)}) collective-permute-start(bf16[112,3840]{1,0:T(8,128)(2,1)S(1)} %collective-permute-done.2.refs_5_), channel_id=1, source_target_pairs={{0,16},{8,120},{16,32},{24,8},{32,48},{40,24},{48,64},{56,40},{64,... | collective-permute-start | bytes 2580488 | tf_op jit(solution)/shard_map/ppermute | solution.py:28
  46.8 13.4 %collective-permute-start.12 = (bf16[112,3840]{1,0:T(8,128)(2,1)S(1)}, bf16[112,3840]{1,0:T(8,128)(2,1)S(1)}, u32[]{:S(2)}, u32[]{:S(2)}) collective-permute-start(bf16[112,3840]{1,0:T(8,128)(2,1)S(1)} %collective-permute-done.8.refs_8_), channel_id=1, source_target_pairs={{8,0},{24,16},{32,40},{48,56},{72,64},{88,80},{96,104},{112,120},{... | collective-permute-start | bytes 2580488 | tf_op jit(solution)/shard_map/ppermute | solution.py:28
  48.1 17.1 %collective-permute-start.9 = (bf16[112,3840]{1,0:T(8,128)(2,1)S(1)}, bf16[112,3840]{1,0:T(8,128)(2,1)S(1)}, u32[]{:S(2)}, u32[]{:S(2)}) collective-permute-start(bf16[112,3840]{1,0:T(8,128)(2,1)S(1)} %collective-permute-done.8.refs_8_), channel_id=1, source_target_pairs={{0,16},{8,120},{16,32},{24,8},{32,48},{40,24},{48,64},{56,40},{64,... | collective-permute-start | bytes 2580488 | tf_op jit(solution)/shard_map/ppermute | solution.py:28
  54.3 12.2 %collective-permute-start.16 = (bf16[112,3840]{1,0:T(8,128)(2,1)S(1)}, bf16[112,3840]{1,0:T(8,128)(2,1)S(1)}, u32[]{:S(2)}, u32[]{:S(2)}) collective-permute-start(bf16[112,3840]{1,0:T(8,128)(2,1)S(1)} %collective-permute-done.14), channel_id=1, source_target_pairs={{0,8},{8,0},{16,24},{24,16},{32,40},{40,32},{48,56},{56,48},{64,72... | collective-permute-start | bytes 2580488 | tf_op jit(solution)/shard_map/ppermute | solution.py:28
  60.2 15.9 %collective-permute-start.15 = (bf16[112,3840]{1,0:T(8,128)(2,1)S(1)}, bf16[112,3840]{1,0:T(8,128)(2,1)S(1)}, u32[]{:S(2)}, u32[]{:S(2)}) collective-permute-start(bf16[112,3840]{1,0:T(8,128)(2,1)S(1)} %collective-permute-done.7.refs_6_), channel_id=1, source_target_pairs={{0,16},{8,120},{16,32},{24,8},{32,48},{40,24},{48,64},{56,40},{64,... | collective-permute-start | bytes 2580488 | tf_op jit(solution)/shard_map/ppermute | solution.py:28
  62.2 7.3 %collective-permute-start.11 = (bf16[112,3840]{1,0:T(8,128)(2,1)S(1)}, bf16[112,3840]{1,0:T(8,128)(2,1)S(1)}, u32[]{:S(2)}, u32[]{:S(2)}) collective-permute-start(bf16[112,3840]{1,0:T(8,128)(2,1)S(1)} %collective-permute-done.7.refs_6_), channel_id=1, source_target_pairs={{8,0},{48,56},{72,64},{112,120},{136,128},{176,184},{200,192},{240... | collective-permute-start | bytes 2580488 | tf_op jit(solution)/shard_map/ppermute | solution.py:28
  65.2 4.3 %collective-permute-start.13 = (bf16[112,3840]{1,0:T(8,128)(2,1)S(1)}, bf16[112,3840]{1,0:T(8,128)(2,1)S(1)}, u32[]{:S(2)}, u32[]{:S(2)}) collective-permute-start(bf16[112,3840]{1,0:T(8,128)(2,1)S(1)} %collective-permute-done.9.refs_9_), channel_id=1, source_target_pairs={{8,0},{48,56},{72,64},{112,120},{136,128},{176,184},{200,192},{240... | collective-permute-start | bytes 2580488 | tf_op jit(solution)/shard_map/ppermute | solution.py:28

commit v3 on v2

--- a/solution.py
+++ b/solution.py
@@ -53,6 +53,15 @@
     whole = jnp.round(values * jnp.exp2(-exponent))
     lane = lax.broadcasted_iota(jnp.int32, values.shape, 1)
     return jnp.where(lane == exponent_lane, exponent, whole).astype(jnp.int32).astype(jnp.int16)
+
+
+def chosen_rows(shift, raw):
+    inside = lax.broadcasted_iota(jnp.int32, (LANES, LANES), 0)
+    chosen = jnp.where(inside == shift, 1.0, 0.0).astype(jnp.bfloat16)
+    return jnp.dot(raw, chosen, preferred_element_type=jnp.float32).astype(jnp.bfloat16)
+
+
+CHUNKS = 1
 
 
 def products_kernel(nb, has_rest, *refs):
@@ -67,54 +76,52 @@
     out, left, raw, right, total, left_sems, raw_sems = refs
     rows, width = own.shape
     half = rows // 2
+    chunk = width // CHUNKS
     yy, core = where[0], where[1]
     reach = jnp.where(core == 0, yy, HALF - 1 - yy)
 
-    def slot(s):
-        return left.at[pl.ds(s * rows, rows)]
+    def copy(source, s, j):
+        at = pl.ds(j * chunk, chunk)
+        return pltpu.make_async_copy(
+            source.at[:, at], left.at[pl.ds(s * rows, rows), at], left_sems.at[s, j]
+        )
 
     for b in range(nb):
         pltpu.make_async_copy(rights[b], raw.at[b], raw_sems.at[b]).start()
-    pltpu.make_async_copy(own, slot(0), left_sems.at[0]).start()
-    pltpu.make_async_copy(sibling, slot(1), left_sems.at[1]).start()
-    for d in range(1, HALF):
-        for part, (near, far) in enumerate(((ga, sb), (gb, sa))):
-            s = 2 * d + part
-
-            @pl.when(d <= reach)
-            def _():
-                pltpu.make_async_copy(near[d - 1], slot(s), left_sems.at[s]).start()
-
-            @pl.when(d > reach)
-            def _():
-                pltpu.make_async_copy(far[HALF - d - 1], slot(s), left_sems.at[s]).start()
-
-    right[...] = jnp.zeros_like(right)
-    inside = lax.broadcasted_iota(jnp.int32, (LANES, LANES), 0)
+    for j in range(CHUNKS):
+        copy(own, 0, j).start()
+        copy(sibling, 1, j).start()
+        for d in range(1, HALF):
+            for part, (near, far) in enumerate(((ga, sb), (gb, sa))):
+
+                @pl.when(d <= reach)
+                def _():
+                    copy(near[d - 1], 2 * d + part, j).start()
+
+                @pl.when(d > reach)
+                def _():
+                    copy(far[HALF - d - 1], 2 * d + part, j).start()
+
+    spare = jnp.zeros((LANES - rows, width), jnp.bfloat16)
+    for b in range(nb):
+        right[pl.ds(b * LANES + rows, LANES - rows)] = spare
     for b in range(nb):
         pltpu.make_async_copy(rights[b], raw.at[b], raw_sems.at[b]).wait()
-    blocks = 5
-
-    @pl.loop(0, width // (LANES * blocks))
-    def _(j):
-        for i in range(blocks):
-            at = pl.ds(pl.multiple_of((j * blocks + i) * LANES, LANES), LANES)
-            for b in range(nb):
-                chosen = jnp.where(inside == maps[b : b + 1, at], 1.0, 0.0).astype(jnp.bfloat16)
-                right[pl.ds(b * LANES, rows), at] = jnp.dot(
-                    raw[b, :, at], chosen, preferred_element_type=jnp.float32
-                ).astype(jnp.bfloat16)
-
-    for s in range(8):
-        pltpu.make_async_copy(own, slot(s), left_sems.at[s]).wait()
-    chunk = 1280
-    for j in range(width // chunk):
+    for i in range(width // LANES):
+        at = pl.ds(i * LANES, LANES)
+        for b in range(nb):
+            right[pl.ds(b * LANES, rows), at] = chosen_rows(maps[b : b + 1, at], raw[b, :, at])
+    for j in range(CHUNKS):
         at = pl.ds(j * chunk, chunk)
+        for s in range(8):
+            copy(own, s, j).wait()
         part = lax.dot_general(
             left[:, at], right[:, at], (((1,), (1,)), ((), ())), preferred_element_type=jnp.float32
         )
         total[...] = part if j == 0 else total[...] + part
 
+    if has_rest:
+        out[:, pl.ds(0, rows)] = rest[...]
     for s in range(8):
         d, other = s // 2, s % 2
         chip = jnp.where(core == 0, yy + HALF - d, yy + d) % HALF
@@ -129,10 +136,12 @@
             )
             sums.append(top + turned)
         if has_rest:
-            out[block] = scaled(jnp.concatenate([sums[0], rest[block, 0], rest[block, 1]], axis=0), rows)
+            spare_rows = jnp.zeros((64 - half, LANES), jnp.float32)
+            out[block, pl.ds(rows, 64)] = scaled(jnp.concatenate([sums[0], spare_rows], axis=0), rows)
         else:
-            for b in range(nb):
-                out[block, core ^ b] = sums[b]
+            first = jnp.where(core == 0, sums[0], sums[1])
+            second = jnp.where(core == 0, sums[1], sums[0])
+            out[block] = scaled(jnp.concatenate([first, second], axis=0), rows)
 
 
 def products(where, maps, lefts, rights, rest=None):
@@ -143,9 +152,7 @@
     extra = [] if rest is None else [rest]
     return pl.pallas_call(
         functools.partial(products_kernel, nb, rest is not None),
-        out_shape=jax.ShapeDtypeStruct((8, 3 * rows // 2, LANES), jnp.int16)
-        if extra
-        else jax.ShapeDtypeStruct((8, nb, rows // 2, LANES), jnp.float32),
+        out_shape=jax.ShapeDtypeStruct((8, rows + 64 if extra else rows, LANES), jnp.int16),
         in_specs=[pl.BlockSpec(memory_space=pltpu.SMEM), vmem]
         + [anywhere] * (len(lefts) + nb)
         + [vmem] * len(extra),
@@ -155,7 +162,7 @@
             pltpu.VMEM((nb, rows, width), jnp.bfloat16),
             pltpu.VMEM((nb * LANES, width), jnp.bfloat16),
             pltpu.VMEM((8 * rows, nb * LANES), jnp.float32),
-            pltpu.SemaphoreType.DMA((8,)),
+            pltpu.SemaphoreType.DMA((8, CHUNKS)),
             pltpu.SemaphoreType.DMA((nb,)),
         ],
         compiler_params=pltpu.CompilerParams(vmem_limit_bytes=40 * 2**20),
@@ -198,9 +205,10 @@
     every = products(where, maps[:1], lefts, [opposite], later)
     shares = lax.all_to_all(every, "ga", 0, 0, tiled=True)
     rows = 2 * bands
-    units = jnp.exp2(shares[:, :, rows : rows + 1].astype(jnp.float32))
-    total = (shares[:, :, :rows].astype(jnp.float32) * units).sum(axis=0).reshape(3, bands, rows)
-    return total.transpose(1, 0, 2).reshape(bands, 3, 2, bands)
+    units = jnp.exp2(shares[:, : 3 * bands, rows : rows + 1].astype(jnp.float32))
+    total = (shares[:, : 3 * bands, :rows].astype(jnp.float32) * units).sum(axis=0)
+    second, third, first = total[:bands], total[bands:rows], total[rows:]
+    return jnp.stack([first, second, third], axis=1).reshape(bands, 3, 2, bands)
 
 
 def solution(mesh):

time: 111 us -> 109 us (0.982)
  Pallas kernels: 11.8 us -> 10.4 us
    pallas_call x2, Pallas kernels: 11.8 us -> 10.4 us  [products(): pl.pallas_call(functools.partial(products_kernel, nb, rest is not None),...]
where the time goes in v3:
time: 109 us
  waiting for transfers between devices  34.5 us (32%)
  starting transfers between devices  34.4 us (32%)
  blocking collectives  26 us (24%)
  Pallas kernels  10.4 us (10%)
  other arithmetic  1.73 us (2%)
  local copies, waits for them, and re-layouts  1.65 us (2%)
    ppermute x17, waiting for transfers between devices, moved(): return lax.ppermute(shard, 'ka', pairs)  34.5 us
    ppermute x17, starting transfers between devices, moved(): return lax.ppermute(shard, 'ka', pairs)  34.4 us
    all_to_all x1, blocking collectives, per_device(): shares = lax.all_to_all(every, 'ga', 0, 0, tiled=True)  26 us
    pallas_call x2, Pallas kernels, products(): pl.pallas_call(functools.partial(products_kernel, nb, rest is not None),...  10.4 us
  transfers between devices with their start and end apart: 17, of which 9 were waited for; matrix products, arithmetic and copies ran while one was open for 0% of the time, Pallas kernels for 5%

profile of v3, /device:TPU:96, one launch (start us, length us, event | category | flops | bytes accessed | tf_op | source)
XLA Modules:
  0.0 108.9 jit_solution(17813413754125025508)
XLA Ops:
  0.0 1.3 %copy.6 = bf16[2,56,3840]{2,1,0:T(8,128)(2,1)S(1)} copy(bf16[2,56,3840]{2,0,1:T(2,128)(2,1)} %bitcast.19) | data formatting | bytes 1720320 | tf_op jit(solution)/shard_map/transpose | solution.py:189
  1.3 1.9 %collective-permute-start = (bf16[112,3840]{1,0:T(8,128)(2,1)S(1)}, bf16[112,3840]{1,0:T(8,128)(2,1)S(1)}, u32[]{:S(2)}, u32[]{:S(2)}) collective-permute-start(bf16[112,3840]{1,0:T(8,128)(2,1)S(1)} %bitcast.14), channel_id=1, source_target_pairs={{0,8},{8,0},{16,24},{24,16},{32,40},{40,32},{48,56},{56,48},{64,72... | collective-permute-start | bytes 2580488 | tf_op jit(solution)/shard_map/ppermute | solution.py:28
  3.2 2.6 %collective-permute-start.1 = (bf16[112,3840]{1,0:T(8,128)(2,1)S(1)}, bf16[112,3840]{1,0:T(8,128)(2,1)S(1)}, u32[]{:S(2)}, u32[]{:S(2)}) collective-permute-start(bf16[112,3840]{1,0:T(8,128)(2,1)S(1)} %bitcast.15), channel_id=1, source_target_pairs={{0,16},{8,120},{16,32},{24,8},{32,48},{40,24},{48,64},{56,40},{64,... | collective-permute-start | bytes 2580488 | tf_op jit(solution)/shard_map/ppermute | solution.py:28
  5.8 2.6 %collective-permute-start.5 = (bf16[112,3840]{1,0:T(8,128)(2,1)S(1)}, bf16[112,3840]{1,0:T(8,128)(2,1)}, u32[]{:S(2)}, u32[]{:S(2)}) collective-permute-start(bf16[112,3840]{1,0:T(8,128)(2,1)S(1)} %collective-permute-done.refs_3_), channel_id=1, source_target_pairs={{0,16},{8,120},{16,32},{24,8},{32,48},{40,24},{48,64},{56,40},{64,... | collective-permute-start | bytes 2580488 | tf_op jit(solution)/shard_map/ppermute | solution.py:28
  8.4 1.9 %collective-permute-start.3 = (bf16[112,3840]{1,0:T(8,128)(2,1)S(1)}, bf16[112,3840]{1,0:T(8,128)(2,1)}, u32[]{:S(2)}, u32[]{:S(2)}) collective-permute-start(bf16[112,3840]{1,0:T(8,128)(2,1)S(1)} %bitcast.16), channel_id=1, source_target_pairs={{0,128},{8,264},{16,144},{24,280},{32,160},{40,296},{48,176},{56,3... | collective-permute-start | bytes 2580488 | tf_op jit(solution)/shard_map/ppermute | solution.py:28
  10.5 8.6 %collective-permute-done.1.refs_4_ = bf16[112,3840]{1,0:T(8,128)(2,1)S(1)} collective-permute-done((bf16[112,3840]{1,0:T(8,128)(2,1)S(1)}, bf16[112,3840]{1,0:T(8,128)(2,1)S(1)}, u32[]{:S(2)}, u32[]{:S(2)}) %collective-permute-start.1) | collective-permute-done | bytes 860192 | tf_op jit(solution)/shard_map/ppermute | solution.py:28
  19.1 1.9 %collective-permute-start.2 = (bf16[112,3840]{1,0:T(8,128)(2,1)S(1)}, bf16[112,3840]{1,0:T(8,128)(2,1)S(1)}, u32[]{:S(2)}, u32[]{:S(2)}) collective-permute-start(bf16[112,3840]{1,0:T(8,128)(2,1)S(1)} %collective-permute-done.1.refs_4_), channel_id=1, source_target_pairs={{0,16},{8,120},{16,32},{24,8},{32,48},{40,24},{48,64},{56,40},{64,... | collective-permute-start | bytes 2580488 | tf_op jit(solution)/shard_map/ppermute | solution.py:28
  21.0 1.3 %collective-permute-start.4 = (bf16[112,3840]{1,0:T(8,128)(2,1)S(1)}, bf16[112,3840]{1,0:T(8,128)(2,1)S(1)}, u32[]{:S(2)}, u32[]{:S(2)}) collective-permute-start(bf16[112,3840]{1,0:T(8,128)(2,1)S(1)} %collective-permute-done.1.refs_4_), channel_id=1, source_target_pairs={{8,0},{16,24},{24,16},{32,40},{40,32},{48,56},{72,64},{80,88},{88,... | collective-permute-start | bytes 2580488 | tf_op jit(solution)/shard_map/ppermute | solution.py:28
  22.3 6.1 %collective-permute-done.5.refs_7_ = bf16[112,3840]{1,0:T(8,128)(2,1)} collective-permute-done((bf16[112,3840]{1,0:T(8,128)(2,1)S(1)}, bf16[112,3840]{1,0:T(8,128)(2,1)}, u32[]{:S(2)}, u32[]{:S(2)}) %collective-permute-start.5) | collective-permute-done | bytes 860192 | tf_op jit(solution)/shard_map/ppermute | solution.py:28
  28.4 1.9 %collective-permute-start.8 = (bf16[112,3840]{1,0:T(8,128)(2,1)}, bf16[112,3840]{1,0:T(8,128)(2,1)S(1)}, u32[]{:S(2)}, u32[]{:S(2)}) collective-permute-start(bf16[112,3840]{1,0:T(8,128)(2,1)} %collective-permute-done.5.refs_7_), channel_id=1, source_target_pairs={{0,16},{8,120},{16,32},{24,8},{32,48},{40,24},{48,64},{56,40},{64,... | collective-permute-start | bytes 2580488 | tf_op jit(solution)/shard_map/ppermute | solution.py:28
  30.4 1.3 %collective-permute-start.6 = (bf16[112,3840]{1,0:T(8,128)(2,1)}, bf16[112,3840]{1,0:T(8,128)(2,1)S(1)}, u32[]{:S(2)}, u32[]{:S(2)}) collective-permute-start(bf16[112,3840]{1,0:T(8,128)(2,1)} %collective-permute-done.5.refs_7_), channel_id=1, source_target_pairs={{8,0},{16,24},{24,16},{32,40},{40,32},{48,56},{72,64},{80,88},{88,... | collective-permute-start | bytes 2580488 | tf_op jit(solution)/shard_map/ppermute | solution.py:28
  32.1 2.2 %collective-permute-start.14 = (bf16[112,3840]{1,0:T(8,128)(2,1)S(1)}, bf16[112,3840]{1,0:T(8,128)(2,1)S(1)}, u32[]{:S(2)}, u32[]{:S(2)}) collective-permute-start(bf16[112,3840]{1,0:T(8,128)(2,1)S(1)} %collective-permute-done.refs_3_), channel_id=1, source_target_pairs={{0,128},{8,264},{16,144},{24,280},{32,160},{40,296},{48,176},{56,3... | collective-permute-start | bytes 2580488 | tf_op jit(solution)/shard_map/ppermute | solution.py:28
  34.3 3.2 %collective-permute-done.2.refs_5_ = bf16[112,3840]{1,0:T(8,128)(2,1)S(1)} collective-permute-done((bf16[112,3840]{1,0:T(8,128)(2,1)S(1)}, bf16[112,3840]{1,0:T(8,128)(2,1)S(1)}, u32[]{:S(2)}, u32[]{:S(2)}) %collective-permute-start.2) | collective-permute-done | bytes 860192 | tf_op jit(solution)/shard_map/ppermute | solution.py:28
  38.9 1.9 %collective-permute-start.7 = (bf16[112,3840]{1,0:T(8,128)(2,1)S(1)}, bf16[112,3840]{1,0:T(8,128)(2,1)S(1)}, u32[]{:S(2)}, u32[]{:S(2)}) collective-permute-start(bf16[112,3840]{1,0:T(8,128)(2,1)S(1)} %collective-permute-done.2.refs_5_), channel_id=1, source_target_pairs={{0,16},{8,120},{16,32},{24,8},{32,48},{40,24},{48,64},{56,40},{64,... | collective-permute-start | bytes 2580488 | tf_op jit(solution)/shard_map/ppermute | solution.py:28
  40.8 6.0 %collective-permute-done.8.refs_8_ = bf16[112,3840]{1,0:T(8,128)(2,1)S(1)} collective-permute-done((bf16[112,3840]{1,0:T(8,128)(2,1)}, bf16[112,3840]{1,0:T(8,128)(2,1)S(1)}, u32[]{:S(2)}, u32[]{:S(2)}) %collective-permute-start.8) | collective-permute-done | bytes 860192 | tf_op jit(solution)/shard_map/ppermute | solution.py:28
  48.1 1.9 %collective-permute-start.9 = (bf16[112,3840]{1,0:T(8,128)(2,1)S(1)}, bf16[112,3840]{1,0:T(8,128)(2,1)S(1)}, u32[]{:S(2)}, u32[]{:S(2)}) collective-permute-start(bf16[112,3840]{1,0:T(8,128)(2,1)S(1)} %collective-permute-done.8.refs_8_), channel_id=1, source_target_pairs={{0,16},{8,120},{16,32},{24,8},{32,48},{40,24},{48,64},{56,40},{64,... | collective-permute-start | bytes 2580488 | tf_op jit(solution)/shard_map/ppermute | solution.py:28
  50.0 4.3 %collective-permute-done.14 = bf16[112,3840]{1,0:T(8,128)(2,1)S(1)} collective-permute-done((bf16[112,3840]{1,0:T(8,128)(2,1)S(1)}, bf16[112,3840]{1,0:T(8,128)(2,1)S(1)}, u32[]{:S(2)}, u32[]{:S(2)}) %collective-permute-start.14) | collective-permute-done | bytes 860192 | tf_op jit(solution)/shard_map/ppermute | solution.py:28
  54.3 5.9 %collective-permute-start.16 = (bf16[112,3840]{1,0:T(8,128)(2,1)S(1)}, bf16[112,3840]{1,0:T(8,128)(2,1)S(1)}, u32[]{:S(2)}, u32[]{:S(2)}) collective-permute-start(bf16[112,3840]{1,0:T(8,128)(2,1)S(1)} %collective-permute-done.14), channel_id=1, source_target_pairs={{0,8},{8,0},{16,24},{24,16},{32,40},{40,32},{48,56},{56,48},{64,72... | collective-permute-start | bytes 2580488 | tf_op jit(solution)/shard_map/ppermute | solution.py:28
  60.2 1.9 %collective-permute-start.15 = (bf16[112,3840]{1,0:T(8,128)(2,1)S(1)}, bf16[112,3840]{1,0:T(8,128)(2,1)S(1)}, u32[]{:S(2)}, u32[]{:S(2)}) collective-permute-start(bf16[112,3840]{1,0:T(8,128)(2,1)S(1)} %collective-permute-done.7.refs_6_), channel_id=1, source_target_pairs={{0,16},{8,120},{16,32},{24,8},{32,48},{40,24},{48,64},{56,40},{64,... | collective-permute-start | bytes 2580488 | tf_op jit(solution)/shard_map/ppermute | solution.py:28
  63.5 1.7 %collective-permute-done.9.refs_9_ = bf16[112,3840]{1,0:T(8,128)(2,1)S(1)} collective-permute-done((bf16[112,3840]{1,0:T(8,128)(2,1)S(1)}, bf16[112,3840]{1,0:T(8,128)(2,1)S(1)}, u32[]{:S(2)}, u32[]{:S(2)}) %collective-permute-start.9) | collective-permute-done | bytes 860192 | tf_op jit(solution)/shard_map/ppermute | solution.py:28
  66.5 2.9 %collective-permute-done.13.refs_15_ = bf16[112,3840]{1,0:T(8,128)(2,1)S(1)} collective-permute-done((bf16[112,3840]{1,0:T(8,128)(2,1)S(1)}, bf16[112,3840]{1,0:T(8,128)(2,1)S(1)}, u32[]{:S(2)}, u32[]{:S(2)}) %collective-permute-start.13) | collective-permute-done | bytes 860192 | tf_op jit(solution)/shard_map/ppermute | solution.py:28
  69.5 5.5 %shard_map.28.refs_17_ = s16[8,112,128]{2,1,0:T(8,128)(2,1)S(1)} custom-call(s32[2]{0:T(128)S(1)} %pad_add_fusion.refs_0_, s32[2,3840]{1,0:T(2,128)S(1)} %fusion.refs_1_, bf16[112,3840]{1,0:T(8,128)(2,1)S(1)} %bitcast.17, bf16[112,3840]{1,0:T(8,128)(2,1)S(1)} %collective-permute-done.refs_3_, bf16[112,3840]{1,0:T(8,128)(2,1)S(1)} %collective-permute-done.1.refs_4_, ...), custom_call_target="tpu_custom_call" | custom-call | flops 1761607680 | bytes 8601600 | tf_op jit(solution)/shard_map/pallas_call | solution.py:153
  76.1 4.9 %shard_map.29 = s16[8,176,128]{2,1,0:T(8,128)(2,1)S(1)} custom-call(s32[2]{0:T(128)S(1)} %pad_add_fusion.refs_0_, s32[1,3840]{1,0:T(1,128)S(1)} %get-tuple-element.16.refs_1_, bf16[112,3840]{1,0:T(8,128)(2,1)S(1)} %bitcast.18, bf16[112,3840]{1,0:T(8,128)(2,1)S(1)} %collective-permute-done.refs_3_, bf16[112,3840]{1,0:T(8,128)(2,1)S(1)} %collective-permute-done.1.refs_4_, ...), custom_call_target="tpu_custom_call" | custom-call | flops 880803840 | bytes 7741440 | tf_op jit(solution)/shard_map/pallas_call | solution.py:153
  81.0 26.0 %all_to_all.5 = s16[8,176,128]{2,1,0:T(8,128)(2,1)S(1)} all-to-all(s16[8,176,128]{2,1,0:T(8,128)(2,1)S(1)} %shard_map.29), channel_id=1, replica_groups=mesh['ka'=64,'ga'=8] {'ga'}, dimensions={0} | all-to-all | bytes 720896 | tf_op jit(solution)/shard_map/all_to_all | solution.py:206
  (28 shorter events, 8.8 us)
Async XLA Ops:
  0.0 10.4 %copy-start = (s32[8,3,3840]{2,0,1:T(8,128)S(1)}, s32[8,3,3840]{2,0,1:T(8,128)}, u32[]{:S(2)}) copy-start(s32[8,3,3840]{2,0,1:T(8,128)} %param.3) | copy-start | bytes 1105924
  1.3 4.5 %collective-permute-start = (bf16[112,3840]{1,0:T(8,128)(2,1)S(1)}, bf16[112,3840]{1,0:T(8,128)(2,1)S(1)}, u32[]{:S(2)}, u32[]{:S(2)}) collective-permute-start(bf16[112,3840]{1,0:T(8,128)(2,1)S(1)} %bitcast.14), channel_id=1, source_target_pairs={{0,8},{8,0},{16,24},{24,16},{32,40},{40,32},{48,56},{56,48},{64,72... | collective-permute-start | bytes 2580488 | tf_op jit(solution)/shard_map/ppermute | solution.py:28
  3.2 15.9 %collective-permute-start.1 = (bf16[112,3840]{1,0:T(8,128)(2,1)S(1)}, bf16[112,3840]{1,0:T(8,128)(2,1)S(1)}, u32[]{:S(2)}, u32[]{:S(2)}) collective-permute-start(bf16[112,3840]{1,0:T(8,128)(2,1)S(1)} %bitcast.15), channel_id=1, source_target_pairs={{0,16},{8,120},{16,32},{24,8},{32,48},{40,24},{48,64},{56,40},{64,... | collective-permute-start | bytes 2580488 | tf_op jit(solution)/shard_map/ppermute | solution.py:28
  5.8 22.6 %collective-permute-start.5 = (bf16[112,3840]{1,0:T(8,128)(2,1)S(1)}, bf16[112,3840]{1,0:T(8,128)(2,1)}, u32[]{:S(2)}, u32[]{:S(2)}) collective-permute-start(bf16[112,3840]{1,0:T(8,128)(2,1)S(1)} %collective-permute-done.refs_3_), channel_id=1, source_target_pairs={{0,16},{8,120},{16,32},{24,8},{32,48},{40,24},{48,64},{56,40},{64,... | collective-permute-start | bytes 2580488 | tf_op jit(solution)/shard_map/ppermute | solution.py:28
  8.4 23.7 %collective-permute-start.3 = (bf16[112,3840]{1,0:T(8,128)(2,1)S(1)}, bf16[112,3840]{1,0:T(8,128)(2,1)}, u32[]{:S(2)}, u32[]{:S(2)}) collective-permute-start(bf16[112,3840]{1,0:T(8,128)(2,1)S(1)} %bitcast.16), channel_id=1, source_target_pairs={{0,128},{8,264},{16,144},{24,280},{32,160},{40,296},{48,176},{56,3... | collective-permute-start | bytes 2580488 | tf_op jit(solution)/shard_map/ppermute | solution.py:28
  19.1 18.4 %collective-permute-start.2 = (bf16[112,3840]{1,0:T(8,128)(2,1)S(1)}, bf16[112,3840]{1,0:T(8,128)(2,1)S(1)}, u32[]{:S(2)}, u32[]{:S(2)}) collective-permute-start(bf16[112,3840]{1,0:T(8,128)(2,1)S(1)} %collective-permute-done.1.refs_4_), channel_id=1, source_target_pairs={{0,16},{8,120},{16,32},{24,8},{32,48},{40,24},{48,64},{56,40},{64,... | collective-permute-start | bytes 2580488 | tf_op jit(solution)/shard_map/ppermute | solution.py:28
  21.0 17.8 %collective-permute-start.4 = (bf16[112,3840]{1,0:T(8,128)(2,1)S(1)}, bf16[112,3840]{1,0:T(8,128)(2,1)S(1)}, u32[]{:S(2)}, u32[]{:S(2)}) collective-permute-start(bf16[112,3840]{1,0:T(8,128)(2,1)S(1)} %collective-permute-done.1.refs_4_), channel_id=1, source_target_pairs={{8,0},{16,24},{24,16},{32,40},{40,32},{48,56},{72,64},{80,88},{88,... | collective-permute-start | bytes 2580488 | tf_op jit(solution)/shard_map/ppermute | solution.py:28
  28.4 18.3 %collective-permute-start.8 = (bf16[112,3840]{1,0:T(8,128)(2,1)}, bf16[112,3840]{1,0:T(8,128)(2,1)S(1)}, u32[]{:S(2)}, u32[]{:S(2)}) collective-permute-start(bf16[112,3840]{1,0:T(8,128)(2,1)} %collective-permute-done.5.refs_7_), channel_id=1, source_target_pairs={{0,16},{8,120},{16,32},{24,8},{32,48},{40,24},{48,64},{56,40},{64,... | collective-permute-start | bytes 2580488 | tf_op jit(solution)/shard_map/ppermute | solution.py:28
  30.4 8.5 %collective-permute-start.6 = (bf16[112,3840]{1,0:T(8,128)(2,1)}, bf16[112,3840]{1,0:T(8,128)(2,1)S(1)}, u32[]{:S(2)}, u32[]{:S(2)}) collective-permute-start(bf16[112,3840]{1,0:T(8,128)(2,1)} %collective-permute-done.5.refs_7_), channel_id=1, source_target_pairs={{8,0},{16,24},{24,16},{32,40},{40,32},{48,56},{72,64},{80,88},{88,... | collective-permute-start | bytes 2580488 | tf_op jit(solution)/shard_map/ppermute | solution.py:28
  32.1 22.2 %collective-permute-start.14 = (bf16[112,3840]{1,0:T(8,128)(2,1)S(1)}, bf16[112,3840]{1,0:T(8,128)(2,1)S(1)}, u32[]{:S(2)}, u32[]{:S(2)}) collective-permute-start(bf16[112,3840]{1,0:T(8,128)(2,1)S(1)} %collective-permute-done.refs_3_), channel_id=1, source_target_pairs={{0,128},{8,264},{16,144},{24,280},{32,160},{40,296},{48,176},{56,3... | collective-permute-start | bytes 2580488 | tf_op jit(solution)/shard_map/ppermute | solution.py:28
  37.5 22.6 %collective-permute-start.10 = (bf16[112,3840]{1,0:T(8,128)(2,1)S(1)}, bf16[112,3840]{1,0:T(8,128)(2,1)S(1)}, u32[]{:S(2)}, u32[]{:S(2)}) collective-permute-start(bf16[112,3840]{1,0:T(8,128)(2,1)S(1)} %collective-permute-done.2.refs_5_), channel_id=1, source_target_pairs={{8,0},{24,16},{32,40},{48,56},{72,64},{88,80},{96,104},{112,120},{... | collective-permute-start | bytes 2580488 | tf_op jit(solution)/shard_map/ppermute | solution.py:28
  38.9 21.4 %collective-permute-start.7 = (bf16[112,3840]{1,0:T(8,128)(2,1)S(1)}, bf16[112,3840]{1,0:T(8,128)(2,1)S(1)}, u32[]{:S(2)}, u32[]{:S(2)}) collective-permute-start(bf16[112,3840]{1,0:T(8,128)(2,1)S(1)} %collective-permute-done.2.refs_5_), channel_id=1, source_target_pairs={{0,16},{8,120},{16,32},{24,8},{32,48},{40,24},{48,64},{56,40},{64,... | collective-permute-start | bytes 2580488 | tf_op jit(solution)/shard_map/ppermute | solution.py:28
  46.8 13.4 %collective-permute-start.12 = (bf16[112,3840]{1,0:T(8,128)(2,1)S(1)}, bf16[112,3840]{1,0:T(8,128)(2,1)S(1)}, u32[]{:S(2)}, u32[]{:S(2)}) collective-permute-start(bf16[112,3840]{1,0:T(8,128)(2,1)S(1)} %collective-permute-done.8.refs_8_), channel_id=1, source_target_pairs={{8,0},{24,16},{32,40},{48,56},{72,64},{88,80},{96,104},{112,120},{... | collective-permute-start | bytes 2580488 | tf_op jit(solution)/shard_map/ppermute | solution.py:28
  48.1 17.1 %collective-permute-start.9 = (bf16[112,3840]{1,0:T(8,128)(2,1)S(1)}, bf16[112,3840]{1,0:T(8,128)(2,1)S(1)}, u32[]{:S(2)}, u32[]{:S(2)}) collective-permute-start(bf16[112,3840]{1,0:T(8,128)(2,1)S(1)} %collective-permute-done.8.refs_8_), channel_id=1, source_target_pairs={{0,16},{8,120},{16,32},{24,8},{32,48},{40,24},{48,64},{56,40},{64,... | collective-permute-start | bytes 2580488 | tf_op jit(solution)/shard_map/ppermute | solution.py:28
  54.3 12.2 %collective-permute-start.16 = (bf16[112,3840]{1,0:T(8,128)(2,1)S(1)}, bf16[112,3840]{1,0:T(8,128)(2,1)S(1)}, u32[]{:S(2)}, u32[]{:S(2)}) collective-permute-start(bf16[112,3840]{1,0:T(8,128)(2,1)S(1)} %collective-permute-done.14), channel_id=1, source_target_pairs={{0,8},{8,0},{16,24},{24,16},{32,40},{40,32},{48,56},{56,48},{64,72... | collective-permute-start | bytes 2580488 | tf_op jit(solution)/shard_map/ppermute | solution.py:28
  60.2 15.9 %collective-permute-start.15 = (bf16[112,3840]{1,0:T(8,128)(2,1)S(1)}, bf16[112,3840]{1,0:T(8,128)(2,1)S(1)}, u32[]{:S(2)}, u32[]{:S(2)}) collective-permute-start(bf16[112,3840]{1,0:T(8,128)(2,1)S(1)} %collective-permute-done.7.refs_6_), channel_id=1, source_target_pairs={{0,16},{8,120},{16,32},{24,8},{32,48},{40,24},{48,64},{56,40},{64,... | collective-permute-start | bytes 2580488 | tf_op jit(solution)/shard_map/ppermute | solution.py:28
  62.2 7.3 %collective-permute-start.11 = (bf16[112,3840]{1,0:T(8,128)(2,1)S(1)}, bf16[112,3840]{1,0:T(8,128)(2,1)S(1)}, u32[]{:S(2)}, u32[]{:S(2)}) collective-permute-start(bf16[112,3840]{1,0:T(8,128)(2,1)S(1)} %collective-permute-done.7.refs_6_), channel_id=1, source_target_pairs={{8,0},{48,56},{72,64},{112,120},{136,128},{176,184},{200,192},{240... | collective-permute-start | bytes 2580488 | tf_op jit(solution)/shard_map/ppermute | solution.py:28
  65.2 4.3 %collective-permute-start.13 = (bf16[112,3840]{1,0:T(8,128)(2,1)S(1)}, bf16[112,3840]{1,0:T(8,128)(2,1)S(1)}, u32[]{:S(2)}, u32[]{:S(2)}) collective-permute-start(bf16[112,3840]{1,0:T(8,128)(2,1)S(1)} %collective-permute-done.9.refs_9_), channel_id=1, source_target_pairs={{8,0},{48,56},{72,64},{112,120},{136,128},{176,184},{200,192},{240... | collective-permute-start | bytes 2580488 | tf_op jit(solution)/shard_map/ppermute | solution.py:28

commit v4 on v3

--- a/solution.py
+++ b/solution.py
@@ -61,46 +61,48 @@
     return jnp.dot(raw, chosen, preferred_element_type=jnp.float32).astype(jnp.bfloat16)
 
 
-CHUNKS = 1
-
-
-def products_kernel(nb, has_rest, *refs):
+def signed(sums, half):
+    rows = 2 * half
+    low = sums[half:]
+    spare = jnp.zeros((half, LANES - rows), jnp.float32)
+    return sums[:half] + jnp.concatenate([low[:, half:rows], -low[:, :half], spare], axis=1)
+
+
+def products_kernel(nb, *refs):
     refs = list(refs)
-    where, maps, own, sibling = refs[:4]
-    del refs[:4]
-    ga, gb, sa, sb = (refs[3 * i : 3 * i + 3] for i in range(4))
-    del refs[:12]
-    rights = refs[:nb]
-    del refs[:nb]
-    rest = refs.pop(0) if has_rest else None
-    out, left, raw, right, total, left_sems, raw_sems = refs
-    rows, width = own.shape
-    half = rows // 2
-    chunk = width // CHUNKS
+    where, maps = refs[:2]
+    del refs[:2]
     yy, core = where[0], where[1]
     reach = jnp.where(core == 0, yy, HALF - 1 - yy)
-
-    def copy(source, s, j):
-        at = pl.ds(j * chunk, chunk)
-        return pltpu.make_async_copy(
-            source.at[:, at], left.at[pl.ds(s * rows, rows), at], left_sems.at[s, j]
-        )
+    if nb == 2:
+        own, sibling = refs[:2]
+        ga, gb, sa, sb = (refs[2 + 3 * i : 5 + 3 * i] for i in range(4))
+        rights = refs[14:16]
+        out, left, raw, right, total, raw_sems, left_sems = refs[16:]
+    else:
+        left, done, *rights = refs[:3]
+        out, raw, right, total, raw_sems = refs[3:]
+    rows, width = raw.shape[1:]
+    half = rows // 2
+
+    def copy(source, s):
+        return pltpu.make_async_copy(source, left.at[pl.ds(s * rows, rows)], left_sems.at[s])
 
     for b in range(nb):
         pltpu.make_async_copy(rights[b], raw.at[b], raw_sems.at[b]).start()
-    for j in range(CHUNKS):
-        copy(own, 0, j).start()
-        copy(sibling, 1, j).start()
+    if nb == 2:
+        copy(own, 0).start()
+        copy(sibling, 1).start()
         for d in range(1, HALF):
             for part, (near, far) in enumerate(((ga, sb), (gb, sa))):
 
                 @pl.when(d <= reach)
                 def _():
-                    copy(near[d - 1], 2 * d + part, j).start()
+                    copy(near[d - 1], 2 * d + part).start()
 
                 @pl.when(d > reach)
                 def _():
-                    copy(far[HALF - d - 1], 2 * d + part, j).start()
+                    copy(far[HALF - d - 1], 2 * d + part).start()
 
     spare = jnp.zeros((LANES - rows, width), jnp.bfloat16)
     for b in range(nb):
@@ -111,31 +113,20 @@
         at = pl.ds(i * LANES, LANES)
         for b in range(nb):
             right[pl.ds(b * LANES, rows), at] = chosen_rows(maps[b : b + 1, at], raw[b, :, at])
-    for j in range(CHUNKS):
-        at = pl.ds(j * chunk, chunk)
+    if nb == 2:
         for s in range(8):
-            copy(own, s, j).wait()
-        part = lax.dot_general(
-            left[:, at], right[:, at], (((1,), (1,)), ((), ())), preferred_element_type=jnp.float32
-        )
-        total[...] = part if j == 0 else total[...] + part
-
-    if has_rest:
-        out[:, pl.ds(0, rows)] = rest[...]
+            copy(own, s).wait()
+    total[...] = lax.dot_general(
+        left[...], right[...], (((1,), (1,)), ((), ())), preferred_element_type=jnp.float32
+    )
+    if nb == 1:
+        out[:, pl.ds(0, rows)] = done[...]
     for s in range(8):
         d, other = s // 2, s % 2
         chip = jnp.where(core == 0, yy + HALF - d, yy + d) % HALF
         block = chip * CORES + jnp.where(other == 0, core, 1 - core)
-        sums = []
-        for b in range(nb):
-            lanes = pl.ds(b * LANES, LANES)
-            top = total[pl.ds(s * rows, half), lanes]
-            low = total[pl.ds(s * rows + half, half), lanes]
-            turned = jnp.concatenate(
-                [low[:, half:rows], -low[:, :half], jnp.zeros((half, LANES - rows), jnp.float32)], axis=1
-            )
-            sums.append(top + turned)
-        if has_rest:
+        sums = [signed(total[pl.ds(s * rows, rows), pl.ds(b * LANES, LANES)], half) for b in range(nb)]
+        if nb == 1:
             spare_rows = jnp.zeros((64 - half, LANES), jnp.float32)
             out[block, pl.ds(rows, 64)] = scaled(jnp.concatenate([sums[0], spare_rows], axis=0), rows)
         else:
@@ -144,34 +135,40 @@
             out[block] = scaled(jnp.concatenate([first, second], axis=0), rows)
 
 
-def products(where, maps, lefts, rights, rest=None):
+def products(where, maps, bands, rights):
     nb = len(rights)
-    rows, width = lefts[0].shape
+    rows, width = rights[0].shape
     anywhere = pl.BlockSpec(memory_space=pl.ANY)
     vmem = pl.BlockSpec(memory_space=pltpu.VMEM)
-    extra = [] if rest is None else [rest]
+    scratch = [
+        pltpu.VMEM((nb, rows, width), jnp.bfloat16),
+        pltpu.VMEM((nb * LANES, width), jnp.bfloat16),
+        pltpu.VMEM((8 * rows, nb * LANES), jnp.float32),
+        pltpu.SemaphoreType.DMA((nb,)),
+    ]
+    if nb == 2:
+        outs = (
+            jax.ShapeDtypeStruct((8, rows, LANES), jnp.int16),
+            pltpu.VMEM((8 * rows, width), jnp.bfloat16),
+        )
+        scratch.append(pltpu.SemaphoreType.DMA((8,)))
+    else:
+        outs = jax.ShapeDtypeStruct((8, rows + 64, LANES), jnp.int16)
     return pl.pallas_call(
-        functools.partial(products_kernel, nb, rest is not None),
-        out_shape=jax.ShapeDtypeStruct((8, rows + 64 if extra else rows, LANES), jnp.int16),
+        functools.partial(products_kernel, nb),
+        out_shape=outs,
         in_specs=[pl.BlockSpec(memory_space=pltpu.SMEM), vmem]
-        + [anywhere] * (len(lefts) + nb)
-        + [vmem] * len(extra),
-        out_specs=vmem,
-        scratch_shapes=[
-            pltpu.VMEM((8 * rows, width), jnp.bfloat16),
-            pltpu.VMEM((nb, rows, width), jnp.bfloat16),
-            pltpu.VMEM((nb * LANES, width), jnp.bfloat16),
-            pltpu.VMEM((8 * rows, nb * LANES), jnp.float32),
-            pltpu.SemaphoreType.DMA((8, CHUNKS)),
-            pltpu.SemaphoreType.DMA((nb,)),
-        ],
-        compiler_params=pltpu.CompilerParams(vmem_limit_bytes=40 * 2**20),
+        + [anywhere if nb == 2 else vmem] * len(bands)
+        + [anywhere] * nb,
+        out_specs=(vmem, vmem) if nb == 2 else vmem,
+        scratch_shapes=scratch,
+        compiler_params=pltpu.CompilerParams(vmem_limit_bytes=24 * 2**20),
         cost_estimate=pl.CostEstimate(
             flops=2 * 8 * rows * nb * LANES * width,
             bytes_accessed=(8 + nb) * rows * width * 2,
             transcendentals=0,
         ),
-    )(where, maps, *lefts, *rights, *extra)
+    )(where, maps, *bands, *rights)
 
 
 def along_z(z, y, c):
@@ -201,8 +198,8 @@
     opposite = moved(after(ga[-1], zb, sa[2], sb[2]), along_y)
     zs = moved(zb, to_sibling)
     lefts = [mine, sibling, *ga[1:], *gb[1:], *sa[1:], *sb[1:]]
-    later = products(where, later_maps, lefts, [za, zs])
-    every = products(where, maps[:1], lefts, [opposite], later)
+    later, packed = products(where, later_maps, lefts, [za, zs])
+    every = products(where, maps[:1], [packed, later], [opposite])
     shares = lax.all_to_all(every, "ga", 0, 0, tiled=True)
     rows = 2 * bands
     units = jnp.exp2(shares[:, : 3 * bands, rows : rows + 1].astype(jnp.float32))

time: 109 us -> 108 us (level)
  Pallas kernels: 10.4 us -> 8.97 us
    pallas_call x2, Pallas kernels: 10.4 us -> 8.97 us  [products(): pl.pallas_call(functools.partial(products_kernel, nb), out_shape=outs, in...]
where the time goes in v4:
time: 108 us
  starting transfers between devices  34.4 us (32%)
  waiting for transfers between devices  34.4 us (32%)
  blocking collectives  26.1 us (24%)
  Pallas kernels  8.97 us (8%)
  other arithmetic  1.73 us (2%)
  local copies, waits for them, and re-layouts  1.65 us (2%)
    ppermute x17, waiting for transfers between devices, moved(): return lax.ppermute(shard, 'ka', pairs)  34.4 us
    ppermute x17, starting transfers between devices, moved(): return lax.ppermute(shard, 'ka', pairs)  34.4 us
    all_to_all x1, blocking collectives, per_device(): shares = lax.all_to_all(every, 'ga', 0, 0, tiled=True)  26.1 us
    pallas_call x2, Pallas kernels, products(): pl.pallas_call(functools.partial(products_kernel, nb), out_shape=outs, in...  8.97 us
  transfers between devices with their start and end apart: 17, of which 9 were waited for; matrix products, arithmetic and copies ran while one was open for 0% of the time, Pallas kernels for 5%

profile of v4, /device:TPU:96, one launch (start us, length us, event | category | flops | bytes accessed | tf_op | source)
XLA Modules:
  0.0 107.6 jit_solution(10909008435868391896)
XLA Ops:
  0.0 1.3 %copy.6 = bf16[2,56,3840]{2,1,0:T(8,128)(2,1)S(1)} copy(bf16[2,56,3840]{2,0,1:T(2,128)(2,1)} %bitcast.18) | data formatting | bytes 1720320 | tf_op jit(solution)/shard_map/transpose | solution.py:186
  1.3 1.9 %collective-permute-start = (bf16[112,3840]{1,0:T(8,128)(2,1)S(1)}, bf16[112,3840]{1,0:T(8,128)(2,1)S(1)}, u32[]{:S(2)}, u32[]{:S(2)}) collective-permute-start(bf16[112,3840]{1,0:T(8,128)(2,1)S(1)} %bitcast.14), channel_id=1, source_target_pairs={{0,8},{8,0},{16,24},{24,16},{32,40},{40,32},{48,56},{56,48},{64,72... | collective-permute-start | bytes 2580488 | tf_op jit(solution)/shard_map/ppermute | solution.py:28
  3.2 2.6 %collective-permute-start.1 = (bf16[112,3840]{1,0:T(8,128)(2,1)S(1)}, bf16[112,3840]{1,0:T(8,128)(2,1)S(1)}, u32[]{:S(2)}, u32[]{:S(2)}) collective-permute-start(bf16[112,3840]{1,0:T(8,128)(2,1)S(1)} %bitcast.15), channel_id=1, source_target_pairs={{0,16},{8,120},{16,32},{24,8},{32,48},{40,24},{48,64},{56,40},{64,... | collective-permute-start | bytes 2580488 | tf_op jit(solution)/shard_map/ppermute | solution.py:28
  5.8 2.6 %collective-permute-start.5 = (bf16[112,3840]{1,0:T(8,128)(2,1)S(1)}, bf16[112,3840]{1,0:T(8,128)(2,1)}, u32[]{:S(2)}, u32[]{:S(2)}) collective-permute-start(bf16[112,3840]{1,0:T(8,128)(2,1)S(1)} %collective-permute-done.refs_3_), channel_id=1, source_target_pairs={{0,16},{8,120},{16,32},{24,8},{32,48},{40,24},{48,64},{56,40},{64,... | collective-permute-start | bytes 2580488 | tf_op jit(solution)/shard_map/ppermute | solution.py:28
  8.4 1.9 %collective-permute-start.3 = (bf16[112,3840]{1,0:T(8,128)(2,1)S(1)}, bf16[112,3840]{1,0:T(8,128)(2,1)}, u32[]{:S(2)}, u32[]{:S(2)}) collective-permute-start(bf16[112,3840]{1,0:T(8,128)(2,1)S(1)} %bitcast.16), channel_id=1, source_target_pairs={{0,128},{8,264},{16,144},{24,280},{32,160},{40,296},{48,176},{56,3... | collective-permute-start | bytes 2580488 | tf_op jit(solution)/shard_map/ppermute | solution.py:28
  10.5 8.6 %collective-permute-done.1.refs_4_ = bf16[112,3840]{1,0:T(8,128)(2,1)S(1)} collective-permute-done((bf16[112,3840]{1,0:T(8,128)(2,1)S(1)}, bf16[112,3840]{1,0:T(8,128)(2,1)S(1)}, u32[]{:S(2)}, u32[]{:S(2)}) %collective-permute-start.1) | collective-permute-done | bytes 860192 | tf_op jit(solution)/shard_map/ppermute | solution.py:28
  19.1 1.9 %collective-permute-start.2 = (bf16[112,3840]{1,0:T(8,128)(2,1)S(1)}, bf16[112,3840]{1,0:T(8,128)(2,1)S(1)}, u32[]{:S(2)}, u32[]{:S(2)}) collective-permute-start(bf16[112,3840]{1,0:T(8,128)(2,1)S(1)} %collective-permute-done.1.refs_4_), channel_id=1, source_target_pairs={{0,16},{8,120},{16,32},{24,8},{32,48},{40,24},{48,64},{56,40},{64,... | collective-permute-start | bytes 2580488 | tf_op jit(solution)/shard_map/ppermute | solution.py:28
  21.0 1.3 %collective-permute-start.4 = (bf16[112,3840]{1,0:T(8,128)(2,1)S(1)}, bf16[112,3840]{1,0:T(8,128)(2,1)S(1)}, u32[]{:S(2)}, u32[]{:S(2)}) collective-permute-start(bf16[112,3840]{1,0:T(8,128)(2,1)S(1)} %collective-permute-done.1.refs_4_), channel_id=1, source_target_pairs={{8,0},{16,24},{24,16},{32,40},{40,32},{48,56},{72,64},{80,88},{88,... | collective-permute-start | bytes 2580488 | tf_op jit(solution)/shard_map/ppermute | solution.py:28
  22.3 6.1 %collective-permute-done.5.refs_7_ = bf16[112,3840]{1,0:T(8,128)(2,1)} collective-permute-done((bf16[112,3840]{1,0:T(8,128)(2,1)S(1)}, bf16[112,3840]{1,0:T(8,128)(2,1)}, u32[]{:S(2)}, u32[]{:S(2)}) %collective-permute-start.5) | collective-permute-done | bytes 860192 | tf_op jit(solution)/shard_map/ppermute | solution.py:28
  28.4 1.9 %collective-permute-start.8 = (bf16[112,3840]{1,0:T(8,128)(2,1)}, bf16[112,3840]{1,0:T(8,128)(2,1)S(1)}, u32[]{:S(2)}, u32[]{:S(2)}) collective-permute-start(bf16[112,3840]{1,0:T(8,128)(2,1)} %collective-permute-done.5.refs_7_), channel_id=1, source_target_pairs={{0,16},{8,120},{16,32},{24,8},{32,48},{40,24},{48,64},{56,40},{64,... | collective-permute-start | bytes 2580488 | tf_op jit(solution)/shard_map/ppermute | solution.py:28
  30.4 1.3 %collective-permute-start.6 = (bf16[112,3840]{1,0:T(8,128)(2,1)}, bf16[112,3840]{1,0:T(8,128)(2,1)S(1)}, u32[]{:S(2)}, u32[]{:S(2)}) collective-permute-start(bf16[112,3840]{1,0:T(8,128)(2,1)} %collective-permute-done.5.refs_7_), channel_id=1, source_target_pairs={{8,0},{16,24},{24,16},{32,40},{40,32},{48,56},{72,64},{80,88},{88,... | collective-permute-start | bytes 2580488 | tf_op jit(solution)/shard_map/ppermute | solution.py:28
  32.1 2.2 %collective-permute-start.14 = (bf16[112,3840]{1,0:T(8,128)(2,1)S(1)}, bf16[112,3840]{1,0:T(8,128)(2,1)S(1)}, u32[]{:S(2)}, u32[]{:S(2)}) collective-permute-start(bf16[112,3840]{1,0:T(8,128)(2,1)S(1)} %collective-permute-done.refs_3_), channel_id=1, source_target_pairs={{0,128},{8,264},{16,144},{24,280},{32,160},{40,296},{48,176},{56,3... | collective-permute-start | bytes 2580488 | tf_op jit(solution)/shard_map/ppermute | solution.py:28
  34.3 3.2 %collective-permute-done.2.refs_5_ = bf16[112,3840]{1,0:T(8,128)(2,1)S(1)} collective-permute-done((bf16[112,3840]{1,0:T(8,128)(2,1)S(1)}, bf16[112,3840]{1,0:T(8,128)(2,1)S(1)}, u32[]{:S(2)}, u32[]{:S(2)}) %collective-permute-start.2) | collective-permute-done | bytes 860192 | tf_op jit(solution)/shard_map/ppermute | solution.py:28
  38.9 1.9 %collective-permute-start.7 = (bf16[112,3840]{1,0:T(8,128)(2,1)S(1)}, bf16[112,3840]{1,0:T(8,128)(2,1)S(1)}, u32[]{:S(2)}, u32[]{:S(2)}) collective-permute-start(bf16[112,3840]{1,0:T(8,128)(2,1)S(1)} %collective-permute-done.2.refs_5_), channel_id=1, source_target_pairs={{0,16},{8,120},{16,32},{24,8},{32,48},{40,24},{48,64},{56,40},{64,... | collective-permute-start | bytes 2580488 | tf_op jit(solution)/shard_map/ppermute | solution.py:28
  40.8 6.0 %collective-permute-done.8.refs_8_ = bf16[112,3840]{1,0:T(8,128)(2,1)S(1)} collective-permute-done((bf16[112,3840]{1,0:T(8,128)(2,1)}, bf16[112,3840]{1,0:T(8,128)(2,1)S(1)}, u32[]{:S(2)}, u32[]{:S(2)}) %collective-permute-start.8) | collective-permute-done | bytes 860192 | tf_op jit(solution)/shard_map/ppermute | solution.py:28
  48.1 1.9 %collective-permute-start.9 = (bf16[112,3840]{1,0:T(8,128)(2,1)S(1)}, bf16[112,3840]{1,0:T(8,128)(2,1)S(1)}, u32[]{:S(2)}, u32[]{:S(2)}) collective-permute-start(bf16[112,3840]{1,0:T(8,128)(2,1)S(1)} %collective-permute-done.8.refs_8_), channel_id=1, source_target_pairs={{0,16},{8,120},{16,32},{24,8},{32,48},{40,24},{48,64},{56,40},{64,... | collective-permute-start | bytes 2580488 | tf_op jit(solution)/shard_map/ppermute | solution.py:28
  50.0 4.3 %collective-permute-done.14 = bf16[112,3840]{1,0:T(8,128)(2,1)S(1)} collective-permute-done((bf16[112,3840]{1,0:T(8,128)(2,1)S(1)}, bf16[112,3840]{1,0:T(8,128)(2,1)S(1)}, u32[]{:S(2)}, u32[]{:S(2)}) %collective-permute-start.14) | collective-permute-done | bytes 860192 | tf_op jit(solution)/shard_map/ppermute | solution.py:28
  54.3 5.9 %collective-permute-start.15 = (bf16[112,3840]{1,0:T(8,128)(2,1)S(1)}, bf16[112,3840]{1,0:T(8,128)(2,1)S(1)}, u32[]{:S(2)}, u32[]{:S(2)}) collective-permute-start(bf16[112,3840]{1,0:T(8,128)(2,1)S(1)} %collective-permute-done.14), channel_id=1, source_target_pairs={{0,8},{8,0},{16,24},{24,16},{32,40},{40,32},{48,56},{56,48},{64,72... | collective-permute-start | bytes 2580488 | tf_op jit(solution)/shard_map/ppermute | solution.py:28
  60.2 1.9 %collective-permute-start.16 = (bf16[112,3840]{1,0:T(8,128)(2,1)S(1)}, bf16[112,3840]{1,0:T(8,128)(2,1)S(1)}, u32[]{:S(2)}, u32[]{:S(2)}) collective-permute-start(bf16[112,3840]{1,0:T(8,128)(2,1)S(1)} %collective-permute-done.7.refs_6_), channel_id=1, source_target_pairs={{0,16},{8,120},{16,32},{24,8},{32,48},{40,24},{48,64},{56,40},{64,... | collective-permute-start | bytes 2580488 | tf_op jit(solution)/shard_map/ppermute | solution.py:28
  63.5 1.7 %collective-permute-done.9.refs_9_ = bf16[112,3840]{1,0:T(8,128)(2,1)S(1)} collective-permute-done((bf16[112,3840]{1,0:T(8,128)(2,1)S(1)}, bf16[112,3840]{1,0:T(8,128)(2,1)S(1)}, u32[]{:S(2)}, u32[]{:S(2)}) %collective-permute-start.9) | collective-permute-done | bytes 860192 | tf_op jit(solution)/shard_map/ppermute | solution.py:28
  66.5 2.9 %collective-permute-done.13.refs_15_ = bf16[112,3840]{1,0:T(8,128)(2,1)S(1)} collective-permute-done((bf16[112,3840]{1,0:T(8,128)(2,1)S(1)}, bf16[112,3840]{1,0:T(8,128)(2,1)S(1)}, u32[]{:S(2)}, u32[]{:S(2)}) %collective-permute-start.13) | collective-permute-done | bytes 860192 | tf_op jit(solution)/shard_map/ppermute | solution.py:28
  69.5 5.5 %shard_map.28 = (s16[8,112,128]{2,1,0:T(8,128)(2,1)S(1)}, bf16[896,3840]{1,0:T(8,128)(2,1)S(1)}) custom-call(s32[2]{0:T(128)S(1)} %pad_add_fusion.refs_0_, s32[2,3840]{1,0:T(2,128)S(1)} %fusion.refs_1_, bf16[112,3840]{1,0:T(8,128)(2,1)S(1)} %bitcast.17, bf16[112,3840]{1,0:T(8,128)(2,1)S(1)} %collective-permute-done.refs_3_, ...), custom_call_target="tpu_custom_call" | custom-call | flops 1761607680 | bytes 8601600 | tf_op jit(solution)/shard_map/pallas_call | solution.py:157
  76.1 3.5 %shard_map.29 = s16[8,176,128]{2,1,0:T(8,128)(2,1)S(1)} custom-call(s32[2]{0:T(128)S(1)} %pad_add_fusion.refs_0_, s32[1,3840]{1,0:T(1,128)S(1)} %get-tuple-element.20.refs_1_, bf16[896,3840]{1,0:T(8,128)(2,1)S(1)} %get-tuple-element.12.refs_2_, s16[8,112,128]{2,1,0:T(8,128)(2,1)S(1)} %get-tuple-element.13.refs_3_, ...), custom_call_target="tpu_custom_call" | custom-call | flops 880803840 | bytes 7741440 | tf_op jit(solution)/shard_map/pallas_call | solution.py:157
  79.6 26.1 %all_to_all.5 = s16[8,176,128]{2,1,0:T(8,128)(2,1)S(1)} all-to-all(s16[8,176,128]{2,1,0:T(8,128)(2,1)S(1)} %shard_map.29), channel_id=1, replica_groups=mesh['ka'=64,'ga'=8] {'ga'}, dimensions={0} | all-to-all | bytes 720896 | tf_op jit(solution)/shard_map/all_to_all | solution.py:203
  (28 shorter events, 8.8 us)
Async XLA Ops:
  0.0 10.4 %copy-start = (s32[8,3,3840]{2,0,1:T(8,128)S(1)}, s32[8,3,3840]{2,0,1:T(8,128)}, u32[]{:S(2)}) copy-start(s32[8,3,3840]{2,0,1:T(8,128)} %param.3) | copy-start | bytes 1105924
  1.3 4.5 %collective-permute-start = (bf16[112,3840]{1,0:T(8,128)(2,1)S(1)}, bf16[112,3840]{1,0:T(8,128)(2,1)S(1)}, u32[]{:S(2)}, u32[]{:S(2)}) collective-permute-start(bf16[112,3840]{1,0:T(8,128)(2,1)S(1)} %bitcast.14), channel_id=1, source_target_pairs={{0,8},{8,0},{16,24},{24,16},{32,40},{40,32},{48,56},{56,48},{64,72... | collective-permute-start | bytes 2580488 | tf_op jit(solution)/shard_map/ppermute | solution.py:28
  3.2 15.9 %collective-permute-start.1 = (bf16[112,3840]{1,0:T(8,128)(2,1)S(1)}, bf16[112,3840]{1,0:T(8,128)(2,1)S(1)}, u32[]{:S(2)}, u32[]{:S(2)}) collective-permute-start(bf16[112,3840]{1,0:T(8,128)(2,1)S(1)} %bitcast.15), channel_id=1, source_target_pairs={{0,16},{8,120},{16,32},{24,8},{32,48},{40,24},{48,64},{56,40},{64,... | collective-permute-start | bytes 2580488 | tf_op jit(solution)/shard_map/ppermute | solution.py:28
  5.8 22.6 %collective-permute-start.5 = (bf16[112,3840]{1,0:T(8,128)(2,1)S(1)}, bf16[112,3840]{1,0:T(8,128)(2,1)}, u32[]{:S(2)}, u32[]{:S(2)}) collective-permute-start(bf16[112,3840]{1,0:T(8,128)(2,1)S(1)} %collective-permute-done.refs_3_), channel_id=1, source_target_pairs={{0,16},{8,120},{16,32},{24,8},{32,48},{40,24},{48,64},{56,40},{64,... | collective-permute-start | bytes 2580488 | tf_op jit(solution)/shard_map/ppermute | solution.py:28
  8.4 23.7 %collective-permute-start.3 = (bf16[112,3840]{1,0:T(8,128)(2,1)S(1)}, bf16[112,3840]{1,0:T(8,128)(2,1)}, u32[]{:S(2)}, u32[]{:S(2)}) collective-permute-start(bf16[112,3840]{1,0:T(8,128)(2,1)S(1)} %bitcast.16), channel_id=1, source_target_pairs={{0,128},{8,264},{16,144},{24,280},{32,160},{40,296},{48,176},{56,3... | collective-permute-start | bytes 2580488 | tf_op jit(solution)/shard_map/ppermute | solution.py:28
  19.1 18.4 %collective-permute-start.2 = (bf16[112,3840]{1,0:T(8,128)(2,1)S(1)}, bf16[112,3840]{1,0:T(8,128)(2,1)S(1)}, u32[]{:S(2)}, u32[]{:S(2)}) collective-permute-start(bf16[112,3840]{1,0:T(8,128)(2,1)S(1)} %collective-permute-done.1.refs_4_), channel_id=1, source_target_pairs={{0,16},{8,120},{16,32},{24,8},{32,48},{40,24},{48,64},{56,40},{64,... | collective-permute-start | bytes 2580488 | tf_op jit(solution)/shard_map/ppermute | solution.py:28
  21.0 17.8 %collective-permute-start.4 = (bf16[112,3840]{1,0:T(8,128)(2,1)S(1)}, bf16[112,3840]{1,0:T(8,128)(2,1)S(1)}, u32[]{:S(2)}, u32[]{:S(2)}) collective-permute-start(bf16[112,3840]{1,0:T(8,128)(2,1)S(1)} %collective-permute-done.1.refs_4_), channel_id=1, source_target_pairs={{8,0},{16,24},{24,16},{32,40},{40,32},{48,56},{72,64},{80,88},{88,... | collective-permute-start | bytes 2580488 | tf_op jit(solution)/shard_map/ppermute | solution.py:28
  28.4 18.3 %collective-permute-start.8 = (bf16[112,3840]{1,0:T(8,128)(2,1)}, bf16[112,3840]{1,0:T(8,128)(2,1)S(1)}, u32[]{:S(2)}, u32[]{:S(2)}) collective-permute-start(bf16[112,3840]{1,0:T(8,128)(2,1)} %collective-permute-done.5.refs_7_), channel_id=1, source_target_pairs={{0,16},{8,120},{16,32},{24,8},{32,48},{40,24},{48,64},{56,40},{64,... | collective-permute-start | bytes 2580488 | tf_op jit(solution)/shard_map/ppermute | solution.py:28
  30.4 8.5 %collective-permute-start.6 = (bf16[112,3840]{1,0:T(8,128)(2,1)}, bf16[112,3840]{1,0:T(8,128)(2,1)S(1)}, u32[]{:S(2)}, u32[]{:S(2)}) collective-permute-start(bf16[112,3840]{1,0:T(8,128)(2,1)} %collective-permute-done.5.refs_7_), channel_id=1, source_target_pairs={{8,0},{16,24},{24,16},{32,40},{40,32},{48,56},{72,64},{80,88},{88,... | collective-permute-start | bytes 2580488 | tf_op jit(solution)/shard_map/ppermute | solution.py:28
  32.1 22.2 %collective-permute-start.14 = (bf16[112,3840]{1,0:T(8,128)(2,1)S(1)}, bf16[112,3840]{1,0:T(8,128)(2,1)S(1)}, u32[]{:S(2)}, u32[]{:S(2)}) collective-permute-start(bf16[112,3840]{1,0:T(8,128)(2,1)S(1)} %collective-permute-done.refs_3_), channel_id=1, source_target_pairs={{0,128},{8,264},{16,144},{24,280},{32,160},{40,296},{48,176},{56,3... | collective-permute-start | bytes 2580488 | tf_op jit(solution)/shard_map/ppermute | solution.py:28
  37.5 22.6 %collective-permute-start.10 = (bf16[112,3840]{1,0:T(8,128)(2,1)S(1)}, bf16[112,3840]{1,0:T(8,128)(2,1)S(1)}, u32[]{:S(2)}, u32[]{:S(2)}) collective-permute-start(bf16[112,3840]{1,0:T(8,128)(2,1)S(1)} %collective-permute-done.2.refs_5_), channel_id=1, source_target_pairs={{8,0},{24,16},{32,40},{48,56},{72,64},{88,80},{96,104},{112,120},{... | collective-permute-start | bytes 2580488 | tf_op jit(solution)/shard_map/ppermute | solution.py:28
  38.9 21.4 %collective-permute-start.7 = (bf16[112,3840]{1,0:T(8,128)(2,1)S(1)}, bf16[112,3840]{1,0:T(8,128)(2,1)S(1)}, u32[]{:S(2)}, u32[]{:S(2)}) collective-permute-start(bf16[112,3840]{1,0:T(8,128)(2,1)S(1)} %collective-permute-done.2.refs_5_), channel_id=1, source_target_pairs={{0,16},{8,120},{16,32},{24,8},{32,48},{40,24},{48,64},{56,40},{64,... | collective-permute-start | bytes 2580488 | tf_op jit(solution)/shard_map/ppermute | solution.py:28
  46.8 13.4 %collective-permute-start.12 = (bf16[112,3840]{1,0:T(8,128)(2,1)S(1)}, bf16[112,3840]{1,0:T(8,128)(2,1)S(1)}, u32[]{:S(2)}, u32[]{:S(2)}) collective-permute-start(bf16[112,3840]{1,0:T(8,128)(2,1)S(1)} %collective-permute-done.8.refs_8_), channel_id=1, source_target_pairs={{8,0},{24,16},{32,40},{48,56},{72,64},{88,80},{96,104},{112,120},{... | collective-permute-start | bytes 2580488 | tf_op jit(solution)/shard_map/ppermute | solution.py:28
  48.1 17.1 %collective-permute-start.9 = (bf16[112,3840]{1,0:T(8,128)(2,1)S(1)}, bf16[112,3840]{1,0:T(8,128)(2,1)S(1)}, u32[]{:S(2)}, u32[]{:S(2)}) collective-permute-start(bf16[112,3840]{1,0:T(8,128)(2,1)S(1)} %collective-permute-done.8.refs_8_), channel_id=1, source_target_pairs={{0,16},{8,120},{16,32},{24,8},{32,48},{40,24},{48,64},{56,40},{64,... | collective-permute-start | bytes 2580488 | tf_op jit(solution)/shard_map/ppermute | solution.py:28
  54.3 12.2 %collective-permute-start.15 = (bf16[112,3840]{1,0:T(8,128)(2,1)S(1)}, bf16[112,3840]{1,0:T(8,128)(2,1)S(1)}, u32[]{:S(2)}, u32[]{:S(2)}) collective-permute-start(bf16[112,3840]{1,0:T(8,128)(2,1)S(1)} %collective-permute-done.14), channel_id=1, source_target_pairs={{0,8},{8,0},{16,24},{24,16},{32,40},{40,32},{48,56},{56,48},{64,72... | collective-permute-start | bytes 2580488 | tf_op jit(solution)/shard_map/ppermute | solution.py:28
  60.2 15.9 %collective-permute-start.16 = (bf16[112,3840]{1,0:T(8,128)(2,1)S(1)}, bf16[112,3840]{1,0:T(8,128)(2,1)S(1)}, u32[]{:S(2)}, u32[]{:S(2)}) collective-permute-start(bf16[112,3840]{1,0:T(8,128)(2,1)S(1)} %collective-permute-done.7.refs_6_), channel_id=1, source_target_pairs={{0,16},{8,120},{16,32},{24,8},{32,48},{40,24},{48,64},{56,40},{64,... | collective-permute-start | bytes 2580488 | tf_op jit(solution)/shard_map/ppermute | solution.py:28
  62.2 7.3 %collective-permute-start.11 = (bf16[112,3840]{1,0:T(8,128)(2,1)S(1)}, bf16[112,3840]{1,0:T(8,128)(2,1)S(1)}, u32[]{:S(2)}, u32[]{:S(2)}) collective-permute-start(bf16[112,3840]{1,0:T(8,128)(2,1)S(1)} %collective-permute-done.7.refs_6_), channel_id=1, source_target_pairs={{8,0},{48,56},{72,64},{112,120},{136,128},{176,184},{200,192},{240... | collective-permute-start | bytes 2580488 | tf_op jit(solution)/shard_map/ppermute | solution.py:28
  65.2 4.3 %collective-permute-start.13 = (bf16[112,3840]{1,0:T(8,128)(2,1)S(1)}, bf16[112,3840]{1,0:T(8,128)(2,1)S(1)}, u32[]{:S(2)}, u32[]{:S(2)}) collective-permute-start(bf16[112,3840]{1,0:T(8,128)(2,1)S(1)} %collective-permute-done.9.refs_9_), channel_id=1, source_target_pairs={{8,0},{48,56},{72,64},{112,120},{136,128},{176,184},{200,192},{240... | collective-permute-start | bytes 2580488 | tf_op jit(solution)/shard_map/ppermute | solution.py:28

commit v5 on v4

--- a/solution.py
+++ b/solution.py
@@ -123,8 +123,8 @@
         out[:, pl.ds(0, rows)] = done[...]
     for s in range(8):
         d, other = s // 2, s % 2
-        chip = jnp.where(core == 0, yy + HALF - d, yy + d) % HALF
-        block = chip * CORES + jnp.where(other == 0, core, 1 - core)
+        chip = jnp.where(core == 0, yy + HALF - d, yy + d) & (HALF - 1)
+        block = (((chip & 1) << 1) | (core ^ other)) << 1 | (chip >> 1)
         sums = [signed(total[pl.ds(s * rows, rows), pl.ds(b * LANES, LANES)], half) for b in range(nb)]
         if nb == 1:
             spare_rows = jnp.zeros((64 - half, LANES), jnp.float32)
@@ -190,8 +190,7 @@
     zb = moved(after(sibling, za), along_z)
     ga, gb, sa, sb = [mine], [sibling], [None], [None]
     for hops in range(1, HALF):
-        deps = {1: [], 2: [], 3: [za, sa[1], sb[1]] if hops == 3 else []}[hops]
-        ga.append(moved(after(ga[-1], *deps), along_y))
+        ga.append(moved(after(ga[-1], za, sa[1], sb[1]) if hops == 3 else ga[-1], along_y))
         gb.append(moved(gb[-1], along_y))
         sa.append(moved(ga[-1], to_sibling, wanted_from_sibling(hops)))
         sb.append(moved(gb[-1], to_sibling, wanted_from_sibling(hops)))
@@ -200,10 +199,16 @@
     lefts = [mine, sibling, *ga[1:], *gb[1:], *sa[1:], *sb[1:]]
     later, packed = products(where, later_maps, lefts, [za, zs])
     every = products(where, maps[:1], [packed, later], [opposite])
-    shares = lax.all_to_all(every, "ga", 0, 0, tiled=True)
+    shares = lax.all_to_all(
+        every, "ga", 0, 0, axis_index_groups=[[0, 1, 2, 3], [4, 5, 6, 7]], tiled=True
+    )
     rows = 2 * bands
     units = jnp.exp2(shares[:, : 3 * bands, rows : rows + 1].astype(jnp.float32))
-    total = (shares[:, : 3 * bands, :rows].astype(jnp.float32) * units).sum(axis=0)
+    sums = shares[:, : 3 * bands, :rows].astype(jnp.float32) * units
+    lower, upper = sums[0::2].sum(axis=0), sums[1::2].sum(axis=0)
+    low = lax.axis_index("ga") < 4
+    theirs = lax.ppermute(jnp.where(low, upper, lower), "ga", [(g, g ^ 4) for g in range(8)])
+    total = jnp.where(low, lower, upper) + theirs
     second, third, first = total[:bands], total[bands:rows], total[rows:]
     return jnp.stack([first, second, third], axis=1).reshape(bands, 3, 2, bands)
 

time: 108 us -> 108 us (level)
  the two profiles are of different devices: /device:TPU:96 before, /device:TPU:2 now
where the time goes in v5:
time: 108 us
  starting transfers between devices  54.8 us (51%)
  waiting for transfers between devices  39.3 us (36%)
  Pallas kernels  9.69 us (9%)
  other arithmetic  1.8 us (2%)
  local copies, waits for them, and re-layouts  1.65 us (2%)
    ppermute x17, starting transfers between devices, moved(): return lax.ppermute(shard, 'ka', pairs)  39.3 us
    ppermute x17, waiting for transfers between devices, moved(): return lax.ppermute(shard, 'ka', pairs)  28.7 us
    pallas_call x2, Pallas kernels, products(): pl.pallas_call(functools.partial(products_kernel, nb), out_shape=outs, in...  9.69 us
    all_to_all x1, starting transfers between devices, per_device(): lax.all_to_all(every, 'ga', 0, 0, axis_index_groups=[[0, 1, 2, 3], [4, 5,...  9.07 us
    all_to_all x1, waiting for transfers between devices, per_device(): lax.all_to_all(every, 'ga', 0, 0, axis_index_groups=[[0, 1, 2, 3], [4, 5,...  6.68 us
    ppermute x1, starting transfers between devices, per_device(): lax.ppermute(jnp.where(low, upper, lower), 'ga', [(g, g ^ 4) for g in ran...  6.37 us
    ppermute x1, waiting for transfers between devices, per_device(): lax.ppermute(jnp.where(low, upper, lower), 'ga', [(g, g ^ 4) for g in ran...  3.91 us
  transfers between devices with their start and end apart: 19, of which 10 were waited for; matrix products, arithmetic and copies ran while one was open for 0% of the time, Pallas kernels for 5%

profile of v5, /device:TPU:2, one launch (start us, length us, event | category | flops | bytes accessed | tf_op | source)
XLA Modules:
  0.0 107.5 jit_solution(3749895226399405523)
XLA Ops:
  1.3 1.9 %collective-permute-start = (bf16[112,3840]{1,0:T(8,128)(2,1)S(1)}, bf16[112,3840]{1,0:T(8,128)(2,1)S(1)}, u32[]{:S(2)}, u32[]{:S(2)}) collective-permute-start(bf16[112,3840]{1,0:T(8,128)(2,1)S(1)} %bitcast.14), channel_id=1, source_target_pairs={{0,8},{8,0},{16,24},{24,16},{32,40},{40,32},{48,56},{56,48},{64,72... | collective-permute-start | bytes 2580488 | tf_op jit(solution)/shard_map/ppermute | solution.py:28
  3.2 3.5 %collective-permute-start.1 = (bf16[112,3840]{1,0:T(8,128)(2,1)S(1)}, bf16[112,3840]{1,0:T(8,128)(2,1)S(1)}, u32[]{:S(2)}, u32[]{:S(2)}) collective-permute-start(bf16[112,3840]{1,0:T(8,128)(2,1)S(1)} %bitcast.15), channel_id=1, source_target_pairs={{0,16},{8,120},{16,32},{24,8},{32,48},{40,24},{48,64},{56,40},{64,... | collective-permute-start | bytes 2580488 | tf_op jit(solution)/shard_map/ppermute | solution.py:28
  6.7 3.5 %collective-permute-start.5 = (bf16[112,3840]{1,0:T(8,128)(2,1)S(1)}, bf16[112,3840]{1,0:T(8,128)(2,1)}, u32[]{:S(2)}, u32[]{:S(2)}) collective-permute-start(bf16[112,3840]{1,0:T(8,128)(2,1)S(1)} %collective-permute-done.refs_3_), channel_id=1, source_target_pairs={{0,16},{8,120},{16,32},{24,8},{32,48},{40,24},{48,64},{56,40},{64,... | collective-permute-start | bytes 2580488 | tf_op jit(solution)/shard_map/ppermute | solution.py:28
  10.2 4.3 %collective-permute-start.3 = (bf16[112,3840]{1,0:T(8,128)(2,1)S(1)}, bf16[112,3840]{1,0:T(8,128)(2,1)}, u32[]{:S(2)}, u32[]{:S(2)}) collective-permute-start(bf16[112,3840]{1,0:T(8,128)(2,1)S(1)} %bitcast.16), channel_id=1, source_target_pairs={{0,128},{8,264},{16,144},{24,280},{32,160},{40,296},{48,176},{56,3... | collective-permute-start | bytes 2580488 | tf_op jit(solution)/shard_map/ppermute | solution.py:28
  14.6 4.7 %collective-permute-done.1.refs_4_ = bf16[112,3840]{1,0:T(8,128)(2,1)S(1)} collective-permute-done((bf16[112,3840]{1,0:T(8,128)(2,1)S(1)}, bf16[112,3840]{1,0:T(8,128)(2,1)S(1)}, u32[]{:S(2)}, u32[]{:S(2)}) %collective-permute-start.1) | collective-permute-done | bytes 860192 | tf_op jit(solution)/shard_map/ppermute | solution.py:28
  20.6 2.7 %collective-permute-start.2 = (bf16[112,3840]{1,0:T(8,128)(2,1)S(1)}, bf16[112,3840]{1,0:T(8,128)(2,1)S(1)}, u32[]{:S(2)}, u32[]{:S(2)}) collective-permute-start(bf16[112,3840]{1,0:T(8,128)(2,1)S(1)} %collective-permute-done.1.refs_4_), channel_id=1, source_target_pairs={{0,16},{8,120},{16,32},{24,8},{32,48},{40,24},{48,64},{56,40},{64,... | collective-permute-start | bytes 2580488 | tf_op jit(solution)/shard_map/ppermute | solution.py:28
  23.3 5.4 %collective-permute-done.5.refs_7_ = bf16[112,3840]{1,0:T(8,128)(2,1)} collective-permute-done((bf16[112,3840]{1,0:T(8,128)(2,1)S(1)}, bf16[112,3840]{1,0:T(8,128)(2,1)}, u32[]{:S(2)}, u32[]{:S(2)}) %collective-permute-start.5) | collective-permute-done | bytes 860192 | tf_op jit(solution)/shard_map/ppermute | solution.py:28
  28.7 2.0 %collective-permute-start.8 = (bf16[112,3840]{1,0:T(8,128)(2,1)}, bf16[112,3840]{1,0:T(8,128)(2,1)S(1)}, u32[]{:S(2)}, u32[]{:S(2)}) collective-permute-start(bf16[112,3840]{1,0:T(8,128)(2,1)} %collective-permute-done.5.refs_7_), channel_id=1, source_target_pairs={{0,16},{8,120},{16,32},{24,8},{32,48},{40,24},{48,64},{56,40},{64,... | collective-permute-start | bytes 2580488 | tf_op jit(solution)/shard_map/ppermute | solution.py:28
  32.0 1.5 %collective-permute-done.3.refs_16_ = bf16[112,3840]{1,0:T(8,128)(2,1)} collective-permute-done((bf16[112,3840]{1,0:T(8,128)(2,1)S(1)}, bf16[112,3840]{1,0:T(8,128)(2,1)}, u32[]{:S(2)}, u32[]{:S(2)}) %collective-permute-start.3) | collective-permute-done | bytes 860192 | tf_op jit(solution)/shard_map/ppermute | solution.py:28
  33.6 2.8 %collective-permute-start.14 = (bf16[112,3840]{1,0:T(8,128)(2,1)S(1)}, bf16[112,3840]{1,0:T(8,128)(2,1)S(1)}, u32[]{:S(2)}, u32[]{:S(2)}) collective-permute-start(bf16[112,3840]{1,0:T(8,128)(2,1)S(1)} %collective-permute-done.refs_3_), channel_id=1, source_target_pairs={{0,128},{8,264},{16,144},{24,280},{32,160},{40,296},{48,176},{56,3... | collective-permute-start | bytes 2580488 | tf_op jit(solution)/shard_map/ppermute | solution.py:28
  36.3 1.5 %collective-permute-done.2.refs_5_ = bf16[112,3840]{1,0:T(8,128)(2,1)S(1)} collective-permute-done((bf16[112,3840]{1,0:T(8,128)(2,1)S(1)}, bf16[112,3840]{1,0:T(8,128)(2,1)S(1)}, u32[]{:S(2)}, u32[]{:S(2)}) %collective-permute-start.2) | collective-permute-done | bytes 860192 | tf_op jit(solution)/shard_map/ppermute | solution.py:28
  39.1 2.7 %collective-permute-start.7 = (bf16[112,3840]{1,0:T(8,128)(2,1)S(1)}, bf16[112,3840]{1,0:T(8,128)(2,1)S(1)}, u32[]{:S(2)}, u32[]{:S(2)}) collective-permute-start(bf16[112,3840]{1,0:T(8,128)(2,1)S(1)} %collective-permute-done.2.refs_5_), channel_id=1, source_target_pairs={{0,16},{8,120},{16,32},{24,8},{32,48},{40,24},{48,64},{56,40},{64,... | collective-permute-start | bytes 2580488 | tf_op jit(solution)/shard_map/ppermute | solution.py:28
  41.8 5.2 %collective-permute-done.8.refs_8_ = bf16[112,3840]{1,0:T(8,128)(2,1)S(1)} collective-permute-done((bf16[112,3840]{1,0:T(8,128)(2,1)}, bf16[112,3840]{1,0:T(8,128)(2,1)S(1)}, u32[]{:S(2)}, u32[]{:S(2)}) %collective-permute-start.8) | collective-permute-done | bytes 860192 | tf_op jit(solution)/shard_map/ppermute | solution.py:28
  48.3 2.0 %collective-permute-start.9 = (bf16[112,3840]{1,0:T(8,128)(2,1)S(1)}, bf16[112,3840]{1,0:T(8,128)(2,1)S(1)}, u32[]{:S(2)}, u32[]{:S(2)}) collective-permute-start(bf16[112,3840]{1,0:T(8,128)(2,1)S(1)} %collective-permute-done.8.refs_8_), channel_id=1, source_target_pairs={{0,16},{8,120},{16,32},{24,8},{32,48},{40,24},{48,64},{56,40},{64,... | collective-permute-start | bytes 2580488 | tf_op jit(solution)/shard_map/ppermute | solution.py:28
  50.4 7.1 %collective-permute-done.14 = bf16[112,3840]{1,0:T(8,128)(2,1)S(1)} collective-permute-done((bf16[112,3840]{1,0:T(8,128)(2,1)S(1)}, bf16[112,3840]{1,0:T(8,128)(2,1)S(1)}, u32[]{:S(2)}, u32[]{:S(2)}) %collective-permute-start.14) | collective-permute-done | bytes 860192 | tf_op jit(solution)/shard_map/ppermute | solution.py:28
  57.4 1.9 %collective-permute-start.15 = (bf16[112,3840]{1,0:T(8,128)(2,1)S(1)}, bf16[112,3840]{1,0:T(8,128)(2,1)S(1)}, u32[]{:S(2)}, u32[]{:S(2)}) collective-permute-start(bf16[112,3840]{1,0:T(8,128)(2,1)S(1)} %collective-permute-done.14), channel_id=1, source_target_pairs={{0,8},{8,0},{16,24},{24,16},{32,40},{40,32},{48,56},{56,48},{64,72... | collective-permute-start | bytes 2580488 | tf_op jit(solution)/shard_map/ppermute | solution.py:28
  59.4 4.4 %collective-permute-start.16 = (bf16[112,3840]{1,0:T(8,128)(2,1)S(1)}, bf16[112,3840]{1,0:T(8,128)(2,1)S(1)}, u32[]{:S(2)}, u32[]{:S(2)}) collective-permute-start(bf16[112,3840]{1,0:T(8,128)(2,1)S(1)} %collective-permute-done.7.refs_6_), channel_id=1, source_target_pairs={{0,16},{8,120},{16,32},{24,8},{32,48},{40,24},{48,64},{56,40},{64,... | collective-permute-start | bytes 2580488 | tf_op jit(solution)/shard_map/ppermute | solution.py:28
  66.8 2.9 %collective-permute-done.13.refs_15_ = bf16[112,3840]{1,0:T(8,128)(2,1)S(1)} collective-permute-done((bf16[112,3840]{1,0:T(8,128)(2,1)S(1)}, bf16[112,3840]{1,0:T(8,128)(2,1)S(1)}, u32[]{:S(2)}, u32[]{:S(2)}) %collective-permute-start.13) | collective-permute-done | bytes 860192 | tf_op jit(solution)/shard_map/ppermute | solution.py:28
  69.7 5.5 %shard_map.28 = (s16[8,112,128]{2,1,0:T(8,128)(2,1)S(1)}, bf16[896,3840]{1,0:T(8,128)(2,1)S(1)}) custom-call(s32[2]{0:T(128)S(1)} %pad_add_fusion.refs_0_, s32[2,3840]{1,0:T(2,128)S(1)} %fusion.refs_1_, bf16[112,3840]{1,0:T(8,128)(2,1)S(1)} %bitcast.17, bf16[112,3840]{1,0:T(8,128)(2,1)S(1)} %collective-permute-done.refs_3_, ...), custom_call_target="tpu_custom_call" | custom-call | flops 1761607680 | bytes 8601600 | tf_op jit(solution)/shard_map/pallas_call | solution.py:157
  75.3 4.2 %shard_map.29 = s16[8,176,128]{2,1,0:T(8,128)(2,1)} custom-call(s32[2]{0:T(128)S(1)} %pad_add_fusion.refs_0_, s32[1,3840]{1,0:T(1,128)S(1)} %get-tuple-element.22.refs_1_, bf16[896,3840]{1,0:T(8,128)(2,1)S(1)} %get-tuple-element.12.refs_2_, s16[8,112,128]{2,1,0:T(8,128)(2,1)S(1)} %get-tuple-element.13.refs_3_, ...), custom_call_target="tpu_custom_call" | custom-call | flops 880803840 | bytes 7741440 | tf_op jit(solution)/shard_map/pallas_call | solution.py:157
  79.5 9.1 %all-to-all-start = ((s16[8,176,128]{2,1,0:T(8,128)(2,1)}), s16[8,176,128]{2,1,0:T(8,128)(2,1)S(1)}, u32[]{:S(2)}, u32[]{:S(2)}) async-start(s16[8,176,128]{2,1,0:T(8,128)(2,1)} %shard_map.29), calls=%async_computation | async-start | bytes 720896 | tf_op jit(solution)/shard_map/all_to_all | solution.py:202
  88.5 6.7 %all-to-all-done = s16[8,176,128]{2,1,0:T(8,128)(2,1)S(1)} async-done(((s16[8,176,128]{2,1,0:T(8,128)(2,1)}), s16[8,176,128]{2,1,0:T(8,128)(2,1)S(1)}, u32[]{:S(2)}, u32[]{:S(2)}) %all-to-all-start) | async-done | bytes 360480 | tf_op jit(solution)/shard_map/all_to_all | solution.py:202
  96.1 6.4 %collective-permute-start.17 = (f32[168,112]{1,0:T(8,128)S(1)}, f32[168,112]{1,0:T(8,128)S(1)}, u32[]{:S(2)}, u32[]{:S(2)}) collective-permute-start(f32[168,112]{1,0:T(8,128)S(1)} %broadcast_select_fusion), channel_id=1, source_target_pairs={{0,4},{1,5},{2,6},{3,7},{4,0},{5,1},{6,2},{7,3},{8,12},{9,13},{10,... | collective-permute-start | bytes 225800 | tf_op jit(solution)/shard_map/ppermute | solution.py:210
  102.5 3.9 %collective-permute-done.17 = f32[168,112]{1,0:T(8,128)S(1)} collective-permute-done((f32[168,112]{1,0:T(8,128)S(1)}, f32[168,112]{1,0:T(8,128)S(1)}, u32[]{:S(2)}, u32[]{:S(2)}) %collective-permute-start.17) | collective-permute-done | bytes 75296 | tf_op jit(solution)/shard_map/ppermute | solution.py:210
  (34 shorter events, 11.6 us)
Async XLA Ops:
  0.0 14.6 %copy-start = (s32[8,3,3840]{2,0,1:T(8,128)S(1)}, s32[8,3,3840]{2,0,1:T(8,128)}, u32[]{:S(2)}) copy-start(s32[8,3,3840]{2,0,1:T(8,128)} %param.3) | copy-start | bytes 1105924
  1.3 5.4 %collective-permute-start = (bf16[112,3840]{1,0:T(8,128)(2,1)S(1)}, bf16[112,3840]{1,0:T(8,128)(2,1)S(1)}, u32[]{:S(2)}, u32[]{:S(2)}) collective-permute-start(bf16[112,3840]{1,0:T(8,128)(2,1)S(1)} %bitcast.14), channel_id=1, source_target_pairs={{0,8},{8,0},{16,24},{24,16},{32,40},{40,32},{48,56},{56,48},{64,72... | collective-permute-start | bytes 2580488 | tf_op jit(solution)/shard_map/ppermute | solution.py:28
  3.2 16.1 %collective-permute-start.1 = (bf16[112,3840]{1,0:T(8,128)(2,1)S(1)}, bf16[112,3840]{1,0:T(8,128)(2,1)S(1)}, u32[]{:S(2)}, u32[]{:S(2)}) collective-permute-start(bf16[112,3840]{1,0:T(8,128)(2,1)S(1)} %bitcast.15), channel_id=1, source_target_pairs={{0,16},{8,120},{16,32},{24,8},{32,48},{40,24},{48,64},{56,40},{64,... | collective-permute-start | bytes 2580488 | tf_op jit(solution)/shard_map/ppermute | solution.py:28
  6.7 21.9 %collective-permute-start.5 = (bf16[112,3840]{1,0:T(8,128)(2,1)S(1)}, bf16[112,3840]{1,0:T(8,128)(2,1)}, u32[]{:S(2)}, u32[]{:S(2)}) collective-permute-start(bf16[112,3840]{1,0:T(8,128)(2,1)S(1)} %collective-permute-done.refs_3_), channel_id=1, source_target_pairs={{0,16},{8,120},{16,32},{24,8},{32,48},{40,24},{48,64},{56,40},{64,... | collective-permute-start | bytes 2580488 | tf_op jit(solution)/shard_map/ppermute | solution.py:28
  10.2 23.3 %collective-permute-start.3 = (bf16[112,3840]{1,0:T(8,128)(2,1)S(1)}, bf16[112,3840]{1,0:T(8,128)(2,1)}, u32[]{:S(2)}, u32[]{:S(2)}) collective-permute-start(bf16[112,3840]{1,0:T(8,128)(2,1)S(1)} %bitcast.16), channel_id=1, source_target_pairs={{0,128},{8,264},{16,144},{24,280},{32,160},{40,296},{48,176},{56,3... | collective-permute-start | bytes 2580488 | tf_op jit(solution)/shard_map/ppermute | solution.py:28
  19.4 19.7 %collective-permute-start.4 = (bf16[112,3840]{1,0:T(8,128)(2,1)S(1)}, bf16[112,3840]{1,0:T(8,128)(2,1)S(1)}, u32[]{:S(2)}, u32[]{:S(2)}) collective-permute-start(bf16[112,3840]{1,0:T(8,128)(2,1)S(1)} %collective-permute-done.1.refs_4_), channel_id=1, source_target_pairs={{8,0},{16,24},{24,16},{32,40},{40,32},{48,56},{72,64},{80,88},{88,... | collective-permute-start | bytes 2580488 | tf_op jit(solution)/shard_map/ppermute | solution.py:28
  20.6 17.1 %collective-permute-start.2 = (bf16[112,3840]{1,0:T(8,128)(2,1)S(1)}, bf16[112,3840]{1,0:T(8,128)(2,1)S(1)}, u32[]{:S(2)}, u32[]{:S(2)}) collective-permute-start(bf16[112,3840]{1,0:T(8,128)(2,1)S(1)} %collective-permute-done.1.refs_4_), channel_id=1, source_target_pairs={{0,16},{8,120},{16,32},{24,8},{32,48},{40,24},{48,64},{56,40},{64,... | collective-permute-start | bytes 2580488 | tf_op jit(solution)/shard_map/ppermute | solution.py:28
  28.7 18.3 %collective-permute-start.8 = (bf16[112,3840]{1,0:T(8,128)(2,1)}, bf16[112,3840]{1,0:T(8,128)(2,1)S(1)}, u32[]{:S(2)}, u32[]{:S(2)}) collective-permute-start(bf16[112,3840]{1,0:T(8,128)(2,1)} %collective-permute-done.5.refs_7_), channel_id=1, source_target_pairs={{0,16},{8,120},{16,32},{24,8},{32,48},{40,24},{48,64},{56,40},{64,... | collective-permute-start | bytes 2580488 | tf_op jit(solution)/shard_map/ppermute | solution.py:28
  30.7 8.4 %collective-permute-start.6 = (bf16[112,3840]{1,0:T(8,128)(2,1)}, bf16[112,3840]{1,0:T(8,128)(2,1)S(1)}, u32[]{:S(2)}, u32[]{:S(2)}) collective-permute-start(bf16[112,3840]{1,0:T(8,128)(2,1)} %collective-permute-done.5.refs_7_), channel_id=1, source_target_pairs={{8,0},{16,24},{24,16},{32,40},{40,32},{48,56},{72,64},{80,88},{88,... | collective-permute-start | bytes 2580488 | tf_op jit(solution)/shard_map/ppermute | solution.py:28
  33.6 23.9 %collective-permute-start.14 = (bf16[112,3840]{1,0:T(8,128)(2,1)S(1)}, bf16[112,3840]{1,0:T(8,128)(2,1)S(1)}, u32[]{:S(2)}, u32[]{:S(2)}) collective-permute-start(bf16[112,3840]{1,0:T(8,128)(2,1)S(1)} %collective-permute-done.refs_3_), channel_id=1, source_target_pairs={{0,128},{8,264},{16,144},{24,280},{32,160},{40,296},{48,176},{56,3... | collective-permute-start | bytes 2580488 | tf_op jit(solution)/shard_map/ppermute | solution.py:28
  37.8 21.6 %collective-permute-start.10 = (bf16[112,3840]{1,0:T(8,128)(2,1)S(1)}, bf16[112,3840]{1,0:T(8,128)(2,1)S(1)}, u32[]{:S(2)}, u32[]{:S(2)}) collective-permute-start(bf16[112,3840]{1,0:T(8,128)(2,1)S(1)} %collective-permute-done.2.refs_5_), channel_id=1, source_target_pairs={{8,0},{24,16},{32,40},{48,56},{72,64},{88,80},{96,104},{112,120},{... | collective-permute-start | bytes 2580488 | tf_op jit(solution)/shard_map/ppermute | solution.py:28
  39.1 20.3 %collective-permute-start.7 = (bf16[112,3840]{1,0:T(8,128)(2,1)S(1)}, bf16[112,3840]{1,0:T(8,128)(2,1)S(1)}, u32[]{:S(2)}, u32[]{:S(2)}) collective-permute-start(bf16[112,3840]{1,0:T(8,128)(2,1)S(1)} %collective-permute-done.2.refs_5_), channel_id=1, source_target_pairs={{0,16},{8,120},{16,32},{24,8},{32,48},{40,24},{48,64},{56,40},{64,... | collective-permute-start | bytes 2580488 | tf_op jit(solution)/shard_map/ppermute | solution.py:28
  47.0 12.4 %collective-permute-start.12 = (bf16[112,3840]{1,0:T(8,128)(2,1)S(1)}, bf16[112,3840]{1,0:T(8,128)(2,1)S(1)}, u32[]{:S(2)}, u32[]{:S(2)}) collective-permute-start(bf16[112,3840]{1,0:T(8,128)(2,1)S(1)} %collective-permute-done.8.refs_8_), channel_id=1, source_target_pairs={{8,0},{24,16},{32,40},{48,56},{72,64},{88,80},{96,104},{112,120},{... | collective-permute-start | bytes 2580488 | tf_op jit(solution)/shard_map/ppermute | solution.py:28
  48.3 17.1 %collective-permute-start.9 = (bf16[112,3840]{1,0:T(8,128)(2,1)S(1)}, bf16[112,3840]{1,0:T(8,128)(2,1)S(1)}, u32[]{:S(2)}, u32[]{:S(2)}) collective-permute-start(bf16[112,3840]{1,0:T(8,128)(2,1)S(1)} %collective-permute-done.8.refs_8_), channel_id=1, source_target_pairs={{0,16},{8,120},{16,32},{24,8},{32,48},{40,24},{48,64},{56,40},{64,... | collective-permute-start | bytes 2580488 | tf_op jit(solution)/shard_map/ppermute | solution.py:28
  57.4 9.3 %collective-permute-start.15 = (bf16[112,3840]{1,0:T(8,128)(2,1)S(1)}, bf16[112,3840]{1,0:T(8,128)(2,1)S(1)}, u32[]{:S(2)}, u32[]{:S(2)}) collective-permute-start(bf16[112,3840]{1,0:T(8,128)(2,1)S(1)} %collective-permute-done.14), channel_id=1, source_target_pairs={{0,8},{8,0},{16,24},{24,16},{32,40},{40,32},{48,56},{56,48},{64,72... | collective-permute-start | bytes 2580488 | tf_op jit(solution)/shard_map/ppermute | solution.py:28
  59.4 15.9 %collective-permute-start.16 = (bf16[112,3840]{1,0:T(8,128)(2,1)S(1)}, bf16[112,3840]{1,0:T(8,128)(2,1)S(1)}, u32[]{:S(2)}, u32[]{:S(2)}) collective-permute-start(bf16[112,3840]{1,0:T(8,128)(2,1)S(1)} %collective-permute-done.7.refs_6_), channel_id=1, source_target_pairs={{0,16},{8,120},{16,32},{24,8},{32,48},{40,24},{48,64},{56,40},{64,... | collective-permute-start | bytes 2580488 | tf_op jit(solution)/shard_map/ppermute | solution.py:28
  63.8 5.9 %collective-permute-start.11 = (bf16[112,3840]{1,0:T(8,128)(2,1)S(1)}, bf16[112,3840]{1,0:T(8,128)(2,1)S(1)}, u32[]{:S(2)}, u32[]{:S(2)}) collective-permute-start(bf16[112,3840]{1,0:T(8,128)(2,1)S(1)} %collective-permute-done.7.refs_6_), channel_id=1, source_target_pairs={{8,0},{48,56},{72,64},{112,120},{136,128},{176,184},{200,192},{240... | collective-permute-start | bytes 2580488 | tf_op jit(solution)/shard_map/ppermute | solution.py:28
  65.4 4.3 %collective-permute-start.13 = (bf16[112,3840]{1,0:T(8,128)(2,1)S(1)}, bf16[112,3840]{1,0:T(8,128)(2,1)S(1)}, u32[]{:S(2)}, u32[]{:S(2)}) collective-permute-start(bf16[112,3840]{1,0:T(8,128)(2,1)S(1)} %collective-permute-done.9.refs_9_), channel_id=1, source_target_pairs={{8,0},{48,56},{72,64},{112,120},{136,128},{176,184},{200,192},{240... | collective-permute-start | bytes 2580488 | tf_op jit(solution)/shard_map/ppermute | solution.py:28
  79.5 15.8 %all-to-all-start = ((s16[8,176,128]{2,1,0:T(8,128)(2,1)}), s16[8,176,128]{2,1,0:T(8,128)(2,1)S(1)}, u32[]{:S(2)}, u32[]{:S(2)}) async-start(s16[8,176,128]{2,1,0:T(8,128)(2,1)} %shard_map.29), calls=%async_computation | async-start | bytes 720896 | tf_op jit(solution)/shard_map/all_to_all | solution.py:202
  96.1 10.3 %collective-permute-start.17 = (f32[168,112]{1,0:T(8,128)S(1)}, f32[168,112]{1,0:T(8,128)S(1)}, u32[]{:S(2)}, u32[]{:S(2)}) collective-permute-start(f32[168,112]{1,0:T(8,128)S(1)} %broadcast_select_fusion), channel_id=1, source_target_pairs={{0,4},{1,5},{2,6},{3,7},{4,0},{5,1},{6,2},{7,3},{8,12},{9,13},{10,... | collective-permute-start | bytes 225800 | tf_op jit(solution)/shard_map/ppermute | solution.py:210

commit v6 on v5

--- a/solution.py
+++ b/solution.py
@@ -1,4 +1,5 @@
 import functools
+import math
 
 import jax
 import jax.numpy as jnp
@@ -49,7 +50,7 @@
 
 def scaled(values, exponent_lane):
     most = jnp.max(jnp.abs(values), axis=1, keepdims=True)
-    exponent = jnp.maximum(jnp.ceil(jnp.log2(jnp.maximum(most, 1e-30) / 32766.0)), -120.0)
+    exponent = jnp.maximum(jnp.ceil(jnp.log2(jnp.maximum(most, 1e-36)) - math.log2(32700)), -126.0)
     whole = jnp.round(values * jnp.exp2(-exponent))
     lane = lax.broadcasted_iota(jnp.int32, values.shape, 1)
     return jnp.where(lane == exponent_lane, exponent, whole).astype(jnp.int32).astype(jnp.int16)

time: 108 us -> 108 us (level)
  no operation moved by 1% of the time
where the time goes in v6:
time: 108 us
  starting transfers between devices  54.8 us (51%)
  waiting for transfers between devices  39.3 us (36%)
  Pallas kernels  9.7 us (9%)
  other arithmetic  1.8 us (2%)
  local copies, waits for them, and re-layouts  1.65 us (2%)
    ppermute x17, starting transfers between devices, moved(): return lax.ppermute(shard, 'ka', pairs)  39.3 us
    ppermute x17, waiting for transfers between devices, moved(): return lax.ppermute(shard, 'ka', pairs)  28.7 us
    pallas_call x2, Pallas kernels, products(): pl.pallas_call(functools.partial(products_kernel, nb), out_shape=outs, in...  9.7 us
    all_to_all x1, starting transfers between devices, per_device(): lax.all_to_all(every, 'ga', 0, 0, axis_index_groups=[[0, 1, 2, 3], [4, 5,...  9.08 us
    all_to_all x1, waiting for transfers between devices, per_device(): lax.all_to_all(every, 'ga', 0, 0, axis_index_groups=[[0, 1, 2, 3], [4, 5,...  6.68 us
    ppermute x1, starting transfers between devices, per_device(): lax.ppermute(jnp.where(low, upper, lower), 'ga', [(g, g ^ 4) for g in ran...  6.37 us
    ppermute x1, waiting for transfers between devices, per_device(): lax.ppermute(jnp.where(low, upper, lower), 'ga', [(g, g ^ 4) for g in ran...  3.91 us
  transfers between devices with their start and end apart: 19, of which 10 were waited for; matrix products, arithmetic and copies ran while one was open for 0% of the time, Pallas kernels for 5%

profile of v6, /device:TPU:2, one launch (start us, length us, event | category | flops | bytes accessed | tf_op | source)
XLA Modules:
  0.0 107.5 jit_solution(4481180503350419976)
XLA Ops:
  1.3 1.9 %collective-permute-start = (bf16[112,3840]{1,0:T(8,128)(2,1)S(1)}, bf16[112,3840]{1,0:T(8,128)(2,1)S(1)}, u32[]{:S(2)}, u32[]{:S(2)}) collective-permute-start(bf16[112,3840]{1,0:T(8,128)(2,1)S(1)} %bitcast.14), channel_id=1, source_target_pairs={{0,8},{8,0},{16,24},{24,16},{32,40},{40,32},{48,56},{56,48},{64,72... | collective-permute-start | bytes 2580488 | tf_op jit(solution)/shard_map/ppermute | solution.py:29
  3.2 3.5 %collective-permute-start.1 = (bf16[112,3840]{1,0:T(8,128)(2,1)S(1)}, bf16[112,3840]{1,0:T(8,128)(2,1)S(1)}, u32[]{:S(2)}, u32[]{:S(2)}) collective-permute-start(bf16[112,3840]{1,0:T(8,128)(2,1)S(1)} %bitcast.15), channel_id=1, source_target_pairs={{0,16},{8,120},{16,32},{24,8},{32,48},{40,24},{48,64},{56,40},{64,... | collective-permute-start | bytes 2580488 | tf_op jit(solution)/shard_map/ppermute | solution.py:29
  6.7 3.5 %collective-permute-start.5 = (bf16[112,3840]{1,0:T(8,128)(2,1)S(1)}, bf16[112,3840]{1,0:T(8,128)(2,1)}, u32[]{:S(2)}, u32[]{:S(2)}) collective-permute-start(bf16[112,3840]{1,0:T(8,128)(2,1)S(1)} %collective-permute-done.refs_3_), channel_id=1, source_target_pairs={{0,16},{8,120},{16,32},{24,8},{32,48},{40,24},{48,64},{56,40},{64,... | collective-permute-start | bytes 2580488 | tf_op jit(solution)/shard_map/ppermute | solution.py:29
  10.2 4.3 %collective-permute-start.3 = (bf16[112,3840]{1,0:T(8,128)(2,1)S(1)}, bf16[112,3840]{1,0:T(8,128)(2,1)}, u32[]{:S(2)}, u32[]{:S(2)}) collective-permute-start(bf16[112,3840]{1,0:T(8,128)(2,1)S(1)} %bitcast.16), channel_id=1, source_target_pairs={{0,128},{8,264},{16,144},{24,280},{32,160},{40,296},{48,176},{56,3... | collective-permute-start | bytes 2580488 | tf_op jit(solution)/shard_map/ppermute | solution.py:29
  14.6 4.7 %collective-permute-done.1.refs_4_ = bf16[112,3840]{1,0:T(8,128)(2,1)S(1)} collective-permute-done((bf16[112,3840]{1,0:T(8,128)(2,1)S(1)}, bf16[112,3840]{1,0:T(8,128)(2,1)S(1)}, u32[]{:S(2)}, u32[]{:S(2)}) %collective-permute-start.1) | collective-permute-done | bytes 860192 | tf_op jit(solution)/shard_map/ppermute | solution.py:29
  20.6 2.7 %collective-permute-start.2 = (bf16[112,3840]{1,0:T(8,128)(2,1)S(1)}, bf16[112,3840]{1,0:T(8,128)(2,1)S(1)}, u32[]{:S(2)}, u32[]{:S(2)}) collective-permute-start(bf16[112,3840]{1,0:T(8,128)(2,1)S(1)} %collective-permute-done.1.refs_4_), channel_id=1, source_target_pairs={{0,16},{8,120},{16,32},{24,8},{32,48},{40,24},{48,64},{56,40},{64,... | collective-permute-start | bytes 2580488 | tf_op jit(solution)/shard_map/ppermute | solution.py:29
  23.3 5.4 %collective-permute-done.5.refs_7_ = bf16[112,3840]{1,0:T(8,128)(2,1)} collective-permute-done((bf16[112,3840]{1,0:T(8,128)(2,1)S(1)}, bf16[112,3840]{1,0:T(8,128)(2,1)}, u32[]{:S(2)}, u32[]{:S(2)}) %collective-permute-start.5) | collective-permute-done | bytes 860192 | tf_op jit(solution)/shard_map/ppermute | solution.py:29
  28.7 2.0 %collective-permute-start.8 = (bf16[112,3840]{1,0:T(8,128)(2,1)}, bf16[112,3840]{1,0:T(8,128)(2,1)S(1)}, u32[]{:S(2)}, u32[]{:S(2)}) collective-permute-start(bf16[112,3840]{1,0:T(8,128)(2,1)} %collective-permute-done.5.refs_7_), channel_id=1, source_target_pairs={{0,16},{8,120},{16,32},{24,8},{32,48},{40,24},{48,64},{56,40},{64,... | collective-permute-start | bytes 2580488 | tf_op jit(solution)/shard_map/ppermute | solution.py:29
  32.0 1.5 %collective-permute-done.3.refs_16_ = bf16[112,3840]{1,0:T(8,128)(2,1)} collective-permute-done((bf16[112,3840]{1,0:T(8,128)(2,1)S(1)}, bf16[112,3840]{1,0:T(8,128)(2,1)}, u32[]{:S(2)}, u32[]{:S(2)}) %collective-permute-start.3) | collective-permute-done | bytes 860192 | tf_op jit(solution)/shard_map/ppermute | solution.py:29
  33.6 2.8 %collective-permute-start.14 = (bf16[112,3840]{1,0:T(8,128)(2,1)S(1)}, bf16[112,3840]{1,0:T(8,128)(2,1)S(1)}, u32[]{:S(2)}, u32[]{:S(2)}) collective-permute-start(bf16[112,3840]{1,0:T(8,128)(2,1)S(1)} %collective-permute-done.refs_3_), channel_id=1, source_target_pairs={{0,128},{8,264},{16,144},{24,280},{32,160},{40,296},{48,176},{56,3... | collective-permute-start | bytes 2580488 | tf_op jit(solution)/shard_map/ppermute | solution.py:29
  36.3 1.5 %collective-permute-done.2.refs_5_ = bf16[112,3840]{1,0:T(8,128)(2,1)S(1)} collective-permute-done((bf16[112,3840]{1,0:T(8,128)(2,1)S(1)}, bf16[112,3840]{1,0:T(8,128)(2,1)S(1)}, u32[]{:S(2)}, u32[]{:S(2)}) %collective-permute-start.2) | collective-permute-done | bytes 860192 | tf_op jit(solution)/shard_map/ppermute | solution.py:29
  39.1 2.7 %collective-permute-start.7 = (bf16[112,3840]{1,0:T(8,128)(2,1)S(1)}, bf16[112,3840]{1,0:T(8,128)(2,1)S(1)}, u32[]{:S(2)}, u32[]{:S(2)}) collective-permute-start(bf16[112,3840]{1,0:T(8,128)(2,1)S(1)} %collective-permute-done.2.refs_5_), channel_id=1, source_target_pairs={{0,16},{8,120},{16,32},{24,8},{32,48},{40,24},{48,64},{56,40},{64,... | collective-permute-start | bytes 2580488 | tf_op jit(solution)/shard_map/ppermute | solution.py:29
  41.8 5.2 %collective-permute-done.8.refs_8_ = bf16[112,3840]{1,0:T(8,128)(2,1)S(1)} collective-permute-done((bf16[112,3840]{1,0:T(8,128)(2,1)}, bf16[112,3840]{1,0:T(8,128)(2,1)S(1)}, u32[]{:S(2)}, u32[]{:S(2)}) %collective-permute-start.8) | collective-permute-done | bytes 860192 | tf_op jit(solution)/shard_map/ppermute | solution.py:29
  48.3 2.0 %collective-permute-start.9 = (bf16[112,3840]{1,0:T(8,128)(2,1)S(1)}, bf16[112,3840]{1,0:T(8,128)(2,1)S(1)}, u32[]{:S(2)}, u32[]{:S(2)}) collective-permute-start(bf16[112,3840]{1,0:T(8,128)(2,1)S(1)} %collective-permute-done.8.refs_8_), channel_id=1, source_target_pairs={{0,16},{8,120},{16,32},{24,8},{32,48},{40,24},{48,64},{56,40},{64,... | collective-permute-start | bytes 2580488 | tf_op jit(solution)/shard_map/ppermute | solution.py:29
  50.4 7.1 %collective-permute-done.14 = bf16[112,3840]{1,0:T(8,128)(2,1)S(1)} collective-permute-done((bf16[112,3840]{1,0:T(8,128)(2,1)S(1)}, bf16[112,3840]{1,0:T(8,128)(2,1)S(1)}, u32[]{:S(2)}, u32[]{:S(2)}) %collective-permute-start.14) | collective-permute-done | bytes 860192 | tf_op jit(solution)/shard_map/ppermute | solution.py:29
  57.4 1.9 %collective-permute-start.15 = (bf16[112,3840]{1,0:T(8,128)(2,1)S(1)}, bf16[112,3840]{1,0:T(8,128)(2,1)S(1)}, u32[]{:S(2)}, u32[]{:S(2)}) collective-permute-start(bf16[112,3840]{1,0:T(8,128)(2,1)S(1)} %collective-permute-done.14), channel_id=1, source_target_pairs={{0,8},{8,0},{16,24},{24,16},{32,40},{40,32},{48,56},{56,48},{64,72... | collective-permute-start | bytes 2580488 | tf_op jit(solution)/shard_map/ppermute | solution.py:29
  59.4 4.4 %collective-permute-start.16 = (bf16[112,3840]{1,0:T(8,128)(2,1)S(1)}, bf16[112,3840]{1,0:T(8,128)(2,1)S(1)}, u32[]{:S(2)}, u32[]{:S(2)}) collective-permute-start(bf16[112,3840]{1,0:T(8,128)(2,1)S(1)} %collective-permute-done.7.refs_6_), channel_id=1, source_target_pairs={{0,16},{8,120},{16,32},{24,8},{32,48},{40,24},{48,64},{56,40},{64,... | collective-permute-start | bytes 2580488 | tf_op jit(solution)/shard_map/ppermute | solution.py:29
  66.8 2.9 %collective-permute-done.13.refs_15_ = bf16[112,3840]{1,0:T(8,128)(2,1)S(1)} collective-permute-done((bf16[112,3840]{1,0:T(8,128)(2,1)S(1)}, bf16[112,3840]{1,0:T(8,128)(2,1)S(1)}, u32[]{:S(2)}, u32[]{:S(2)}) %collective-permute-start.13) | collective-permute-done | bytes 860192 | tf_op jit(solution)/shard_map/ppermute | solution.py:29
  69.7 5.5 %shard_map.28 = (s16[8,112,128]{2,1,0:T(8,128)(2,1)S(1)}, bf16[896,3840]{1,0:T(8,128)(2,1)S(1)}) custom-call(s32[2]{0:T(128)S(1)} %pad_add_fusion.refs_0_, s32[2,3840]{1,0:T(2,128)S(1)} %fusion.refs_1_, bf16[112,3840]{1,0:T(8,128)(2,1)S(1)} %bitcast.17, bf16[112,3840]{1,0:T(8,128)(2,1)S(1)} %collective-permute-done.refs_3_, ...), custom_call_target="tpu_custom_call" | custom-call | flops 1761607680 | bytes 8601600 | tf_op jit(solution)/shard_map/pallas_call | solution.py:158
  75.3 4.2 %shard_map.29 = s16[8,176,128]{2,1,0:T(8,128)(2,1)} custom-call(s32[2]{0:T(128)S(1)} %pad_add_fusion.refs_0_, s32[1,3840]{1,0:T(1,128)S(1)} %get-tuple-element.22.refs_1_, bf16[896,3840]{1,0:T(8,128)(2,1)S(1)} %get-tuple-element.12.refs_2_, s16[8,112,128]{2,1,0:T(8,128)(2,1)S(1)} %get-tuple-element.13.refs_3_, ...), custom_call_target="tpu_custom_call" | custom-call | flops 880803840 | bytes 7741440 | tf_op jit(solution)/shard_map/pallas_call | solution.py:158
  79.5 9.1 %all-to-all-start = ((s16[8,176,128]{2,1,0:T(8,128)(2,1)}), s16[8,176,128]{2,1,0:T(8,128)(2,1)S(1)}, u32[]{:S(2)}, u32[]{:S(2)}) async-start(s16[8,176,128]{2,1,0:T(8,128)(2,1)} %shard_map.29), calls=%async_computation | async-start | bytes 720896 | tf_op jit(solution)/shard_map/all_to_all | solution.py:203
  88.5 6.7 %all-to-all-done = s16[8,176,128]{2,1,0:T(8,128)(2,1)S(1)} async-done(((s16[8,176,128]{2,1,0:T(8,128)(2,1)}), s16[8,176,128]{2,1,0:T(8,128)(2,1)S(1)}, u32[]{:S(2)}, u32[]{:S(2)}) %all-to-all-start) | async-done | bytes 360480 | tf_op jit(solution)/shard_map/all_to_all | solution.py:203
  96.1 6.4 %collective-permute-start.17 = (f32[168,112]{1,0:T(8,128)S(1)}, f32[168,112]{1,0:T(8,128)S(1)}, u32[]{:S(2)}, u32[]{:S(2)}) collective-permute-start(f32[168,112]{1,0:T(8,128)S(1)} %broadcast_select_fusion), channel_id=1, source_target_pairs={{0,4},{1,5},{2,6},{3,7},{4,0},{5,1},{6,2},{7,3},{8,12},{9,13},{10,... | collective-permute-start | bytes 225800 | tf_op jit(solution)/shard_map/ppermute | solution.py:211
  102.5 3.9 %collective-permute-done.17 = f32[168,112]{1,0:T(8,128)S(1)} collective-permute-done((f32[168,112]{1,0:T(8,128)S(1)}, f32[168,112]{1,0:T(8,128)S(1)}, u32[]{:S(2)}, u32[]{:S(2)}) %collective-permute-start.17) | collective-permute-done | bytes 75296 | tf_op jit(solution)/shard_map/ppermute | solution.py:211
  (34 shorter events, 11.6 us)
Async XLA Ops:
  0.0 14.6 %copy-start = (s32[8,3,3840]{2,0,1:T(8,128)S(1)}, s32[8,3,3840]{2,0,1:T(8,128)}, u32[]{:S(2)}) copy-start(s32[8,3,3840]{2,0,1:T(8,128)} %param.3) | copy-start | bytes 1105924
  1.3 5.4 %collective-permute-start = (bf16[112,3840]{1,0:T(8,128)(2,1)S(1)}, bf16[112,3840]{1,0:T(8,128)(2,1)S(1)}, u32[]{:S(2)}, u32[]{:S(2)}) collective-permute-start(bf16[112,3840]{1,0:T(8,128)(2,1)S(1)} %bitcast.14), channel_id=1, source_target_pairs={{0,8},{8,0},{16,24},{24,16},{32,40},{40,32},{48,56},{56,48},{64,72... | collective-permute-start | bytes 2580488 | tf_op jit(solution)/shard_map/ppermute | solution.py:29
  3.2 16.1 %collective-permute-start.1 = (bf16[112,3840]{1,0:T(8,128)(2,1)S(1)}, bf16[112,3840]{1,0:T(8,128)(2,1)S(1)}, u32[]{:S(2)}, u32[]{:S(2)}) collective-permute-start(bf16[112,3840]{1,0:T(8,128)(2,1)S(1)} %bitcast.15), channel_id=1, source_target_pairs={{0,16},{8,120},{16,32},{24,8},{32,48},{40,24},{48,64},{56,40},{64,... | collective-permute-start | bytes 2580488 | tf_op jit(solution)/shard_map/ppermute | solution.py:29
  6.7 21.9 %collective-permute-start.5 = (bf16[112,3840]{1,0:T(8,128)(2,1)S(1)}, bf16[112,3840]{1,0:T(8,128)(2,1)}, u32[]{:S(2)}, u32[]{:S(2)}) collective-permute-start(bf16[112,3840]{1,0:T(8,128)(2,1)S(1)} %collective-permute-done.refs_3_), channel_id=1, source_target_pairs={{0,16},{8,120},{16,32},{24,8},{32,48},{40,24},{48,64},{56,40},{64,... | collective-permute-start | bytes 2580488 | tf_op jit(solution)/shard_map/ppermute | solution.py:29
  10.2 23.3 %collective-permute-start.3 = (bf16[112,3840]{1,0:T(8,128)(2,1)S(1)}, bf16[112,3840]{1,0:T(8,128)(2,1)}, u32[]{:S(2)}, u32[]{:S(2)}) collective-permute-start(bf16[112,3840]{1,0:T(8,128)(2,1)S(1)} %bitcast.16), channel_id=1, source_target_pairs={{0,128},{8,264},{16,144},{24,280},{32,160},{40,296},{48,176},{56,3... | collective-permute-start | bytes 2580488 | tf_op jit(solution)/shard_map/ppermute | solution.py:29
  19.4 19.7 %collective-permute-start.4 = (bf16[112,3840]{1,0:T(8,128)(2,1)S(1)}, bf16[112,3840]{1,0:T(8,128)(2,1)S(1)}, u32[]{:S(2)}, u32[]{:S(2)}) collective-permute-start(bf16[112,3840]{1,0:T(8,128)(2,1)S(1)} %collective-permute-done.1.refs_4_), channel_id=1, source_target_pairs={{8,0},{16,24},{24,16},{32,40},{40,32},{48,56},{72,64},{80,88},{88,... | collective-permute-start | bytes 2580488 | tf_op jit(solution)/shard_map/ppermute | solution.py:29
  20.6 17.1 %collective-permute-start.2 = (bf16[112,3840]{1,0:T(8,128)(2,1)S(1)}, bf16[112,3840]{1,0:T(8,128)(2,1)S(1)}, u32[]{:S(2)}, u32[]{:S(2)}) collective-permute-start(bf16[112,3840]{1,0:T(8,128)(2,1)S(1)} %collective-permute-done.1.refs_4_), channel_id=1, source_target_pairs={{0,16},{8,120},{16,32},{24,8},{32,48},{40,24},{48,64},{56,40},{64,... | collective-permute-start | bytes 2580488 | tf_op jit(solution)/shard_map/ppermute | solution.py:29
  28.7 18.3 %collective-permute-start.8 = (bf16[112,3840]{1,0:T(8,128)(2,1)}, bf16[112,3840]{1,0:T(8,128)(2,1)S(1)}, u32[]{:S(2)}, u32[]{:S(2)}) collective-permute-start(bf16[112,3840]{1,0:T(8,128)(2,1)} %collective-permute-done.5.refs_7_), channel_id=1, source_target_pairs={{0,16},{8,120},{16,32},{24,8},{32,48},{40,24},{48,64},{56,40},{64,... | collective-permute-start | bytes 2580488 | tf_op jit(solution)/shard_map/ppermute | solution.py:29
  30.7 8.4 %collective-permute-start.6 = (bf16[112,3840]{1,0:T(8,128)(2,1)}, bf16[112,3840]{1,0:T(8,128)(2,1)S(1)}, u32[]{:S(2)}, u32[]{:S(2)}) collective-permute-start(bf16[112,3840]{1,0:T(8,128)(2,1)} %collective-permute-done.5.refs_7_), channel_id=1, source_target_pairs={{8,0},{16,24},{24,16},{32,40},{40,32},{48,56},{72,64},{80,88},{88,... | collective-permute-start | bytes 2580488 | tf_op jit(solution)/shard_map/ppermute | solution.py:29
  33.6 23.9 %collective-permute-start.14 = (bf16[112,3840]{1,0:T(8,128)(2,1)S(1)}, bf16[112,3840]{1,0:T(8,128)(2,1)S(1)}, u32[]{:S(2)}, u32[]{:S(2)}) collective-permute-start(bf16[112,3840]{1,0:T(8,128)(2,1)S(1)} %collective-permute-done.refs_3_), channel_id=1, source_target_pairs={{0,128},{8,264},{16,144},{24,280},{32,160},{40,296},{48,176},{56,3... | collective-permute-start | bytes 2580488 | tf_op jit(solution)/shard_map/ppermute | solution.py:29
  37.8 21.6 %collective-permute-start.10 = (bf16[112,3840]{1,0:T(8,128)(2,1)S(1)}, bf16[112,3840]{1,0:T(8,128)(2,1)S(1)}, u32[]{:S(2)}, u32[]{:S(2)}) collective-permute-start(bf16[112,3840]{1,0:T(8,128)(2,1)S(1)} %collective-permute-done.2.refs_5_), channel_id=1, source_target_pairs={{8,0},{24,16},{32,40},{48,56},{72,64},{88,80},{96,104},{112,120},{... | collective-permute-start | bytes 2580488 | tf_op jit(solution)/shard_map/ppermute | solution.py:29
  39.1 20.3 %collective-permute-start.7 = (bf16[112,3840]{1,0:T(8,128)(2,1)S(1)}, bf16[112,3840]{1,0:T(8,128)(2,1)S(1)}, u32[]{:S(2)}, u32[]{:S(2)}) collective-permute-start(bf16[112,3840]{1,0:T(8,128)(2,1)S(1)} %collective-permute-done.2.refs_5_), channel_id=1, source_target_pairs={{0,16},{8,120},{16,32},{24,8},{32,48},{40,24},{48,64},{56,40},{64,... | collective-permute-start | bytes 2580488 | tf_op jit(solution)/shard_map/ppermute | solution.py:29
  47.0 12.4 %collective-permute-start.12 = (bf16[112,3840]{1,0:T(8,128)(2,1)S(1)}, bf16[112,3840]{1,0:T(8,128)(2,1)S(1)}, u32[]{:S(2)}, u32[]{:S(2)}) collective-permute-start(bf16[112,3840]{1,0:T(8,128)(2,1)S(1)} %collective-permute-done.8.refs_8_), channel_id=1, source_target_pairs={{8,0},{24,16},{32,40},{48,56},{72,64},{88,80},{96,104},{112,120},{... | collective-permute-start | bytes 2580488 | tf_op jit(solution)/shard_map/ppermute | solution.py:29
  48.3 17.1 %collective-permute-start.9 = (bf16[112,3840]{1,0:T(8,128)(2,1)S(1)}, bf16[112,3840]{1,0:T(8,128)(2,1)S(1)}, u32[]{:S(2)}, u32[]{:S(2)}) collective-permute-start(bf16[112,3840]{1,0:T(8,128)(2,1)S(1)} %collective-permute-done.8.refs_8_), channel_id=1, source_target_pairs={{0,16},{8,120},{16,32},{24,8},{32,48},{40,24},{48,64},{56,40},{64,... | collective-permute-start | bytes 2580488 | tf_op jit(solution)/shard_map/ppermute | solution.py:29
  57.4 9.3 %collective-permute-start.15 = (bf16[112,3840]{1,0:T(8,128)(2,1)S(1)}, bf16[112,3840]{1,0:T(8,128)(2,1)S(1)}, u32[]{:S(2)}, u32[]{:S(2)}) collective-permute-start(bf16[112,3840]{1,0:T(8,128)(2,1)S(1)} %collective-permute-done.14), channel_id=1, source_target_pairs={{0,8},{8,0},{16,24},{24,16},{32,40},{40,32},{48,56},{56,48},{64,72... | collective-permute-start | bytes 2580488 | tf_op jit(solution)/shard_map/ppermute | solution.py:29
  59.4 15.9 %collective-permute-start.16 = (bf16[112,3840]{1,0:T(8,128)(2,1)S(1)}, bf16[112,3840]{1,0:T(8,128)(2,1)S(1)}, u32[]{:S(2)}, u32[]{:S(2)}) collective-permute-start(bf16[112,3840]{1,0:T(8,128)(2,1)S(1)} %collective-permute-done.7.refs_6_), channel_id=1, source_target_pairs={{0,16},{8,120},{16,32},{24,8},{32,48},{40,24},{48,64},{56,40},{64,... | collective-permute-start | bytes 2580488 | tf_op jit(solution)/shard_map/ppermute | solution.py:29
  63.8 5.9 %collective-permute-start.11 = (bf16[112,3840]{1,0:T(8,128)(2,1)S(1)}, bf16[112,3840]{1,0:T(8,128)(2,1)S(1)}, u32[]{:S(2)}, u32[]{:S(2)}) collective-permute-start(bf16[112,3840]{1,0:T(8,128)(2,1)S(1)} %collective-permute-done.7.refs_6_), channel_id=1, source_target_pairs={{8,0},{48,56},{72,64},{112,120},{136,128},{176,184},{200,192},{240... | collective-permute-start | bytes 2580488 | tf_op jit(solution)/shard_map/ppermute | solution.py:29
  65.4 4.3 %collective-permute-start.13 = (bf16[112,3840]{1,0:T(8,128)(2,1)S(1)}, bf16[112,3840]{1,0:T(8,128)(2,1)S(1)}, u32[]{:S(2)}, u32[]{:S(2)}) collective-permute-start(bf16[112,3840]{1,0:T(8,128)(2,1)S(1)} %collective-permute-done.9.refs_9_), channel_id=1, source_target_pairs={{8,0},{48,56},{72,64},{112,120},{136,128},{176,184},{200,192},{240... | collective-permute-start | bytes 2580488 | tf_op jit(solution)/shard_map/ppermute | solution.py:29
  79.5 15.8 %all-to-all-start = ((s16[8,176,128]{2,1,0:T(8,128)(2,1)}), s16[8,176,128]{2,1,0:T(8,128)(2,1)S(1)}, u32[]{:S(2)}, u32[]{:S(2)}) async-start(s16[8,176,128]{2,1,0:T(8,128)(2,1)} %shard_map.29), calls=%async_computation | async-start | bytes 720896 | tf_op jit(solution)/shard_map/all_to_all | solution.py:203
  96.1 10.3 %collective-permute-start.17 = (f32[168,112]{1,0:T(8,128)S(1)}, f32[168,112]{1,0:T(8,128)S(1)}, u32[]{:S(2)}, u32[]{:S(2)}) collective-permute-start(f32[168,112]{1,0:T(8,128)S(1)} %broadcast_select_fusion), channel_id=1, source_target_pairs={{0,4},{1,5},{2,6},{3,7},{4,0},{5,1},{6,2},{7,3},{8,12},{9,13},{10,... | collective-permute-start | bytes 225800 | tf_op jit(solution)/shard_map/ppermute | solution.py:211

commit v7 on v6

--- a/solution.py
+++ b/solution.py
@@ -184,19 +184,27 @@
     where = jnp.stack([yy, core]).astype(jnp.int32)
     maps = lax.dynamic_index_in_dim(shift_maps, position >> 3, 0, keepdims=False) & (LANES - 1)
     later_maps = jnp.where(core == 0, maps[1:], jnp.stack([maps[2], maps[1]]))
-    mine = coeffs.transpose(1, 0, 2).reshape(2 * bands, width)
-
-    sibling = moved(mine, to_sibling)
+
+    def rows_of(shard):
+        return shard.transpose(1, 0, 2).reshape(2 * bands, width)
+
+    mine = rows_of(coeffs)
+    near = moved(coeffs, to_sibling)
+    sibling = rows_of(near)
     za = moved(mine, along_z)
     zb = moved(after(sibling, za), along_z)
-    ga, gb, sa, sb = [mine], [sibling], [None], [None]
+    ga, gb, sa, sb = [None], [None], [None], [None]
     for hops in range(1, HALF):
-        ga.append(moved(after(ga[-1], za, sa[1], sb[1]) if hops == 3 else ga[-1], along_y))
-        gb.append(moved(gb[-1], along_y))
+        if hops == 1:
+            ga.append(rows_of(moved(coeffs, along_y)))
+            gb.append(rows_of(moved(near, along_y)))
+        else:
+            ga.append(moved(after(ga[-1], za, sa[1], sb[1]) if hops == 3 else ga[-1], along_y))
+            gb.append(moved(gb[-1], along_y))
         sa.append(moved(ga[-1], to_sibling, wanted_from_sibling(hops)))
         sb.append(moved(gb[-1], to_sibling, wanted_from_sibling(hops)))
-    opposite = moved(after(ga[-1], zb, sa[2], sb[2]), along_y)
-    zs = moved(zb, to_sibling)
+    opposite = moved(after(ga[-1], sa[2], sb[2]), along_y)
+    zs = moved(after(zb, ga[-1]), to_sibling)
     lefts = [mine, sibling, *ga[1:], *gb[1:], *sa[1:], *sb[1:]]
     later, packed = products(where, later_maps, lefts, [za, zs])
     every = products(where, maps[:1], [packed, later], [opposite])

time: 108 us -> 108 us (level)
  the two profiles are of different devices: /device:TPU:2 before, /device:TPU:24 now
where the time goes in v7:
time: 108 us
  starting transfers between devices  67.2 us (62%)
  waiting for transfers between devices  24.3 us (22%)
  Pallas kernels  9.83 us (9%)
  local copies, waits for them, and re-layouts  4.18 us (4%)
  other arithmetic  1.8 us (2%)
    ppermute x17, starting transfers between devices, moved(): return lax.ppermute(shard, 'ka', pairs)  52.8 us
    ppermute x17, waiting for transfers between devices, moved(): return lax.ppermute(shard, 'ka', pairs)  12.3 us
    ppermute x1, starting transfers between devices, per_device(): lax.ppermute(jnp.where(low, upper, lower), 'ga', [(g, g ^ 4) for g in ran...  10.9 us
    pallas_call x2, Pallas kernels, products(): pl.pallas_call(functools.partial(products_kernel, nb), out_shape=outs, in...  9.83 us
    all_to_all x1, waiting for transfers between devices, per_device(): lax.all_to_all(every, 'ga', 0, 0, axis_index_groups=[[0, 1, 2, 3], [4, 5,...  8.52 us
    transpose x4, local copies, waits for them, and re-layouts, rows_of(): return shard.transpose(1, 0, 2).reshape(2 * bands, width)  3.82 us
    ppermute x1, waiting for transfers between devices, per_device(): lax.ppermute(jnp.where(low, upper, lower), 'ga', [(g, g ^ 4) for g in ran...  3.48 us
    all_to_all x1, starting transfers between devices, per_device(): lax.all_to_all(every, 'ga', 0, 0, axis_index_groups=[[0, 1, 2, 3], [4, 5,...  3.47 us
  transfers between devices with their start and end apart: 19, of which 8 were waited for; matrix products, arithmetic and copies ran while one was open for 4% of the time, Pallas kernels for 5%

profile of v7, /device:TPU:24, one launch (start us, length us, event | category | flops | bytes accessed | tf_op | source)
XLA Modules:
  0.0 107.7 jit_solution(17956938875921388394)
XLA Ops:
  0.0 2.0 %collective-permute-start = (bf16[56,2,3840]{2,1,0:T(2,128)(2,1)}, bf16[56,2,3840]{2,1,0:T(2,128)(2,1)S(1)}, u32[]{:S(2)}, u32[]{:S(2)}) collective-permute-start(bf16[56,2,3840]{2,1,0:T(2,128)(2,1)} %param.2), channel_id=1, source_target_pairs={{0,8},{8,0},{16,24},{24,16},{32,40},{40,32},{48,56},{56,48},{64,72... | collective-permute-start | bytes 2580488 | tf_op jit(solution)/shard_map/ppermute | solution.py:29
  2.1 4.7 %collective-permute-start.1 = (bf16[56,2,3840]{2,1,0:T(2,128)(2,1)}, bf16[56,2,3840]{2,1,0:T(2,128)(2,1)}, u32[]{:S(2)}, u32[]{:S(2)}) collective-permute-start(bf16[56,2,3840]{2,1,0:T(2,128)(2,1)} %param.2), channel_id=1, source_target_pairs={{0,16},{8,120},{16,32},{24,8},{32,48},{40,24},{48,64},{56,40},{64,... | collective-permute-start | bytes 2580488 | tf_op jit(solution)/shard_map/ppermute | solution.py:29
  6.8 2.6 %collective-permute-start.5 = (bf16[56,2,3840]{2,1,0:T(2,128)(2,1)S(1)}, bf16[56,2,3840]{2,1,0:T(2,128)(2,1)}, u32[]{:S(2)}, u32[]{:S(2)}) collective-permute-start(bf16[56,2,3840]{2,1,0:T(2,128)(2,1)S(1)} %collective-permute-done), channel_id=1, source_target_pairs={{0,16},{8,120},{16,32},{24,8},{32,48},{40,24},{48,64},{56,40},{64,... | collective-permute-start | bytes 2580488 | tf_op jit(solution)/shard_map/ppermute | solution.py:29
  10.6 4.3 %collective-permute-start.3 = (bf16[112,3840]{1,0:T(8,128)(2,1)S(1)}, bf16[112,3840]{1,0:T(8,128)(2,1)S(1)}, u32[]{:S(2)}, u32[]{:S(2)}) collective-permute-start(bf16[112,3840]{1,0:T(8,128)(2,1)S(1)} %bitcast.20), channel_id=1, source_target_pairs={{0,128},{8,264},{16,144},{24,280},{32,160},{40,296},{48,176},{56,3... | collective-permute-start | bytes 2580488 | tf_op jit(solution)/shard_map/ppermute | solution.py:29
  15.0 2.3 %collective-permute-done.1 = bf16[56,2,3840]{2,1,0:T(2,128)(2,1)} collective-permute-done((bf16[56,2,3840]{2,1,0:T(2,128)(2,1)}, bf16[56,2,3840]{2,1,0:T(2,128)(2,1)}, u32[]{:S(2)}, u32[]{:S(2)}) %collective-permute-start.1) | collective-permute-done | bytes 860192 | tf_op jit(solution)/shard_map/ppermute | solution.py:29
  18.6 5.6 %collective-permute-start.2 = (bf16[112,3840]{1,0:T(8,128)(2,1)S(1)}, bf16[112,3840]{1,0:T(8,128)(2,1)S(1)}, u32[]{:S(2)}, u32[]{:S(2)}) collective-permute-start(bf16[112,3840]{1,0:T(8,128)(2,1)S(1)} %bitcast.22), channel_id=1, source_target_pairs={{0,16},{8,120},{16,32},{24,8},{32,48},{40,24},{48,64},{56,40},{64,... | collective-permute-start | bytes 2580488 | tf_op jit(solution)/shard_map/ppermute | solution.py:29
  24.2 1.3 %collective-permute-start.4 = (bf16[112,3840]{1,0:T(8,128)(2,1)S(1)}, bf16[112,3840]{1,0:T(8,128)(2,1)S(1)}, u32[]{:S(2)}, u32[]{:S(2)}) collective-permute-start(bf16[112,3840]{1,0:T(8,128)(2,1)S(1)} %bitcast.23), channel_id=1, source_target_pairs={{8,0},{16,24},{24,16},{32,40},{40,32},{48,56},{72,64},{80,88},{88,... | collective-permute-start | bytes 2580488 | tf_op jit(solution)/shard_map/ppermute | solution.py:29
  27.7 2.3 %collective-permute-start.6 = (bf16[112,3840]{1,0:T(8,128)(2,1)S(1)}, bf16[112,3840]{1,0:T(8,128)(2,1)S(1)}, u32[]{:S(2)}, u32[]{:S(2)}) collective-permute-start(bf16[112,3840]{1,0:T(8,128)(2,1)S(1)} %bitcast.25), channel_id=1, source_target_pairs={{8,0},{16,24},{24,16},{32,40},{40,32},{48,56},{72,64},{80,88},{88,... | collective-permute-start | bytes 2580488 | tf_op jit(solution)/shard_map/ppermute | solution.py:29
  30.0 4.7 %collective-permute-start.8 = (bf16[112,3840]{1,0:T(8,128)(2,1)S(1)}, bf16[112,3840]{1,0:T(8,128)(2,1)S(1)}, u32[]{:S(2)}, u32[]{:S(2)}) collective-permute-start(bf16[112,3840]{1,0:T(8,128)(2,1)S(1)} %bitcast.26), channel_id=1, source_target_pairs={{0,16},{8,120},{16,32},{24,8},{32,48},{40,24},{48,64},{56,40},{64,... | collective-permute-start | bytes 2580488 | tf_op jit(solution)/shard_map/ppermute | solution.py:29
  34.9 4.3 %collective-permute-start.14 = (bf16[112,3840]{1,0:T(8,128)(2,1)S(1)}, bf16[112,3840]{1,0:T(8,128)(2,1)S(1)}, u32[]{:S(2)}, u32[]{:S(2)}) collective-permute-start(bf16[112,3840]{1,0:T(8,128)(2,1)S(1)} %bitcast.28), channel_id=1, source_target_pairs={{0,128},{8,264},{16,144},{24,280},{32,160},{40,296},{48,176},{56,3... | collective-permute-start | bytes 2580488 | tf_op jit(solution)/shard_map/ppermute | solution.py:29
  40.5 2.1 %collective-permute-start.7 = (bf16[112,3840]{1,0:T(8,128)(2,1)S(1)}, bf16[112,3840]{1,0:T(8,128)(2,1)S(1)}, u32[]{:S(2)}, u32[]{:S(2)}) collective-permute-start(bf16[112,3840]{1,0:T(8,128)(2,1)S(1)} %collective-permute-done.2.refs_5_), channel_id=1, source_target_pairs={{0,16},{8,120},{16,32},{24,8},{32,48},{40,24},{48,64},{56,40},{64,... | collective-permute-start | bytes 2580488 | tf_op jit(solution)/shard_map/ppermute | solution.py:29
  42.6 2.4 %collective-permute-done.8.refs_8_ = bf16[112,3840]{1,0:T(8,128)(2,1)S(1)} collective-permute-done((bf16[112,3840]{1,0:T(8,128)(2,1)S(1)}, bf16[112,3840]{1,0:T(8,128)(2,1)S(1)}, u32[]{:S(2)}, u32[]{:S(2)}) %collective-permute-start.8) | collective-permute-done | bytes 860192 | tf_op jit(solution)/shard_map/ppermute | solution.py:29
  45.0 5.6 %collective-permute-start.9 = (bf16[112,3840]{1,0:T(8,128)(2,1)S(1)}, bf16[112,3840]{1,0:T(8,128)(2,1)S(1)}, u32[]{:S(2)}, u32[]{:S(2)}) collective-permute-start(bf16[112,3840]{1,0:T(8,128)(2,1)S(1)} %collective-permute-done.8.refs_8_), channel_id=1, source_target_pairs={{0,16},{8,120},{16,32},{24,8},{32,48},{40,24},{48,64},{56,40},{64,... | collective-permute-start | bytes 2580488 | tf_op jit(solution)/shard_map/ppermute | solution.py:29
  52.0 4.8 %collective-permute-done.14 = bf16[112,3840]{1,0:T(8,128)(2,1)S(1)} collective-permute-done((bf16[112,3840]{1,0:T(8,128)(2,1)S(1)}, bf16[112,3840]{1,0:T(8,128)(2,1)S(1)}, u32[]{:S(2)}, u32[]{:S(2)}) %collective-permute-start.14) | collective-permute-done | bytes 860192 | tf_op jit(solution)/shard_map/ppermute | solution.py:29
  56.8 2.5 %collective-permute-start.15 = (bf16[112,3840]{1,0:T(8,128)(2,1)S(1)}, bf16[112,3840]{1,0:T(8,128)(2,1)S(1)}, u32[]{:S(2)}, u32[]{:S(2)}) collective-permute-start(bf16[112,3840]{1,0:T(8,128)(2,1)S(1)} %collective-permute-done.14), channel_id=1, source_target_pairs={{0,8},{8,0},{16,24},{24,16},{32,40},{40,32},{48,56},{56,48},{64,72... | collective-permute-start | bytes 2580488 | tf_op jit(solution)/shard_map/ppermute | solution.py:29
  59.3 4.5 %collective-permute-start.16 = (bf16[112,3840]{1,0:T(8,128)(2,1)S(1)}, bf16[112,3840]{1,0:T(8,128)(2,1)S(1)}, u32[]{:S(2)}, u32[]{:S(2)}) collective-permute-start(bf16[112,3840]{1,0:T(8,128)(2,1)S(1)} %collective-permute-done.7.refs_6_), channel_id=1, source_target_pairs={{0,16},{8,120},{16,32},{24,8},{32,48},{40,24},{48,64},{56,40},{64,... | collective-permute-start | bytes 2580488 | tf_op jit(solution)/shard_map/ppermute | solution.py:29
  63.7 2.4 %collective-permute-start.11 = (bf16[112,3840]{1,0:T(8,128)(2,1)S(1)}, bf16[112,3840]{1,0:T(8,128)(2,1)S(1)}, u32[]{:S(2)}, u32[]{:S(2)}) collective-permute-start(bf16[112,3840]{1,0:T(8,128)(2,1)S(1)} %collective-permute-done.7.refs_6_), channel_id=1, source_target_pairs={{8,0},{48,56},{72,64},{112,120},{136,128},{176,184},{200,192},{240... | collective-permute-start | bytes 2580488 | tf_op jit(solution)/shard_map/ppermute | solution.py:29
  68.1 1.4 %collective-permute-done.13.refs_15_ = bf16[112,3840]{1,0:T(8,128)(2,1)S(1)} collective-permute-done((bf16[112,3840]{1,0:T(8,128)(2,1)S(1)}, bf16[112,3840]{1,0:T(8,128)(2,1)S(1)}, u32[]{:S(2)}, u32[]{:S(2)}) %collective-permute-start.13) | collective-permute-done | bytes 860192 | tf_op jit(solution)/shard_map/ppermute | solution.py:29
  69.4 5.6 %shard_map.28 = (s16[8,112,128]{2,1,0:T(8,128)(2,1)S(1)}, bf16[896,3840]{1,0:T(8,128)(2,1)S(1)}) custom-call(s32[2]{0:T(128)S(1)} %pad_add_fusion.refs_0_, s32[2,3840]{1,0:T(2,128)S(1)} %fusion.refs_1_, bf16[112,3840]{1,0:T(8,128)(2,1)S(1)} %bitcast.21, bf16[112,3840]{1,0:T(8,128)(2,1)S(1)} %bitcast.29, bf16[112,3840]{1,0:T(8,128)(2,1)S(1)} %bitcast.24, ...), custom_call_target="tpu_custom_call" | custom-call | flops 1761607680 | bytes 8601600 | tf_op jit(solution)/shard_map/pallas_call | solution.py:158
  75.1 4.2 %shard_map.29 = s16[8,176,128]{2,1,0:T(8,128)(2,1)} custom-call(s32[2]{0:T(128)S(1)} %pad_add_fusion.refs_0_, s32[1,3840]{1,0:T(1,128)S(1)} %get-tuple-element.24.refs_1_, bf16[896,3840]{1,0:T(8,128)(2,1)S(1)} %get-tuple-element.14.refs_2_, s16[8,112,128]{2,1,0:T(8,128)(2,1)S(1)} %get-tuple-element.15.refs_3_, ...), custom_call_target="tpu_custom_call" | custom-call | flops 880803840 | bytes 7741440 | tf_op jit(solution)/shard_map/pallas_call | solution.py:158
  79.3 3.5 %all-to-all-start = ((s16[8,176,128]{2,1,0:T(8,128)(2,1)}), s16[8,176,128]{2,1,0:T(8,128)(2,1)S(1)}, u32[]{:S(2)}, u32[]{:S(2)}) async-start(s16[8,176,128]{2,1,0:T(8,128)(2,1)} %shard_map.29), calls=%async_computation | async-start | bytes 720896 | tf_op jit(solution)/shard_map/all_to_all | solution.py:211
  82.8 8.5 %all-to-all-done = s16[8,176,128]{2,1,0:T(8,128)(2,1)S(1)} async-done(((s16[8,176,128]{2,1,0:T(8,128)(2,1)}), s16[8,176,128]{2,1,0:T(8,128)(2,1)S(1)}, u32[]{:S(2)}, u32[]{:S(2)}) %all-to-all-start) | async-done | bytes 360480 | tf_op jit(solution)/shard_map/all_to_all | solution.py:211
  92.2 10.9 %collective-permute-start.17 = (f32[168,112]{1,0:T(8,128)S(1)}, f32[168,112]{1,0:T(8,128)S(1)}, u32[]{:S(2)}, u32[]{:S(2)}) collective-permute-start(f32[168,112]{1,0:T(8,128)S(1)} %broadcast_select_fusion), channel_id=1, source_target_pairs={{0,4},{1,5},{2,6},{3,7},{4,0},{5,1},{6,2},{7,3},{8,12},{9,13},{10,... | collective-permute-start | bytes 225800 | tf_op jit(solution)/shard_map/ppermute | solution.py:219
  103.1 3.5 %collective-permute-done.17 = f32[168,112]{1,0:T(8,128)S(1)} collective-permute-done((f32[168,112]{1,0:T(8,128)S(1)}, f32[168,112]{1,0:T(8,128)S(1)}, u32[]{:S(2)}, u32[]{:S(2)}) %collective-permute-start.17) | collective-permute-done | bytes 75296 | tf_op jit(solution)/shard_map/ppermute | solution.py:219
  (37 shorter events, 11.5 us)
Async XLA Ops:
  0.0 15.0 %copy-start = (s32[8,3,3840]{2,0,1:T(8,128)S(1)}, s32[8,3,3840]{2,0,1:T(8,128)}, u32[]{:S(2)}) copy-start(s32[8,3,3840]{2,0,1:T(8,128)} %param.3) | copy-start | bytes 1105924
  0.0 6.8 %collective-permute-start = (bf16[56,2,3840]{2,1,0:T(2,128)(2,1)}, bf16[56,2,3840]{2,1,0:T(2,128)(2,1)S(1)}, u32[]{:S(2)}, u32[]{:S(2)}) collective-permute-start(bf16[56,2,3840]{2,1,0:T(2,128)(2,1)} %param.2), channel_id=1, source_target_pairs={{0,8},{8,0},{16,24},{24,16},{32,40},{40,32},{48,56},{56,48},{64,72... | collective-permute-start | bytes 2580488 | tf_op jit(solution)/shard_map/ppermute | solution.py:29
  2.1 15.3 %collective-permute-start.1 = (bf16[56,2,3840]{2,1,0:T(2,128)(2,1)}, bf16[56,2,3840]{2,1,0:T(2,128)(2,1)}, u32[]{:S(2)}, u32[]{:S(2)}) collective-permute-start(bf16[56,2,3840]{2,1,0:T(2,128)(2,1)} %param.2), channel_id=1, source_target_pairs={{0,16},{8,120},{16,32},{24,8},{32,48},{40,24},{48,64},{56,40},{64,... | collective-permute-start | bytes 2580488 | tf_op jit(solution)/shard_map/ppermute | solution.py:29
  6.8 19.7 %collective-permute-start.5 = (bf16[56,2,3840]{2,1,0:T(2,128)(2,1)S(1)}, bf16[56,2,3840]{2,1,0:T(2,128)(2,1)}, u32[]{:S(2)}, u32[]{:S(2)}) collective-permute-start(bf16[56,2,3840]{2,1,0:T(2,128)(2,1)S(1)} %collective-permute-done), channel_id=1, source_target_pairs={{0,16},{8,120},{16,32},{24,8},{32,48},{40,24},{48,64},{56,40},{64,... | collective-permute-start | bytes 2580488 | tf_op jit(solution)/shard_map/ppermute | solution.py:29
  10.6 24.2 %collective-permute-start.3 = (bf16[112,3840]{1,0:T(8,128)(2,1)S(1)}, bf16[112,3840]{1,0:T(8,128)(2,1)S(1)}, u32[]{:S(2)}, u32[]{:S(2)}) collective-permute-start(bf16[112,3840]{1,0:T(8,128)(2,1)S(1)} %bitcast.20), channel_id=1, source_target_pairs={{0,128},{8,264},{16,144},{24,280},{32,160},{40,296},{48,176},{56,3... | collective-permute-start | bytes 2580488 | tf_op jit(solution)/shard_map/ppermute | solution.py:29
  18.6 20.5 %collective-permute-start.2 = (bf16[112,3840]{1,0:T(8,128)(2,1)S(1)}, bf16[112,3840]{1,0:T(8,128)(2,1)S(1)}, u32[]{:S(2)}, u32[]{:S(2)}) collective-permute-start(bf16[112,3840]{1,0:T(8,128)(2,1)S(1)} %bitcast.22), channel_id=1, source_target_pairs={{0,16},{8,120},{16,32},{24,8},{32,48},{40,24},{48,64},{56,40},{64,... | collective-permute-start | bytes 2580488 | tf_op jit(solution)/shard_map/ppermute | solution.py:29
  24.2 16.3 %collective-permute-start.4 = (bf16[112,3840]{1,0:T(8,128)(2,1)S(1)}, bf16[112,3840]{1,0:T(8,128)(2,1)S(1)}, u32[]{:S(2)}, u32[]{:S(2)}) collective-permute-start(bf16[112,3840]{1,0:T(8,128)(2,1)S(1)} %bitcast.23), channel_id=1, source_target_pairs={{8,0},{16,24},{24,16},{32,40},{40,32},{48,56},{72,64},{80,88},{88,... | collective-permute-start | bytes 2580488 | tf_op jit(solution)/shard_map/ppermute | solution.py:29
  27.7 12.8 %collective-permute-start.6 = (bf16[112,3840]{1,0:T(8,128)(2,1)S(1)}, bf16[112,3840]{1,0:T(8,128)(2,1)S(1)}, u32[]{:S(2)}, u32[]{:S(2)}) collective-permute-start(bf16[112,3840]{1,0:T(8,128)(2,1)S(1)} %bitcast.25), channel_id=1, source_target_pairs={{8,0},{16,24},{24,16},{32,40},{40,32},{48,56},{72,64},{80,88},{88,... | collective-permute-start | bytes 2580488 | tf_op jit(solution)/shard_map/ppermute | solution.py:29
  30.0 15.0 %collective-permute-start.8 = (bf16[112,3840]{1,0:T(8,128)(2,1)S(1)}, bf16[112,3840]{1,0:T(8,128)(2,1)S(1)}, u32[]{:S(2)}, u32[]{:S(2)}) collective-permute-start(bf16[112,3840]{1,0:T(8,128)(2,1)S(1)} %bitcast.26), channel_id=1, source_target_pairs={{0,16},{8,120},{16,32},{24,8},{32,48},{40,24},{48,64},{56,40},{64,... | collective-permute-start | bytes 2580488 | tf_op jit(solution)/shard_map/ppermute | solution.py:29
  34.9 21.9 %collective-permute-start.14 = (bf16[112,3840]{1,0:T(8,128)(2,1)S(1)}, bf16[112,3840]{1,0:T(8,128)(2,1)S(1)}, u32[]{:S(2)}, u32[]{:S(2)}) collective-permute-start(bf16[112,3840]{1,0:T(8,128)(2,1)S(1)} %bitcast.28), channel_id=1, source_target_pairs={{0,128},{8,264},{16,144},{24,280},{32,160},{40,296},{48,176},{56,3... | collective-permute-start | bytes 2580488 | tf_op jit(solution)/shard_map/ppermute | solution.py:29
  39.1 20.1 %collective-permute-start.10 = (bf16[112,3840]{1,0:T(8,128)(2,1)S(1)}, bf16[112,3840]{1,0:T(8,128)(2,1)S(1)}, u32[]{:S(2)}, u32[]{:S(2)}) collective-permute-start(bf16[112,3840]{1,0:T(8,128)(2,1)S(1)} %collective-permute-done.2.refs_5_), channel_id=1, source_target_pairs={{8,0},{24,16},{32,40},{48,56},{72,64},{88,80},{96,104},{112,120},{... | collective-permute-start | bytes 2580488 | tf_op jit(solution)/shard_map/ppermute | solution.py:29
  40.5 16.2 %collective-permute-start.7 = (bf16[112,3840]{1,0:T(8,128)(2,1)S(1)}, bf16[112,3840]{1,0:T(8,128)(2,1)S(1)}, u32[]{:S(2)}, u32[]{:S(2)}) collective-permute-start(bf16[112,3840]{1,0:T(8,128)(2,1)S(1)} %collective-permute-done.2.refs_5_), channel_id=1, source_target_pairs={{0,16},{8,120},{16,32},{24,8},{32,48},{40,24},{48,64},{56,40},{64,... | collective-permute-start | bytes 2580488 | tf_op jit(solution)/shard_map/ppermute | solution.py:29
  45.0 21.1 %collective-permute-start.9 = (bf16[112,3840]{1,0:T(8,128)(2,1)S(1)}, bf16[112,3840]{1,0:T(8,128)(2,1)S(1)}, u32[]{:S(2)}, u32[]{:S(2)}) collective-permute-start(bf16[112,3840]{1,0:T(8,128)(2,1)S(1)} %collective-permute-done.8.refs_8_), channel_id=1, source_target_pairs={{0,16},{8,120},{16,32},{24,8},{32,48},{40,24},{48,64},{56,40},{64,... | collective-permute-start | bytes 2580488 | tf_op jit(solution)/shard_map/ppermute | solution.py:29
  50.6 8.7 %collective-permute-start.12 = (bf16[112,3840]{1,0:T(8,128)(2,1)S(1)}, bf16[112,3840]{1,0:T(8,128)(2,1)S(1)}, u32[]{:S(2)}, u32[]{:S(2)}) collective-permute-start(bf16[112,3840]{1,0:T(8,128)(2,1)S(1)} %collective-permute-done.8.refs_8_), channel_id=1, source_target_pairs={{8,0},{24,16},{32,40},{48,56},{72,64},{88,80},{96,104},{112,120},{... | collective-permute-start | bytes 2580488 | tf_op jit(solution)/shard_map/ppermute | solution.py:29
  56.8 12.7 %collective-permute-start.15 = (bf16[112,3840]{1,0:T(8,128)(2,1)S(1)}, bf16[112,3840]{1,0:T(8,128)(2,1)S(1)}, u32[]{:S(2)}, u32[]{:S(2)}) collective-permute-start(bf16[112,3840]{1,0:T(8,128)(2,1)S(1)} %collective-permute-done.14), channel_id=1, source_target_pairs={{0,8},{8,0},{16,24},{24,16},{32,40},{40,32},{48,56},{56,48},{64,72... | collective-permute-start | bytes 2580488 | tf_op jit(solution)/shard_map/ppermute | solution.py:29
  59.3 15.8 %collective-permute-start.16 = (bf16[112,3840]{1,0:T(8,128)(2,1)S(1)}, bf16[112,3840]{1,0:T(8,128)(2,1)S(1)}, u32[]{:S(2)}, u32[]{:S(2)}) collective-permute-start(bf16[112,3840]{1,0:T(8,128)(2,1)S(1)} %collective-permute-done.7.refs_6_), channel_id=1, source_target_pairs={{0,16},{8,120},{16,32},{24,8},{32,48},{40,24},{48,64},{56,40},{64,... | collective-permute-start | bytes 2580488 | tf_op jit(solution)/shard_map/ppermute | solution.py:29
  63.7 4.3 %collective-permute-start.11 = (bf16[112,3840]{1,0:T(8,128)(2,1)S(1)}, bf16[112,3840]{1,0:T(8,128)(2,1)S(1)}, u32[]{:S(2)}, u32[]{:S(2)}) collective-permute-start(bf16[112,3840]{1,0:T(8,128)(2,1)S(1)} %collective-permute-done.7.refs_6_), channel_id=1, source_target_pairs={{8,0},{48,56},{72,64},{112,120},{136,128},{176,184},{200,192},{240... | collective-permute-start | bytes 2580488 | tf_op jit(solution)/shard_map/ppermute | solution.py:29
  66.1 3.3 %collective-permute-start.13 = (bf16[112,3840]{1,0:T(8,128)(2,1)S(1)}, bf16[112,3840]{1,0:T(8,128)(2,1)S(1)}, u32[]{:S(2)}, u32[]{:S(2)}) collective-permute-start(bf16[112,3840]{1,0:T(8,128)(2,1)S(1)} %collective-permute-done.9.refs_9_), channel_id=1, source_target_pairs={{8,0},{48,56},{72,64},{112,120},{136,128},{176,184},{200,192},{240... | collective-permute-start | bytes 2580488 | tf_op jit(solution)/shard_map/ppermute | solution.py:29
  79.3 12.0 %all-to-all-start = ((s16[8,176,128]{2,1,0:T(8,128)(2,1)}), s16[8,176,128]{2,1,0:T(8,128)(2,1)S(1)}, u32[]{:S(2)}, u32[]{:S(2)}) async-start(s16[8,176,128]{2,1,0:T(8,128)(2,1)} %shard_map.29), calls=%async_computation | async-start | bytes 720896 | tf_op jit(solution)/shard_map/all_to_all | solution.py:211
  92.2 14.4 %collective-permute-start.17 = (f32[168,112]{1,0:T(8,128)S(1)}, f32[168,112]{1,0:T(8,128)S(1)}, u32[]{:S(2)}, u32[]{:S(2)}) collective-permute-start(f32[168,112]{1,0:T(8,128)S(1)} %broadcast_select_fusion), channel_id=1, source_target_pairs={{0,4},{1,5},{2,6},{3,7},{4,0},{5,1},{6,2},{7,3},{8,12},{9,13},{10,... | collective-permute-start | bytes 225800 | tf_op jit(solution)/shard_map/ppermute | solution.py:219

commit v8 on v6

--- a/solution.py
+++ b/solution.py
@@ -154,7 +154,7 @@
         )
         scratch.append(pltpu.SemaphoreType.DMA((8,)))
     else:
-        outs = jax.ShapeDtypeStruct((8, rows + 64, LANES), jnp.int16)
+        outs = pltpu.VMEM((8, rows + 64, LANES), jnp.int16)
     return pl.pallas_call(
         functools.partial(products_kernel, nb),
         out_shape=outs,

time: 108 us -> 108 us (level)
  no operation moved by 1% of the time
where the time goes in v8:
time: 108 us
  starting transfers between devices  54.8 us (51%)
  waiting for transfers between devices  39.3 us (36%)
  Pallas kernels  9.7 us (9%)
  other arithmetic  1.8 us (2%)
  local copies, waits for them, and re-layouts  1.65 us (2%)
    ppermute x17, starting transfers between devices, moved(): return lax.ppermute(shard, 'ka', pairs)  39.3 us
    ppermute x17, waiting for transfers between devices, moved(): return lax.ppermute(shard, 'ka', pairs)  28.7 us
    pallas_call x2, Pallas kernels, products(): pl.pallas_call(functools.partial(products_kernel, nb), out_shape=outs, in...  9.7 us
    all_to_all x1, starting transfers between devices, per_device(): lax.all_to_all(every, 'ga', 0, 0, axis_index_groups=[[0, 1, 2, 3], [4, 5,...  9.08 us
    all_to_all x1, waiting for transfers between devices, per_device(): lax.all_to_all(every, 'ga', 0, 0, axis_index_groups=[[0, 1, 2, 3], [4, 5,...  6.68 us
    ppermute x1, starting transfers between devices, per_device(): lax.ppermute(jnp.where(low, upper, lower), 'ga', [(g, g ^ 4) for g in ran...  6.37 us
    ppermute x1, waiting for transfers between devices, per_device(): lax.ppermute(jnp.where(low, upper, lower), 'ga', [(g, g ^ 4) for g in ran...  3.91 us
  transfers between devices with their start and end apart: 19, of which 10 were waited for; matrix products, arithmetic and copies ran while one was open for 0% of the time, Pallas kernels for 5%

profile of v8, /device:TPU:2, one launch (start us, length us, event | category | flops | bytes accessed | tf_op | source)
XLA Modules:
  0.0 107.5 jit_solution(4481180503350419976)
XLA Ops:
  1.3 1.9 %collective-permute-start = (bf16[112,3840]{1,0:T(8,128)(2,1)S(1)}, bf16[112,3840]{1,0:T(8,128)(2,1)S(1)}, u32[]{:S(2)}, u32[]{:S(2)}) collective-permute-start(bf16[112,3840]{1,0:T(8,128)(2,1)S(1)} %bitcast.14), channel_id=1, source_target_pairs={{0,8},{8,0},{16,24},{24,16},{32,40},{40,32},{48,56},{56,48},{64,72... | collective-permute-start | bytes 2580488 | tf_op jit(solution)/shard_map/ppermute | solution.py:29
  3.2 3.5 %collective-permute-start.1 = (bf16[112,3840]{1,0:T(8,128)(2,1)S(1)}, bf16[112,3840]{1,0:T(8,128)(2,1)S(1)}, u32[]{:S(2)}, u32[]{:S(2)}) collective-permute-start(bf16[112,3840]{1,0:T(8,128)(2,1)S(1)} %bitcast.15), channel_id=1, source_target_pairs={{0,16},{8,120},{16,32},{24,8},{32,48},{40,24},{48,64},{56,40},{64,... | collective-permute-start | bytes 2580488 | tf_op jit(solution)/shard_map/ppermute | solution.py:29
  6.7 3.5 %collective-permute-start.5 = (bf16[112,3840]{1,0:T(8,128)(2,1)S(1)}, bf16[112,3840]{1,0:T(8,128)(2,1)}, u32[]{:S(2)}, u32[]{:S(2)}) collective-permute-start(bf16[112,3840]{1,0:T(8,128)(2,1)S(1)} %collective-permute-done.refs_3_), channel_id=1, source_target_pairs={{0,16},{8,120},{16,32},{24,8},{32,48},{40,24},{48,64},{56,40},{64,... | collective-permute-start | bytes 2580488 | tf_op jit(solution)/shard_map/ppermute | solution.py:29
  10.2 4.3 %collective-permute-start.3 = (bf16[112,3840]{1,0:T(8,128)(2,1)S(1)}, bf16[112,3840]{1,0:T(8,128)(2,1)}, u32[]{:S(2)}, u32[]{:S(2)}) collective-permute-start(bf16[112,3840]{1,0:T(8,128)(2,1)S(1)} %bitcast.16), channel_id=1, source_target_pairs={{0,128},{8,264},{16,144},{24,280},{32,160},{40,296},{48,176},{56,3... | collective-permute-start | bytes 2580488 | tf_op jit(solution)/shard_map/ppermute | solution.py:29
  14.6 4.7 %collective-permute-done.1.refs_4_ = bf16[112,3840]{1,0:T(8,128)(2,1)S(1)} collective-permute-done((bf16[112,3840]{1,0:T(8,128)(2,1)S(1)}, bf16[112,3840]{1,0:T(8,128)(2,1)S(1)}, u32[]{:S(2)}, u32[]{:S(2)}) %collective-permute-start.1) | collective-permute-done | bytes 860192 | tf_op jit(solution)/shard_map/ppermute | solution.py:29
  20.6 2.7 %collective-permute-start.2 = (bf16[112,3840]{1,0:T(8,128)(2,1)S(1)}, bf16[112,3840]{1,0:T(8,128)(2,1)S(1)}, u32[]{:S(2)}, u32[]{:S(2)}) collective-permute-start(bf16[112,3840]{1,0:T(8,128)(2,1)S(1)} %collective-permute-done.1.refs_4_), channel_id=1, source_target_pairs={{0,16},{8,120},{16,32},{24,8},{32,48},{40,24},{48,64},{56,40},{64,... | collective-permute-start | bytes 2580488 | tf_op jit(solution)/shard_map/ppermute | solution.py:29
  23.3 5.4 %collective-permute-done.5.refs_7_ = bf16[112,3840]{1,0:T(8,128)(2,1)} collective-permute-done((bf16[112,3840]{1,0:T(8,128)(2,1)S(1)}, bf16[112,3840]{1,0:T(8,128)(2,1)}, u32[]{:S(2)}, u32[]{:S(2)}) %collective-permute-start.5) | collective-permute-done | bytes 860192 | tf_op jit(solution)/shard_map/ppermute | solution.py:29
  28.7 2.0 %collective-permute-start.8 = (bf16[112,3840]{1,0:T(8,128)(2,1)}, bf16[112,3840]{1,0:T(8,128)(2,1)S(1)}, u32[]{:S(2)}, u32[]{:S(2)}) collective-permute-start(bf16[112,3840]{1,0:T(8,128)(2,1)} %collective-permute-done.5.refs_7_), channel_id=1, source_target_pairs={{0,16},{8,120},{16,32},{24,8},{32,48},{40,24},{48,64},{56,40},{64,... | collective-permute-start | bytes 2580488 | tf_op jit(solution)/shard_map/ppermute | solution.py:29
  32.0 1.5 %collective-permute-done.3.refs_16_ = bf16[112,3840]{1,0:T(8,128)(2,1)} collective-permute-done((bf16[112,3840]{1,0:T(8,128)(2,1)S(1)}, bf16[112,3840]{1,0:T(8,128)(2,1)}, u32[]{:S(2)}, u32[]{:S(2)}) %collective-permute-start.3) | collective-permute-done | bytes 860192 | tf_op jit(solution)/shard_map/ppermute | solution.py:29
  33.6 2.8 %collective-permute-start.14 = (bf16[112,3840]{1,0:T(8,128)(2,1)S(1)}, bf16[112,3840]{1,0:T(8,128)(2,1)S(1)}, u32[]{:S(2)}, u32[]{:S(2)}) collective-permute-start(bf16[112,3840]{1,0:T(8,128)(2,1)S(1)} %collective-permute-done.refs_3_), channel_id=1, source_target_pairs={{0,128},{8,264},{16,144},{24,280},{32,160},{40,296},{48,176},{56,3... | collective-permute-start | bytes 2580488 | tf_op jit(solution)/shard_map/ppermute | solution.py:29
  36.3 1.5 %collective-permute-done.2.refs_5_ = bf16[112,3840]{1,0:T(8,128)(2,1)S(1)} collective-permute-done((bf16[112,3840]{1,0:T(8,128)(2,1)S(1)}, bf16[112,3840]{1,0:T(8,128)(2,1)S(1)}, u32[]{:S(2)}, u32[]{:S(2)}) %collective-permute-start.2) | collective-permute-done | bytes 860192 | tf_op jit(solution)/shard_map/ppermute | solution.py:29
  39.1 2.7 %collective-permute-start.7 = (bf16[112,3840]{1,0:T(8,128)(2,1)S(1)}, bf16[112,3840]{1,0:T(8,128)(2,1)S(1)}, u32[]{:S(2)}, u32[]{:S(2)}) collective-permute-start(bf16[112,3840]{1,0:T(8,128)(2,1)S(1)} %collective-permute-done.2.refs_5_), channel_id=1, source_target_pairs={{0,16},{8,120},{16,32},{24,8},{32,48},{40,24},{48,64},{56,40},{64,... | collective-permute-start | bytes 2580488 | tf_op jit(solution)/shard_map/ppermute | solution.py:29
  41.8 5.2 %collective-permute-done.8.refs_8_ = bf16[112,3840]{1,0:T(8,128)(2,1)S(1)} collective-permute-done((bf16[112,3840]{1,0:T(8,128)(2,1)}, bf16[112,3840]{1,0:T(8,128)(2,1)S(1)}, u32[]{:S(2)}, u32[]{:S(2)}) %collective-permute-start.8) | collective-permute-done | bytes 860192 | tf_op jit(solution)/shard_map/ppermute | solution.py:29
  48.3 2.0 %collective-permute-start.9 = (bf16[112,3840]{1,0:T(8,128)(2,1)S(1)}, bf16[112,3840]{1,0:T(8,128)(2,1)S(1)}, u32[]{:S(2)}, u32[]{:S(2)}) collective-permute-start(bf16[112,3840]{1,0:T(8,128)(2,1)S(1)} %collective-permute-done.8.refs_8_), channel_id=1, source_target_pairs={{0,16},{8,120},{16,32},{24,8},{32,48},{40,24},{48,64},{56,40},{64,... | collective-permute-start | bytes 2580488 | tf_op jit(solution)/shard_map/ppermute | solution.py:29
  50.4 7.1 %collective-permute-done.14 = bf16[112,3840]{1,0:T(8,128)(2,1)S(1)} collective-permute-done((bf16[112,3840]{1,0:T(8,128)(2,1)S(1)}, bf16[112,3840]{1,0:T(8,128)(2,1)S(1)}, u32[]{:S(2)}, u32[]{:S(2)}) %collective-permute-start.14) | collective-permute-done | bytes 860192 | tf_op jit(solution)/shard_map/ppermute | solution.py:29
  57.4 1.9 %collective-permute-start.15 = (bf16[112,3840]{1,0:T(8,128)(2,1)S(1)}, bf16[112,3840]{1,0:T(8,128)(2,1)S(1)}, u32[]{:S(2)}, u32[]{:S(2)}) collective-permute-start(bf16[112,3840]{1,0:T(8,128)(2,1)S(1)} %collective-permute-done.14), channel_id=1, source_target_pairs={{0,8},{8,0},{16,24},{24,16},{32,40},{40,32},{48,56},{56,48},{64,72... | collective-permute-start | bytes 2580488 | tf_op jit(solution)/shard_map/ppermute | solution.py:29
  59.4 4.4 %collective-permute-start.16 = (bf16[112,3840]{1,0:T(8,128)(2,1)S(1)}, bf16[112,3840]{1,0:T(8,128)(2,1)S(1)}, u32[]{:S(2)}, u32[]{:S(2)}) collective-permute-start(bf16[112,3840]{1,0:T(8,128)(2,1)S(1)} %collective-permute-done.7.refs_6_), channel_id=1, source_target_pairs={{0,16},{8,120},{16,32},{24,8},{32,48},{40,24},{48,64},{56,40},{64,... | collective-permute-start | bytes 2580488 | tf_op jit(solution)/shard_map/ppermute | solution.py:29
  66.8 2.9 %collective-permute-done.13.refs_15_ = bf16[112,3840]{1,0:T(8,128)(2,1)S(1)} collective-permute-done((bf16[112,3840]{1,0:T(8,128)(2,1)S(1)}, bf16[112,3840]{1,0:T(8,128)(2,1)S(1)}, u32[]{:S(2)}, u32[]{:S(2)}) %collective-permute-start.13) | collective-permute-done | bytes 860192 | tf_op jit(solution)/shard_map/ppermute | solution.py:29
  69.7 5.5 %shard_map.28 = (s16[8,112,128]{2,1,0:T(8,128)(2,1)S(1)}, bf16[896,3840]{1,0:T(8,128)(2,1)S(1)}) custom-call(s32[2]{0:T(128)S(1)} %pad_add_fusion.refs_0_, s32[2,3840]{1,0:T(2,128)S(1)} %fusion.refs_1_, bf16[112,3840]{1,0:T(8,128)(2,1)S(1)} %bitcast.17, bf16[112,3840]{1,0:T(8,128)(2,1)S(1)} %collective-permute-done.refs_3_, ...), custom_call_target="tpu_custom_call" | custom-call | flops 1761607680 | bytes 8601600 | tf_op jit(solution)/shard_map/pallas_call | solution.py:158
  75.3 4.2 %shard_map.29 = s16[8,176,128]{2,1,0:T(8,128)(2,1)} custom-call(s32[2]{0:T(128)S(1)} %pad_add_fusion.refs_0_, s32[1,3840]{1,0:T(1,128)S(1)} %get-tuple-element.22.refs_1_, bf16[896,3840]{1,0:T(8,128)(2,1)S(1)} %get-tuple-element.12.refs_2_, s16[8,112,128]{2,1,0:T(8,128)(2,1)S(1)} %get-tuple-element.13.refs_3_, ...), custom_call_target="tpu_custom_call" | custom-call | flops 880803840 | bytes 7741440 | tf_op jit(solution)/shard_map/pallas_call | solution.py:158
  79.5 9.1 %all-to-all-start = ((s16[8,176,128]{2,1,0:T(8,128)(2,1)}), s16[8,176,128]{2,1,0:T(8,128)(2,1)S(1)}, u32[]{:S(2)}, u32[]{:S(2)}) async-start(s16[8,176,128]{2,1,0:T(8,128)(2,1)} %shard_map.29), calls=%async_computation | async-start | bytes 720896 | tf_op jit(solution)/shard_map/all_to_all | solution.py:203
  88.5 6.7 %all-to-all-done = s16[8,176,128]{2,1,0:T(8,128)(2,1)S(1)} async-done(((s16[8,176,128]{2,1,0:T(8,128)(2,1)}), s16[8,176,128]{2,1,0:T(8,128)(2,1)S(1)}, u32[]{:S(2)}, u32[]{:S(2)}) %all-to-all-start) | async-done | bytes 360480 | tf_op jit(solution)/shard_map/all_to_all | solution.py:203
  96.1 6.4 %collective-permute-start.17 = (f32[168,112]{1,0:T(8,128)S(1)}, f32[168,112]{1,0:T(8,128)S(1)}, u32[]{:S(2)}, u32[]{:S(2)}) collective-permute-start(f32[168,112]{1,0:T(8,128)S(1)} %broadcast_select_fusion), channel_id=1, source_target_pairs={{0,4},{1,5},{2,6},{3,7},{4,0},{5,1},{6,2},{7,3},{8,12},{9,13},{10,... | collective-permute-start | bytes 225800 | tf_op jit(solution)/shard_map/ppermute | solution.py:211
  102.5 3.9 %collective-permute-done.17 = f32[168,112]{1,0:T(8,128)S(1)} collective-permute-done((f32[168,112]{1,0:T(8,128)S(1)}, f32[168,112]{1,0:T(8,128)S(1)}, u32[]{:S(2)}, u32[]{:S(2)}) %collective-permute-start.17) | collective-permute-done | bytes 75296 | tf_op jit(solution)/shard_map/ppermute | solution.py:211
  (34 shorter events, 11.6 us)
Async XLA Ops:
  0.0 14.6 %copy-start = (s32[8,3,3840]{2,0,1:T(8,128)S(1)}, s32[8,3,3840]{2,0,1:T(8,128)}, u32[]{:S(2)}) copy-start(s32[8,3,3840]{2,0,1:T(8,128)} %param.3) | copy-start | bytes 1105924
  1.3 5.4 %collective-permute-start = (bf16[112,3840]{1,0:T(8,128)(2,1)S(1)}, bf16[112,3840]{1,0:T(8,128)(2,1)S(1)}, u32[]{:S(2)}, u32[]{:S(2)}) collective-permute-start(bf16[112,3840]{1,0:T(8,128)(2,1)S(1)} %bitcast.14), channel_id=1, source_target_pairs={{0,8},{8,0},{16,24},{24,16},{32,40},{40,32},{48,56},{56,48},{64,72... | collective-permute-start | bytes 2580488 | tf_op jit(solution)/shard_map/ppermute | solution.py:29
  3.2 16.1 %collective-permute-start.1 = (bf16[112,3840]{1,0:T(8,128)(2,1)S(1)}, bf16[112,3840]{1,0:T(8,128)(2,1)S(1)}, u32[]{:S(2)}, u32[]{:S(2)}) collective-permute-start(bf16[112,3840]{1,0:T(8,128)(2,1)S(1)} %bitcast.15), channel_id=1, source_target_pairs={{0,16},{8,120},{16,32},{24,8},{32,48},{40,24},{48,64},{56,40},{64,... | collective-permute-start | bytes 2580488 | tf_op jit(solution)/shard_map/ppermute | solution.py:29
  6.7 21.9 %collective-permute-start.5 = (bf16[112,3840]{1,0:T(8,128)(2,1)S(1)}, bf16[112,3840]{1,0:T(8,128)(2,1)}, u32[]{:S(2)}, u32[]{:S(2)}) collective-permute-start(bf16[112,3840]{1,0:T(8,128)(2,1)S(1)} %collective-permute-done.refs_3_), channel_id=1, source_target_pairs={{0,16},{8,120},{16,32},{24,8},{32,48},{40,24},{48,64},{56,40},{64,... | collective-permute-start | bytes 2580488 | tf_op jit(solution)/shard_map/ppermute | solution.py:29
  10.2 23.3 %collective-permute-start.3 = (bf16[112,3840]{1,0:T(8,128)(2,1)S(1)}, bf16[112,3840]{1,0:T(8,128)(2,1)}, u32[]{:S(2)}, u32[]{:S(2)}) collective-permute-start(bf16[112,3840]{1,0:T(8,128)(2,1)S(1)} %bitcast.16), channel_id=1, source_target_pairs={{0,128},{8,264},{16,144},{24,280},{32,160},{40,296},{48,176},{56,3... | collective-permute-start | bytes 2580488 | tf_op jit(solution)/shard_map/ppermute | solution.py:29
  19.4 19.7 %collective-permute-start.4 = (bf16[112,3840]{1,0:T(8,128)(2,1)S(1)}, bf16[112,3840]{1,0:T(8,128)(2,1)S(1)}, u32[]{:S(2)}, u32[]{:S(2)}) collective-permute-start(bf16[112,3840]{1,0:T(8,128)(2,1)S(1)} %collective-permute-done.1.refs_4_), channel_id=1, source_target_pairs={{8,0},{16,24},{24,16},{32,40},{40,32},{48,56},{72,64},{80,88},{88,... | collective-permute-start | bytes 2580488 | tf_op jit(solution)/shard_map/ppermute | solution.py:29
  20.6 17.1 %collective-permute-start.2 = (bf16[112,3840]{1,0:T(8,128)(2,1)S(1)}, bf16[112,3840]{1,0:T(8,128)(2,1)S(1)}, u32[]{:S(2)}, u32[]{:S(2)}) collective-permute-start(bf16[112,3840]{1,0:T(8,128)(2,1)S(1)} %collective-permute-done.1.refs_4_), channel_id=1, source_target_pairs={{0,16},{8,120},{16,32},{24,8},{32,48},{40,24},{48,64},{56,40},{64,... | collective-permute-start | bytes 2580488 | tf_op jit(solution)/shard_map/ppermute | solution.py:29
  28.7 18.3 %collective-permute-start.8 = (bf16[112,3840]{1,0:T(8,128)(2,1)}, bf16[112,3840]{1,0:T(8,128)(2,1)S(1)}, u32[]{:S(2)}, u32[]{:S(2)}) collective-permute-start(bf16[112,3840]{1,0:T(8,128)(2,1)} %collective-permute-done.5.refs_7_), channel_id=1, source_target_pairs={{0,16},{8,120},{16,32},{24,8},{32,48},{40,24},{48,64},{56,40},{64,... | collective-permute-start | bytes 2580488 | tf_op jit(solution)/shard_map/ppermute | solution.py:29
  30.7 8.4 %collective-permute-start.6 = (bf16[112,3840]{1,0:T(8,128)(2,1)}, bf16[112,3840]{1,0:T(8,128)(2,1)S(1)}, u32[]{:S(2)}, u32[]{:S(2)}) collective-permute-start(bf16[112,3840]{1,0:T(8,128)(2,1)} %collective-permute-done.5.refs_7_), channel_id=1, source_target_pairs={{8,0},{16,24},{24,16},{32,40},{40,32},{48,56},{72,64},{80,88},{88,... | collective-permute-start | bytes 2580488 | tf_op jit(solution)/shard_map/ppermute | solution.py:29
  33.6 23.9 %collective-permute-start.14 = (bf16[112,3840]{1,0:T(8,128)(2,1)S(1)}, bf16[112,3840]{1,0:T(8,128)(2,1)S(1)}, u32[]{:S(2)}, u32[]{:S(2)}) collective-permute-start(bf16[112,3840]{1,0:T(8,128)(2,1)S(1)} %collective-permute-done.refs_3_), channel_id=1, source_target_pairs={{0,128},{8,264},{16,144},{24,280},{32,160},{40,296},{48,176},{56,3... | collective-permute-start | bytes 2580488 | tf_op jit(solution)/shard_map/ppermute | solution.py:29
  37.8 21.6 %collective-permute-start.10 = (bf16[112,3840]{1,0:T(8,128)(2,1)S(1)}, bf16[112,3840]{1,0:T(8,128)(2,1)S(1)}, u32[]{:S(2)}, u32[]{:S(2)}) collective-permute-start(bf16[112,3840]{1,0:T(8,128)(2,1)S(1)} %collective-permute-done.2.refs_5_), channel_id=1, source_target_pairs={{8,0},{24,16},{32,40},{48,56},{72,64},{88,80},{96,104},{112,120},{... | collective-permute-start | bytes 2580488 | tf_op jit(solution)/shard_map/ppermute | solution.py:29
  39.1 20.3 %collective-permute-start.7 = (bf16[112,3840]{1,0:T(8,128)(2,1)S(1)}, bf16[112,3840]{1,0:T(8,128)(2,1)S(1)}, u32[]{:S(2)}, u32[]{:S(2)}) collective-permute-start(bf16[112,3840]{1,0:T(8,128)(2,1)S(1)} %collective-permute-done.2.refs_5_), channel_id=1, source_target_pairs={{0,16},{8,120},{16,32},{24,8},{32,48},{40,24},{48,64},{56,40},{64,... | collective-permute-start | bytes 2580488 | tf_op jit(solution)/shard_map/ppermute | solution.py:29
  47.0 12.4 %collective-permute-start.12 = (bf16[112,3840]{1,0:T(8,128)(2,1)S(1)}, bf16[112,3840]{1,0:T(8,128)(2,1)S(1)}, u32[]{:S(2)}, u32[]{:S(2)}) collective-permute-start(bf16[112,3840]{1,0:T(8,128)(2,1)S(1)} %collective-permute-done.8.refs_8_), channel_id=1, source_target_pairs={{8,0},{24,16},{32,40},{48,56},{72,64},{88,80},{96,104},{112,120},{... | collective-permute-start | bytes 2580488 | tf_op jit(solution)/shard_map/ppermute | solution.py:29
  48.3 17.1 %collective-permute-start.9 = (bf16[112,3840]{1,0:T(8,128)(2,1)S(1)}, bf16[112,3840]{1,0:T(8,128)(2,1)S(1)}, u32[]{:S(2)}, u32[]{:S(2)}) collective-permute-start(bf16[112,3840]{1,0:T(8,128)(2,1)S(1)} %collective-permute-done.8.refs_8_), channel_id=1, source_target_pairs={{0,16},{8,120},{16,32},{24,8},{32,48},{40,24},{48,64},{56,40},{64,... | collective-permute-start | bytes 2580488 | tf_op jit(solution)/shard_map/ppermute | solution.py:29
  57.4 9.3 %collective-permute-start.15 = (bf16[112,3840]{1,0:T(8,128)(2,1)S(1)}, bf16[112,3840]{1,0:T(8,128)(2,1)S(1)}, u32[]{:S(2)}, u32[]{:S(2)}) collective-permute-start(bf16[112,3840]{1,0:T(8,128)(2,1)S(1)} %collective-permute-done.14), channel_id=1, source_target_pairs={{0,8},{8,0},{16,24},{24,16},{32,40},{40,32},{48,56},{56,48},{64,72... | collective-permute-start | bytes 2580488 | tf_op jit(solution)/shard_map/ppermute | solution.py:29
  59.4 15.9 %collective-permute-start.16 = (bf16[112,3840]{1,0:T(8,128)(2,1)S(1)}, bf16[112,3840]{1,0:T(8,128)(2,1)S(1)}, u32[]{:S(2)}, u32[]{:S(2)}) collective-permute-start(bf16[112,3840]{1,0:T(8,128)(2,1)S(1)} %collective-permute-done.7.refs_6_), channel_id=1, source_target_pairs={{0,16},{8,120},{16,32},{24,8},{32,48},{40,24},{48,64},{56,40},{64,... | collective-permute-start | bytes 2580488 | tf_op jit(solution)/shard_map/ppermute | solution.py:29
  63.8 5.9 %collective-permute-start.11 = (bf16[112,3840]{1,0:T(8,128)(2,1)S(1)}, bf16[112,3840]{1,0:T(8,128)(2,1)S(1)}, u32[]{:S(2)}, u32[]{:S(2)}) collective-permute-start(bf16[112,3840]{1,0:T(8,128)(2,1)S(1)} %collective-permute-done.7.refs_6_), channel_id=1, source_target_pairs={{8,0},{48,56},{72,64},{112,120},{136,128},{176,184},{200,192},{240... | collective-permute-start | bytes 2580488 | tf_op jit(solution)/shard_map/ppermute | solution.py:29
  65.4 4.3 %collective-permute-start.13 = (bf16[112,3840]{1,0:T(8,128)(2,1)S(1)}, bf16[112,3840]{1,0:T(8,128)(2,1)S(1)}, u32[]{:S(2)}, u32[]{:S(2)}) collective-permute-start(bf16[112,3840]{1,0:T(8,128)(2,1)S(1)} %collective-permute-done.9.refs_9_), channel_id=1, source_target_pairs={{8,0},{48,56},{72,64},{112,120},{136,128},{176,184},{200,192},{240... | collective-permute-start | bytes 2580488 | tf_op jit(solution)/shard_map/ppermute | solution.py:29
  79.5 15.8 %all-to-all-start = ((s16[8,176,128]{2,1,0:T(8,128)(2,1)}), s16[8,176,128]{2,1,0:T(8,128)(2,1)S(1)}, u32[]{:S(2)}, u32[]{:S(2)}) async-start(s16[8,176,128]{2,1,0:T(8,128)(2,1)} %shard_map.29), calls=%async_computation | async-start | bytes 720896 | tf_op jit(solution)/shard_map/all_to_all | solution.py:203
  96.1 10.3 %collective-permute-start.17 = (f32[168,112]{1,0:T(8,128)S(1)}, f32[168,112]{1,0:T(8,128)S(1)}, u32[]{:S(2)}, u32[]{:S(2)}) collective-permute-start(f32[168,112]{1,0:T(8,128)S(1)} %broadcast_select_fusion), channel_id=1, source_target_pairs={{0,4},{1,5},{2,6},{3,7},{4,0},{5,1},{6,2},{7,3},{8,12},{9,13},{10,... | collective-permute-start | bytes 225800 | tf_op jit(solution)/shard_map/ppermute | solution.py:211
